TPU v7x, 128 devices: a whole 4x4x4 slice. The times are simulated.
128 devices in a mesh: grp: 2 (over core), row: 4 (over z), col: 16 (over y, x).
Axes of the slice: x: 4, y: 4, z: 4, core: 2. Of those that a mesh axis runs over, the one named last changes fastest.
Arguments:
- jacobian: float32 [512, 16384], P(('grp', 'row', 'col')), may hold values from -0.25 to 0.25
- covariance: float32 [16384, 8192], P(('grp', 'row'), 'col'), as said below
- noise: float32 [512], replicated, may hold values from 0.5 to 2
- innovation: float32 [512], replicated, may hold values from -36 to 36
Outputs:
- delta: float32 [16384], P(('grp', 'row'))
- new_covariance: float32 [16384, 8192], P(('grp', 'row'), 'col')
Inputs may be any that keep to these rules, and one draw needn't show every extreme that they name: Each block of 8192 rows of covariance is symmetric and positive definite.
All inputs are finite; a program needn't handle non-finite values.
Results may differ from a plain program's by a relative error of at most 0.00075.
Values sent between devices are 32-bit elements; how exact they have to be, the bound alone decides.
No kernel may reach another device: no remote copies, remote signals or barrier semaphores. Data moves between devices by JAX's collectives and lax.ppermute only.
A program may use at most 64 MiB of HBM per device.

v0:
```python
import jax
import jax.numpy as jnp
from jax import lax
from jax.sharding import PartitionSpec as P


def spread(value, axis, root):
    mine = lax.axis_index(axis) == root
    return lax.psum(jnp.where(mine, value, jnp.zeros_like(value)), axis)


def per_device(jacobian, covariance, noise, innovation):
    high = lax.Precision.HIGHEST
    rows_dev = covariance.shape[0]
    cols_dev = covariance.shape[1]
    row_index = lax.axis_index("row")
    col_index = lax.axis_index("col")
    piece = lax.all_to_all(jacobian, ("grp", "row", "col"), split_axis=1, concat_axis=0, tiled=True)
    jac_rows = lax.all_gather(piece, "col", axis=1, tiled=True)
    partial_cols = jnp.dot(jac_rows, covariance, precision=high, preferred_element_type=jnp.float32)
    prod_cols = lax.psum(partial_cols, "row")
    root_row = col_index * cols_dev // rows_dev
    offset = jnp.clip(col_index * cols_dev - row_index * rows_dev, 0, rows_dev - cols_dev)
    own_slice = lax.dynamic_slice_in_dim(jac_rows, offset, cols_dev, 1)
    jac_cols = spread(own_slice, "row", root_row)
    partial_system = jnp.dot(
        prod_cols, jac_cols.T, precision=high, preferred_element_type=jnp.float32
    )
    system = lax.psum(partial_system, ("grp", "col")) + jnp.diag(noise)
    lower = jnp.linalg.cholesky(system)
    solved_cols = jax.scipy.linalg.cho_solve((lower, True), prod_cols)
    solve_e = jax.scipy.linalg.cho_solve((lower, True), innovation)
    partial_rows = jnp.dot(
        jac_cols, covariance.T, precision=high, preferred_element_type=jnp.float32
    )
    prod_rows = lax.psum(partial_rows, "col")
    change = lax.dot_general(
        prod_rows,
        solved_cols,
        (((0,), (0,)), ((), ())),
        precision=high,
        preferred_element_type=jnp.float32,
    )
    new_covariance = (covariance - change) / 0.98
    delta = lax.dot_general(
        prod_rows,
        solve_e,
        (((0,), (0,)), ((), ())),
        precision=high,
        preferred_element_type=jnp.float32,
    )
    return (delta, new_covariance)


def solution(mesh):
    in_specs = (P(("grp", "row", "col"), None), P(("grp", "row"), "col"), P(), P())
    out_specs = (P(("grp", "row")), P(("grp", "row"), "col"))
    return jax.shard_map(
        per_device, mesh=mesh, in_specs=in_specs, out_specs=out_specs, check_vma=False
    )
```

profile of v0, /device:TPU:1, one launch (start us, length us, event | category | flops | bytes accessed | tf_op | source)
XLA Modules:
  0.0 426.3 jit_solution(15825322838967120839)
XLA Ops:
  7.2 22.4 %all_to_all.19 = f32[4,128,128]{2,0,1:T(4,128)S(1)} all-to-all(f32[4,128,128]{2,0,1:T(4,128)} %bitcast.167), channel_id=1, replica_groups=mesh['grp'=2,'row'=4,'col'=16] {'grp','row','col'}, dimensions={1} | all-to-all | bytes 524288 | tf_op jit(solution)/shard_map/all_to_all | solution.py:18
  30.6 47.2 %all-gather.2.cloned.1.call-done = f32[512,2048]{0,1:T(8,128)} async-done(((f32[512,128]{0,1:T(8,128)}), f32[512,2048]{0,1:T(8,128)}) %all-gather.2.cloned.1.call-update) | async-done | bytes 4194320 | tf_op jit(solution)/shard_map/all_gather | solution.py:19
  77.8 10.2 %fusion.110 = f32[512,512]{1,0:T(8,128)} fusion(f32[512,2048]{0,1:T(8,128)} %all-gather.2.cloned.1.call-done, f32[2048,512]{1,0:T(8,128)} %param.5), kind=kOutput, calls=%fused_computation.163 | convolution fusion | flops 6442450944 | bytes 9437184 | tf_op jit(solution)/shard_map/dot_general | solution.py:20
  88.0 2.4 dynamic-slice_select_fusion
  90.5 59.0 %all-reduce.10.cloned.1.call-done = (f32[512,512]{0,1:T(8,128)}, f32[512,512]{1,0:T(8,128)}) async-done(((f32[512,512]{0,1:T(8,128)}, f32[512,512]{1,0:T(8,128)}), (f32[512,512]{0,1:T(8,128)}, f32[512,512]{1,0:T(8,128)})) %all-reduce.10.cloned.1.call-update) | async-done | bytes 2097168 | tf_op jit(solution)/shard_map/psum | solution.py:9
  149.4 4.5 %fusion.111 = f32[512,512]{0,1:T(8,128)} fusion(f32[512,512]{1,0:T(8,128)} %get-tuple-element.27, f32[512,512]{0,1:T(8,128)} %get-tuple-element.26), kind=kOutput, calls=%fused_computation.164 | convolution fusion | flops 1610612736 | bytes 3145728 | tf_op jit(solution)/shard_map/dot_general | solution.py:26
  154.2 16.6 %fusion.109 = f32[512,2048]{1,0:T(8,128)} fusion(f32[512,512]{0,1:T(8,128)S(1)} %copy-done.1, f32[2048,512]{1,0:T(8,128)} %param.5), kind=kOutput, calls=%fused_computation.162 | convolution fusion | flops 6442450944 | bytes 9437184 | tf_op jit(solution)/shard_map/dot_general | solution.py:33
  170.8 87.6 %all-reduce.8.cloned.1.call-done = f32[512,512]{0,1:T(8,128)} async-done(((f32[512,512]{0,1:T(8,128)}), f32[512,512]{0,1:T(8,128)}) %all-reduce.8.cloned.1.call-update) | async-done | bytes 1048592 | tf_op jit(solution)/shard_map/psum | solution.py:29
  258.4 1.4 select_add_fusion
  260.4 11.7 %cholesky.103 = f32[128,128]{1,0:T(8,128)S(1)} custom-call(f32[128,128]{1,0:T(8,128)S(1)} %cholesky.263), custom_call_target="Cholesky" | custom-call | tf_op jit(solution)/shard_map/jit(cholesky)/cholesky | solution.py:30
  272.3 9.8 %custom-call.40 = f32[1,128,128]{1,2,0:T(8,128)S(1)} custom-call(f32[1,128,128]{2,1,0:T(8,128)S(1)} %get-tuple-element.35), custom_call_target="InvertDiagBlocksLowerTriangular" | custom-call | tf_op jit(solution)/shard_map/jit(cholesky)/cholesky | solution.py:30
  282.9 11.7 %cholesky.215 = f32[128,128]{1,0:T(8,128)S(1)} custom-call(f32[128,128]{1,0:T(8,128)S(1)} %cholesky.267), custom_call_target="Cholesky" | custom-call | tf_op jit(solution)/shard_map/jit(cholesky)/cholesky | solution.py:30
  294.8 10.2 %custom-call.41 = f32[1,128,128]{1,2,0:T(8,128)S(1)} custom-call(f32[1,128,128]{2,1,0:T(8,128)S(1)} %get-tuple-element.33), custom_call_target="InvertDiagBlocksLowerTriangular" | custom-call | tf_op jit(solution)/shard_map/jit(cholesky)/cholesky | solution.py:30
  305.5 1.5 convolution_subtract_fusion.7
  307.0 11.7 %cholesky.236 = f32[128,128]{1,0:T(8,128)S(1)} custom-call(f32[128,128]{1,0:T(8,128)S(1)} %cholesky.272), custom_call_target="Cholesky" | custom-call | tf_op jit(solution)/shard_map/jit(cholesky)/cholesky | solution.py:30
  318.8 9.8 %custom-call.42 = f32[1,128,128]{1,2,0:T(8,128)S(1)} custom-call(f32[1,128,128]{2,1,0:T(8,128)S(1)} %get-tuple-element.31), custom_call_target="InvertDiagBlocksLowerTriangular" | custom-call | tf_op jit(solution)/shard_map/jit(cholesky)/cholesky | solution.py:30
  330.3 11.8 %cholesky.253 = f32[128,128]{1,0:T(8,128)S(1)} custom-call(f32[128,128]{1,0:T(8,128)S(1)} %convolution_subtract_fusion.8), custom_call_target="Cholesky" | custom-call | tf_op jit(solution)/shard_map/jit(cholesky)/cholesky | solution.py:30
  347.0 8.6 %while.1 = (s32[]{:T(128)}, f32[512,512]{0,1:T(8,128)S(1)}, s32[4,2]{0,1:T(2,128)S(1)}, f32[4,128,128]{2,1,0:T(8,128)S(1)}, s32[]{:T(128)}) while((s32[]{:T(128)}, f32[512,512]{0,1:T(8,128)S(1)}, s32[4,2]{0,1:T(2,128)S(1)}, f32[4,128,128]{2,1,0:T(8,128)S(1)}, s32[]{:T(128)}) %tuple.29), condition=%wide.while_cond, body=%wide.while_body.sunk | while | flops 2 | bytes 393329 | solution.py:32
  347.7 1.4 dynamic-slice.7
  349.9 1.4 dynamic-slice.7
  354.2 1.4 dynamic-slice.7
  355.7 39.3 %custom-call.43 = f32[4,128,128]{1,2,0:T(8,128)S(1)} custom-call(f32[4,128,128]{2,1,0:T(8,128)S(1)} %get-tuple-element.9), custom_call_target="InvertDiagBlocksLowerTriangular" | custom-call | tf_op jit(solution)/shard_map/jit(_cho_solve)/triangular_solve | solution.py:32
  404.2 5.2 %fusion.71 = f32[1,2048]{1,0:T(1,128)} fusion(f32[512,2048]{1,0:T(8,128)} %all-reduce.6.cloned.1.call-done, f32[128,1]{0,1:T(1,128)S(1)} %convolution_bitcast_fusion.5, f32[128,1]{0,1:T(1,128)S(1)} %convolution_bitcast_fusion.3, f32[128,1]{0,1:T(1,128)S(1)} %convolution_bitcast_fusion.1, f32[128,1]{0,1:T(1,128)S(1)} %convolution_bitcast_fusion), kind=kOutput, calls=%fused_computation.115 | convolution fusion | flops 12584448 | bytes 4204544 | tf_op jit(solution)/shard_map/dot_general | solution.py:45
  409.4 10.1 %subtract_multiply_fusion = f32[2048,512]{1,0:T(8,128)} fusion(f32[2048,512]{1,0:T(8,128)S(1)} %copy-done, f32[512,2048]{1,0:T(8,128)} %all-reduce.6.cloned.1.call-done, f32[128,512]{1,0:T(8,128)S(1)} %fusion.69, f32[128,512]{1,0:T(8,128)S(1)} %fusion.66, f32[128,512]{1,0:T(8,128)S(1)} %fusion.63, f32[128,512]{1,0:T(8,128)S(1)} %fusion.61), kind=kOutput, calls=%fused_computation.2 | convolution fusion | flops 6445334528 | bytes 13631488 | tf_op jit(solution)/shard_map/dot_general | solution.py:37
  (100 shorter events, 20.9 us)
Async XLA Ops:
  7.2 70.6 %all-gather.2.cloned.1.call-start = ((), (), s32[]{:S(2)}) async-start(), calls=%async_computation.1 | async-start | bytes 4456448 | tf_op jit(solution)/shard_map/all_gather | solution.py:19
  30.5 118.9 %all-reduce.10.cloned.1.call-start = ((), (), s32[]{:S(2)}) async-start(), calls=%async_computation.4 | async-start | bytes 4194304 | tf_op jit(solution)/shard_map/psum | solution.py:9
  90.4 168.0 %all-reduce.8.cloned.1.call-start = ((), (), s32[]{:S(2)}) async-start(), calls=%async_computation.3 | async-start | bytes 2097152 | tf_op jit(solution)/shard_map/psum | solution.py:29
  149.4 4.8 %copy-start.1 = (f32[512,512]{0,1:T(8,128)S(1)}, f32[512,512]{0,1:T(8,128)}, u32[]{:S(2)}) copy-start(f32[512,512]{0,1:T(8,128)} %get-tuple-element.26) | copy-start | bytes 3145732
  154.0 250.2 %all-reduce.6.cloned.1.call-start = ((), (), s32[]{:S(2)}) async-start(), calls=%async_computation.2 | async-start | bytes 8388608 | tf_op jit(solution)/shard_map/psum | solution.py:36
  170.8 87.6 %copy-start.6 = (f32[512]{0:T(512)S(1)}, f32[512]{0:T(512)}, u32[]{:S(2)}) copy-start(f32[512]{0:T(512)} %param.6) | copy-start | bytes 6148
  258.4 1.8 copy-start.3
  260.4 44.5 %copy-start.4 = (f32[512,512]{1,0:T(8,128)}, f32[512,512]{1,0:T(8,128)S(1)}, u32[]{:S(2)}) copy-start(f32[512,512]{1,0:T(8,128)S(1)} %fusion.19) | copy-start | bytes 3145732
  294.7 100.3 %copy-start.5 = (f32[512]{0:T(512)S(1)}, f32[512]{0:T(512)}, u32[]{:S(2)}) copy-start(f32[512]{0:T(512)} %param.7) | copy-start | bytes 6148
  305.1 92.8 %copy-start.2 = (f32[512,512]{1,0:T(8,128)S(1)}, f32[512,512]{1,0:T(8,128)}, u32[]{:S(2)}) copy-start(f32[512,512]{1,0:T(8,128)} %get-tuple-element.27) | copy-start | bytes 3145732
  404.2 5.2 %copy-start = (f32[2048,512]{1,0:T(8,128)S(1)}, f32[2048,512]{1,0:T(8,128)}, u32[]{:S(2)}) copy-start(f32[2048,512]{1,0:T(8,128)} %param.5) | copy-start | bytes 12582916
Sparse Core Ops, SparseCore 0:
  30.6 47.1 all-gather.1
  90.5 58.8 all-reduce.9
  154.1 104.2 all-reduce.7
  262.2 103.4 all-reduce.5
where the time goes:
time: 432 us; the launch traced here: 426 us
  waiting for transfers between devices  194 us (45%)
  other arithmetic  122 us (28%)
  matrix products  59.8 us (14%)
  blocking collectives  22.4 us (5%)
  between operations  17 us (4%)
  local copies, waits for them, and re-layouts  10.3 us (2%)
    psum x1, waiting for transfers between devices, per_device(): system = lax.psum(partial_system, ('grp', 'col')) + jnp.diag(noise)  87.6 us
    another operation x14, other arithmetic, per_device(): lower = jnp.linalg.cholesky(system)  79 us
    psum x1, waiting for transfers between devices, spread(): return lax.psum(jnp.where(mine, value, jnp.zeros_like(value)), axis)  59 us
    all_gather x1, waiting for transfers between devices, per_device(): jac_rows = lax.all_gather(piece, 'col', axis=1, tiled=True)  47.2 us
    another operation x3, other arithmetic, per_device(): solve_e = jax.scipy.linalg.cho_solve((lower, True), innovation)  39.4 us
    all_to_all x1, blocking collectives, per_device(): lax.all_to_all(jacobian, ('grp', 'row', 'col'), split_axis=1, concat_axis...  22.4 us
    dot_general x1, matrix products, per_device(): jnp.dot(jac_cols, covariance.T, precision=high, preferred_element_type=jn...  16.6 us
    dot_general x1, matrix products, per_device(): jnp.dot(jac_rows, covariance, precision=high, preferred_element_type=jnp....  10.2 us
  transfers between devices with their start and end apart: 4, of which 3 were waited for; matrix products, arithmetic and copies ran while one was open for 37% of the time, Pallas kernels for 0%

commit v1 on v0

v1 whole, which is shorter than its diff:
```python
import jax
import jax.numpy as jnp
from jax import lax
from jax.experimental import pallas as pl
from jax.experimental.pallas import tpu as pltpu
from jax.sharding import PartitionSpec as P

HI = lax.Precision.HIGHEST
B = 128
Q = 8
Z = 4
YX = 4


def dot6(a, b):
    return jnp.dot(a, b, precision=HI, preferred_element_type=jnp.float32)


def sweep_block(a):
    n = B // Q
    rows = [a[Q * i:Q * i + Q, :] for i in range(n)]
    lane = lax.broadcasted_iota(jnp.int32, (Q, B), 1)
    sub = lax.broadcasted_iota(jnp.int32, (Q, B), 0)
    for p in range(n):
        r = rows[p]
        cols = [jnp.broadcast_to(r[:, Q * p + j:Q * p + j + 1], (Q, B)) for j in range(Q)]
        for k in range(Q):
            inv = 1.0 / jnp.broadcast_to(cols[k][k:k + 1, :], (Q, B))
            scaled = cols[k] * inv
            new = []
            for j in range(Q):
                if j == k:
                    new.append(jnp.where(sub == k, -inv, scaled))
                else:
                    row = jnp.broadcast_to(cols[j][k:k + 1, :], (Q, B))
                    new.append(jnp.where(sub == k, row * inv, cols[j] - scaled * row))
            row = jnp.broadcast_to(r[k:k + 1, :], (Q, B))
            r = jnp.where(sub == k, row * inv, r - scaled * row)
            cols = new
        for j in range(Q):
            r = jnp.where(lane == Q * p + j, cols[j], r)
        inside = (lane >= Q * p) & (lane < Q * p + Q)
        splat = [jnp.broadcast_to(r[j:j + 1, :], (Q, B)) for j in range(Q)]
        for b in [(p + 1 + i) % n for i in range(n - 1)]:
            old = rows[b]
            acc = jnp.where(inside, 0.0, old)
            for j in range(Q):
                acc = acc - jnp.broadcast_to(old[:, Q * p + j:Q * p + j + 1], (Q, B)) * splat[j]
            rows[b] = acc
        rows[p] = r
    return jnp.concatenate(rows, axis=0)


def inverse_kernel(s_ref, noise_ref, out_ref):
    m = out_ref.shape[0]
    n = m // B
    row_id = lax.broadcasted_iota(jnp.int32, (m, m), 0)
    col_id = lax.broadcasted_iota(jnp.int32, (m, m), 1)
    out_ref[...] = s_ref[...] + jnp.where(row_id == col_id, noise_ref[...], 0.0)

    def step(k, carry):
        at = pl.ds(pl.multiple_of(k * B, B), B)
        neg = sweep_block(out_ref[at, at])
        strip = out_ref[at, :]
        left = out_ref[:, at]
        col = lax.broadcasted_iota(jnp.int32, (B, m), 1)
        here = (col >= k * B) & (col < k * B + B)
        t = jnp.where(here, jnp.concatenate([neg] * n, axis=1), -dot6(neg, strip))
        big = lax.broadcasted_iota(jnp.int32, (m, m), 1)
        keep = jnp.where((big >= k * B) & (big < k * B + B), 0.0, out_ref[...])
        out_ref[...] = keep - dot6(left, t)
        out_ref[at, :] = t
        return carry

    lax.fori_loop(0, n, step, 0)


def negative_inverse(system, noise):
    vmem = pl.BlockSpec(memory_space=pltpu.VMEM)
    return pl.pallas_call(
        inverse_kernel,
        out_shape=jax.ShapeDtypeStruct(system.shape, jnp.float32),
        in_specs=[vmem, vmem],
        out_specs=vmem,
        compiler_params=pltpu.CompilerParams(vmem_limit_bytes=24 * 2**20),
        name="inverse",
    )(system, noise)


def split(a):
    high = a.astype(jnp.bfloat16)
    return high, (a - high.astype(jnp.float32)).astype(jnp.bfloat16)


def final_kernel(z_ref, neg_ref, innov_ref, p0, p1, p2, p3, rows_ref, cov_ref, new_ref, delta_ref, yh, yl, u):
    @pl.when(pl.program_id(0) == 0)
    def _():
        neg = neg_ref[...]
        for j, piece in enumerate((p0, p1, p2, p3)):
            place = lax.rem(z_ref[0] + (Z - j), Z)
            at = pl.ds(pl.multiple_of(place * B, B), B)
            yh[:, at], yl[:, at] = split(dot6(neg, piece[...]))
        u[...] = -jnp.sum(neg * innov_ref[...], axis=1, keepdims=True)

    chunk = rows_ref[0]
    ch, cl = split(chunk)

    def tdot(a, b):
        return lax.dot_general(a, b, (((0,), (0,)), ((), ())), preferred_element_type=jnp.float32)

    change = tdot(ch, yh[...]) + (tdot(ch, yl[...]) + tdot(cl, yh[...]))
    new_ref[...] = (cov_ref[...] + change) / 0.98
    delta_ref[0] = jnp.sum(chunk * u[...], axis=0, keepdims=True)


def finish(z, neg, innovation, pieces, prod_rows, covariance):
    m = neg.shape[0]
    rows_dev, cols_dev = covariance.shape
    whole = lambda *shape: pl.BlockSpec(shape, lambda i: (0,) * len(shape))
    place = lambda i: (i % YX) * Z + i // YX
    new, delta = pl.pallas_call(
        final_kernel,
        grid=(rows_dev // B,),
        out_shape=(
            jax.ShapeDtypeStruct((rows_dev, cols_dev), jnp.float32),
            jax.ShapeDtypeStruct((rows_dev // B, 1, B), jnp.float32),
        ),
        in_specs=[
            pl.BlockSpec(memory_space=pltpu.SMEM),
            whole(m, m),
            whole(1, m),
            *[whole(m, B)] * 4,
            pl.BlockSpec((1, m, B), lambda i: (i, 0, 0)),
            pl.BlockSpec((B, cols_dev), lambda i: (place(i), 0)),
        ],
        out_specs=(
            pl.BlockSpec((B, cols_dev), lambda i: (place(i), 0)),
            pl.BlockSpec((1, 1, B), lambda i: (place(i), 0, 0)),
        ),
        scratch_shapes=[
            pltpu.VMEM((m, cols_dev), jnp.bfloat16),
            pltpu.VMEM((m, cols_dev), jnp.bfloat16),
            pltpu.VMEM((m, 1), jnp.float32),
        ],
        compiler_params=pltpu.CompilerParams(vmem_limit_bytes=24 * 2**20),
        name="finish",
    )(z, neg, innovation, *pieces, prod_rows, covariance)
    return delta.reshape(rows_dev), new


def exchange(value, axes):
    return lax.all_to_all(value, axes, split_axis=0, concat_axis=0, tiled=True)


def per_device(jacobian, covariance, noise, innovation):
    m = noise.shape[0]
    mine = jacobian.shape[0]
    rows_dev, cols_dev = covariance.shape
    g = lax.axis_index("grp")
    z = lax.axis_index("row")
    reorder = lambda v: v.reshape(8, 16, mine).transpose(1, 0, 2).reshape(1, m)
    noise, innovation = reorder(noise), reorder(innovation)

    sent = jacobian.reshape(mine, 8, rows_dev).transpose(1, 0, 2)
    part = exchange(sent, ("grp", "row")).reshape(8 * mine, rows_dev)
    jac_rows = lax.all_gather(part, "col", axis=0, tiled=True)

    sent = jacobian.reshape(mine, 2, 16, Z, B).transpose(1, 3, 2, 0, 4).reshape(128, mine, B)
    piece = exchange(sent, ("grp", "row", "col")).reshape(8, 16, mine, B)
    piece = piece.transpose(1, 0, 2, 3).reshape(1, m, B)
    jac_cols = exchange(jnp.broadcast_to(piece, (Z, m, B)), ("row",))
    jac_cols = jac_cols.transpose(1, 0, 2).reshape(m, cols_dev)

    partial = jnp.dot(jac_rows, covariance, precision=HI, preferred_element_type=jnp.float32)
    system = jnp.dot(partial, jac_cols.T, precision=HI, preferred_element_type=jnp.float32)

    half = m // 2
    swap = [(0, 1), (1, 0)]
    own = lax.dynamic_slice_in_dim(system, g * half, half, 0)
    other = lax.dynamic_slice_in_dim(system, (1 - g) * half, half, 0)
    own = own + lax.ppermute(other, "grp", swap)
    got = exchange(own.reshape(64, half // 64, m), ("row", "col"))
    share = jnp.sum(got, axis=0, keepdims=True)
    own = exchange(jnp.broadcast_to(share, (64, half // 64, m)), ("row", "col")).reshape(half, m)
    other = lax.ppermute(own, "grp", swap)
    first = jnp.where(g == 0, own, other)
    second = jnp.where(g == 0, other, own)
    neg = negative_inverse(jnp.concatenate([first, second], axis=0), noise)

    spots = [(a, b, x) for a in range(Z) for b in range(YX) for x in range(YX)]
    number = lambda a, b, x: (a * YX + b) * YX + x
    total = None
    for j in range(Z):
        sub = lax.rem(z + j, Z)
        out = lax.dynamic_slice_in_dim(partial, sub * B, B, 1)
        perm = [(number(a, b, x), number(b, (a + j) % Z, x)) for a, b, x in spots]
        came = lax.ppermute(out, ("row", "col"), perm)
        total = came if total is None else total + came
    prod_rows = lax.all_gather(total, "col", axis=0)
    pieces = []
    for j in range(Z):
        perm = [(number(a, b, x), number((b + j) % Z, a, x)) for a, b, x in spots]
        pieces.append(lax.ppermute(total, ("row", "col"), perm))

    return finish(z.reshape(1), neg, innovation, pieces, prod_rows, covariance)


def solution(mesh):
    in_specs = (P(("grp", "row", "col"), None), P(("grp", "row"), "col"), P(), P())
    out_specs = (P(("grp", "row")), P(("grp", "row"), "col"))
    return jax.shard_map(
        per_device, mesh=mesh, in_specs=in_specs, out_specs=out_specs, check_vma=False
    )
```

time: 432 us -> 262 us (0.61)
  other arithmetic: 122 us -> 1.13 us
  waiting for transfers between devices: 194 us -> 97.9 us
  matrix products: 59.8 us -> 11.1 us
  blocking collectives: 22.4 us -> 69.9 us
  Pallas kernels: 0 us -> 36.1 us
  starting transfers between devices: 0.34 us -> 19.6 us
    psum x3 -> x0, waiting for transfers between devices: 147 us -> none  [the longest x1 87.6 us: per_device(): system = lax.psum(partial_system, ('grp', 'col')) + jnp.diag(noise)]
    another operation x17 -> x0, other arithmetic: 118 us -> none  [the longest x14 79 us: per_device(): lower = jnp.linalg.cholesky(system)]
    all_to_all x1 -> x4, blocking collectives: 22.4 us -> 69.9 us  [exchange(): return lax.all_to_all(value, axes, split_axis=0, concat_axis=0, tiled=True)]
    pallas_call x0 -> x2, Pallas kernels: none -> 36.1 us  [the longest x1 23.3 us: negative_inverse(): pl.pallas_call(inverse_kernel, out_shape=jax.ShapeDtypeStruct(system.shap...]
    dot_general x5 -> x2, matrix products: 46.6 us -> 11.1 us  [the longest x1 9.26 us: per_device(): jnp.dot(jac_rows, covariance, precision=HI, preferred_element_type=jnp.fl...]
    ppermute x0 -> x10, waiting for transfers between devices: none -> 32.3 us  [the longest x4 21 us: per_device(): pieces.append(lax.ppermute(total, ('row', 'col'), perm))]
    ppermute x0 -> x10, starting transfers between devices: none -> 16 us  [the longest x4 7.89 us: per_device(): came = lax.ppermute(out, ('row', 'col'), perm)]
    all_to_all x0 -> x1, waiting for transfers between devices: none -> 14.3 us  [exchange(): return lax.all_to_all(value, axes, split_axis=0, concat_axis=0, tiled=True)]
  transfers between devices with their start and end apart: 4 -> 13, of which waited for: 3 -> 6; matrix products, arithmetic and copies ran while one was open for 37% -> 2% of each run, Pallas kernels for 0% -> 9%
where the time goes in v1:
time: 262 us; the launch traced here: 258 us
  waiting for transfers between devices  97.9 us (37%)
  blocking collectives  69.9 us (27%)
  Pallas kernels  36.1 us (14%)
  starting transfers between devices  19.6 us (7%)
  between operations  14.3 us (5%)
  matrix products  11.1 us (4%)
  local copies, waits for them, and re-layouts  7.97 us (3%)
    all_to_all x4, blocking collectives, exchange(): return lax.all_to_all(value, axes, split_axis=0, concat_axis=0, tiled=True)  69.9 us
    all_gather x1, waiting for transfers between devices, per_device(): jac_rows = lax.all_gather(part, 'col', axis=0, tiled=True)  51.3 us
    pallas_call x1, Pallas kernels, negative_inverse(): pl.pallas_call(inverse_kernel, out_shape=jax.ShapeDtypeStruct(system.shap...  23.3 us
    ppermute x4, waiting for transfers between devices, per_device(): pieces.append(lax.ppermute(total, ('row', 'col'), perm))  21 us
    all_to_all x1, waiting for transfers between devices, exchange(): return lax.all_to_all(value, axes, split_axis=0, concat_axis=0, tiled=True)  14.3 us
    pallas_call x1, Pallas kernels, finish(): pl.pallas_call(final_kernel, grid=(rows_dev // B,), out_shape=(jax.ShapeD...  12.8 us
    ppermute x4, waiting for transfers between devices, per_device(): came = lax.ppermute(out, ('row', 'col'), perm)  9.74 us
    dot_general x1, matrix products, per_device(): jnp.dot(jac_rows, covariance, precision=HI, preferred_element_type=jnp.fl...  9.26 us
  transfers between devices with their start and end apart: 13, of which 6 were waited for; matrix products, arithmetic and copies ran while one was open for 2% of the time, Pallas kernels for 9%

profile of v1, /device:TPU:1, one launch (start us, length us, event | category | flops | bytes accessed | tf_op | source)
XLA Modules:
  0.0 258.0 jit_solution(3349943191704984771)
XLA Ops:
  7.2 13.4 %all_to_all.25 = f32[8,4,2048]{2,1,0:T(4,128)S(1)} all-to-all(f32[8,4,2048]{2,1,0:T(4,128)} %bitcast.23), channel_id=1, replica_groups=mesh['grp'=2,'row'=4,'col'=16] {'grp','row'}, dimensions={0} | all-to-all | bytes 524288 | tf_op jit(solution)/shard_map/all_to_all | solution.py:152
  21.5 51.3 %all-gather.4.cloned.1.call-done = f32[512,2048]{1,0:T(8,128)} async-done(((f32[32,2048]{1,0:T(8,128)}), f32[512,2048]{1,0:T(8,128)}) %all-gather.4.cloned.1.call-update) | async-done | bytes 4194320 | tf_op jit(solution)/shard_map/all_gather | solution.py:166
  72.8 9.3 %fusion = f32[512,512]{1,0:T(8,128)S(1)} fusion(f32[512,2048]{1,0:T(8,128)} %all-gather.4.cloned.1.call-done, f32[2048,512]{1,0:T(8,128)} %cov_ref.1), kind=kOutput, calls=%fused_computation.10 | convolution fusion | flops 6442450944 | bytes 9437184 | tf_op jit(solution)/shard_map/dot_general | solution.py:174
  82.2 1.2 collective-permute-start.3
  83.4 4.8 %collective-permute-start.5 = (f32[512,128]{1,0:T(8,128)S(1)}, f32[512,128]{1,0:T(8,128)S(1)}, u32[]{:S(2)}, u32[]{:S(2)}) collective-permute-start(f32[512,128]{1,0:T(8,128)S(1)} %get-tuple-element.7), channel_id=1, source_target_pairs={{0,12},{1,13},{2,14},{3,15},{4,28},{5,29},{6,30},{7,31},{8,44},{9,... | collective-permute-start | bytes 786440 | tf_op jit(solution)/shard_map/ppermute | solution.py:197
  88.2 1.2 collective-permute-start.4
  90.7 9.2 %collective-permute-done.5 = f32[512,128]{1,0:T(8,128)S(1)} collective-permute-done((f32[512,128]{1,0:T(8,128)S(1)}, f32[512,128]{1,0:T(8,128)S(1)}, u32[]{:S(2)}, u32[]{:S(2)}) %collective-permute-start.5) | collective-permute-done | bytes 262176 | tf_op jit(solution)/shard_map/ppermute | solution.py:197
  101.1 24.2 %all_to_all.26 = f32[128,4,128]{2,1,0:T(4,128)S(1)} all-to-all(f32[128,4,128]{2,1,0:T(4,128)S(1)} %copy.19), channel_id=1, replica_groups=mesh['grp'=2,'row'=4,'col'=16] {'grp','row','col'}, dimensions={0} | all-to-all | bytes 524288 | tf_op jit(solution)/shard_map/all_to_all | solution.py:152
  125.6 1.1 broadcast_in_dim.14
  126.7 3.5 %all-to-all-start.2 = ((f32[4,512,128]{1,2,0:T(8,128)}), f32[4,512,128]{1,2,0:T(8,128)S(1)}, u32[]{:S(2)}, u32[]{:S(2)}) async-start(f32[4,512,128]{1,2,0:T(8,128)} %broadcast_in_dim.14), calls=%async_computation.2 | async-start | bytes 2097152 | tf_op jit(solution)/shard_map/all_to_all | solution.py:152
  130.2 14.3 %all-to-all-done.2 = f32[4,512,128]{1,2,0:T(8,128)S(1)} async-done(((f32[4,512,128]{1,2,0:T(8,128)}), f32[4,512,128]{1,2,0:T(8,128)S(1)}, u32[]{:S(2)}, u32[]{:S(2)}) %all-to-all-start.2) | async-done | bytes 1048608 | tf_op jit(solution)/shard_map/all_to_all | solution.py:152
  144.5 1.8 fusion.1
  146.4 1.8 collective-permute-start
  148.2 1.5 collective-permute-done
  150.0 17.0 %all_to_all.27 = f32[64,4,512]{2,1,0:T(4,128)S(1)} all-to-all(f32[64,4,512]{2,1,0:T(4,128)S(1)} %reshape.56), channel_id=1, replica_groups=mesh['grp'=2,'row'=4,'col'=16] {'row','col'}, dimensions={0} | all-to-all | bytes 1048576 | tf_op jit(solution)/shard_map/all_to_all | solution.py:152
  167.2 15.3 %all_to_all.28 = f32[64,4,512]{2,1,0:T(4,128)S(1)} all-to-all(f32[64,4,512]{2,1,0:T(4,128)S(1)} %broadcast_in_dim.15), channel_id=1, replica_groups=mesh['grp'=2,'row'=4,'col'=16] {'row','col'}, dimensions={0} | all-to-all | bytes 1048576 | tf_op jit(solution)/shard_map/all_to_all | solution.py:152
  182.7 3.4 %collective-permute-start.1 = (f32[256,512]{1,0:T(8,128)S(1)}, f32[256,512]{1,0:T(8,128)S(1)}, u32[]{:S(2)}, u32[]{:S(2)}) collective-permute-start(f32[256,512]{1,0:T(8,128)S(1)} %reshape.57), channel_id=1, source_target_pairs={{0,64},{64,0},{1,65},{65,1},{2,66},{66,2},{3,67},{67,3},{4,68},{68... | collective-permute-start | bytes 1572872 | tf_op jit(solution)/shard_map/ppermute | solution.py:185
  186.6 0.9 collective-permute-start.9
  187.4 1.3 collective-permute-start.8
  189.7 23.3 %inverse.1.neg_ref = f32[512,512]{1,0:T(8,128)S(1)} custom-call(f32[512,512]{1,0:T(8,128)S(1)} %pad_maximum_fusion.s_ref, f32[1,512]{1,0:T(1,128)S(1)} %reshape.59.noise_ref), custom_call_target="tpu_custom_call" | custom-call | tf_op jit(solution)/shard_map/inverse/pallas_call | solution.py:80
  213.0 21.0 %collective-permute-done.7.p1 = f32[512,128]{1,0:T(8,128)S(1)} collective-permute-done((f32[512,128]{1,0:T(8,128)S(1)}, f32[512,128]{1,0:T(8,128)S(1)}, u32[]{:S(2)}, u32[]{:S(2)}) %collective-permute-start.7) | collective-permute-done | bytes 262176 | tf_op jit(solution)/shard_map/ppermute | solution.py:203
  234.0 2.2 copy-done
  236.2 2.2 copy-done.1
  238.4 12.8 %finish.1 = (f32[2048,512]{1,0:T(8,128)}, f32[16,1,128]{2,1,0:T(1,128)}) custom-call(s32[1]{0:T(128)} %bitcast.z_ref, f32[512,512]{1,0:T(8,128)S(1)} %inverse.1.neg_ref, f32[1,512]{1,0:T(1,128)S(1)} %reshape.61.innov_ref, f32[512,128]{1,0:T(8,128)S(1)} %collective-permute-done.6.p0, f32[512,128]{1,0:T(8,128)S(1)} %collective-permute-done.7.p1, ...), custom_call_target="tpu_custom_call" | custom-call | tf_op jit(solution)/shard_map/finish/pallas_call | solution.py:121
  (47 shorter events, 5.8 us)
Async XLA Ops:
  7.2 65.6 %all-gather.4.cloned.1.call-start = ((), (), s32[]{:S(2)}) async-start(), calls=%async_computation.5 | async-start | bytes 4456448 | tf_op jit(solution)/shard_map/all_gather | solution.py:166
  21.4 212.6 %all-gather.6.cloned.1.call-start = ((), (), s32[]{:S(2)}) async-start(), calls=%async_computation.6 | async-start | bytes 4456448 | tf_op jit(solution)/shard_map/all_gather | solution.py:199
  21.5 79.2 %copy-start.3 = (f32[4,16384]{1,0:T(4,128)S(1)}, f32[4,16384]{1,0:T(4,128)}, u32[]{:S(2)}) copy-start(f32[4,16384]{1,0:T(4,128)} %param.4) | copy-start | bytes 786436
  82.2 8.5 %collective-permute-start.3 = (f32[512,128]{1,0:T(8,128)S(1)}, f32[512,128]{1,0:T(8,128)S(1)}, u32[]{:S(2)}, u32[]{:S(2)}) collective-permute-start(f32[512,128]{1,0:T(8,128)S(1)} %get-tuple-element.6), channel_id=1, source_target_pairs={{0,4},{1,5},{2,6},{3,7},{4,20},{5,21},{6,22},{7,23},{8,36},{9,37},... | collective-permute-start | bytes 786440 | tf_op jit(solution)/shard_map/ppermute | solution.py:197
  83.4 16.4 %collective-permute-start.5 = (f32[512,128]{1,0:T(8,128)S(1)}, f32[512,128]{1,0:T(8,128)S(1)}, u32[]{:S(2)}, u32[]{:S(2)}) collective-permute-start(f32[512,128]{1,0:T(8,128)S(1)} %get-tuple-element.7), channel_id=1, source_target_pairs={{0,12},{1,13},{2,14},{3,15},{4,28},{5,29},{6,30},{7,31},{8,44},{9,... | collective-permute-start | bytes 786440 | tf_op jit(solution)/shard_map/ppermute | solution.py:197
  88.2 11.6 %collective-permute-start.4 = (f32[512,128]{1,0:T(8,128)S(1)}, f32[512,128]{1,0:T(8,128)S(1)}, u32[]{:S(2)}, u32[]{:S(2)}) collective-permute-start(f32[512,128]{1,0:T(8,128)S(1)} %get-tuple-element.8), channel_id=1, source_target_pairs={{0,8},{1,9},{2,10},{3,11},{4,24},{5,25},{6,26},{7,27},{8,40},{9,41... | collective-permute-start | bytes 786440 | tf_op jit(solution)/shard_map/ppermute | solution.py:197
  89.4 10.4 %collective-permute-start.2 = (f32[512,128]{1,0:T(8,128)S(1)}, f32[512,128]{1,0:T(8,128)S(1)}, u32[]{:S(2)}, u32[]{:S(2)}) collective-permute-start(f32[512,128]{1,0:T(8,128)S(1)} %get-tuple-element.9), channel_id=1, source_target_pairs={{0,0},{1,1},{2,2},{3,3},{4,16},{5,17},{6,18},{7,19},{8,32},{9,33},... | collective-permute-start | bytes 786440 | tf_op jit(solution)/shard_map/ppermute | solution.py:197
  126.7 17.8 %all-to-all-start.2 = ((f32[4,512,128]{1,2,0:T(8,128)}), f32[4,512,128]{1,2,0:T(8,128)S(1)}, u32[]{:S(2)}, u32[]{:S(2)}) async-start(f32[4,512,128]{1,2,0:T(8,128)} %broadcast_in_dim.14), calls=%async_computation.2 | async-start | bytes 2097152 | tf_op jit(solution)/shard_map/all_to_all | solution.py:152
  146.3 39.7 %copy-start.4 = (f32[512]{0:T(512)S(1)}, f32[512]{0:T(512)}, u32[]{:S(2)}) copy-start(f32[512]{0:T(512)} %param.6) | copy-start | bytes 6148
  146.3 40.0 %copy-start.5 = (f32[512]{0:T(512)S(1)}, f32[512]{0:T(512)}, u32[]{:S(2)}) copy-start(f32[512]{0:T(512)} %param.7) | copy-start | bytes 6148
  146.4 40.2 %copy-start.2 = (f32[512,128]{1,0:T(8,128)S(1)}, f32[512,128]{1,0:T(8,128)}, u32[]{:S(2)}) copy-start(f32[512,128]{1,0:T(8,128)} %add_add_fusion) | copy-start | bytes 786436
  146.4 3.3 %collective-permute-start = (f32[256,512]{1,0:T(8,128)S(1)}, f32[256,512]{1,0:T(8,128)S(1)}, u32[]{:S(2)}, u32[]{:S(2)}) collective-permute-start(f32[256,512]{1,0:T(8,128)S(1)} %constant_dynamic-slice_fusion.4), channel_id=1, source_target_pairs={{0,64},{64,0},{1,65},{65,1},{2,66},{66,2},{3,67},{67,3},{4,68},{68... | collective-permute-start | bytes 1572872 | tf_op jit(solution)/shard_map/ppermute | solution.py:181
  182.7 6.9 %collective-permute-start.1 = (f32[256,512]{1,0:T(8,128)S(1)}, f32[256,512]{1,0:T(8,128)S(1)}, u32[]{:S(2)}, u32[]{:S(2)}) collective-permute-start(f32[256,512]{1,0:T(8,128)S(1)} %reshape.57), channel_id=1, source_target_pairs={{0,64},{64,0},{1,65},{65,1},{2,66},{66,2},{3,67},{67,3},{4,68},{68... | collective-permute-start | bytes 1572872 | tf_op jit(solution)/shard_map/ppermute | solution.py:185
  186.6 26.4 %collective-permute-start.9 = (f32[512,128]{1,0:T(8,128)S(1)}, f32[512,128]{1,0:T(8,128)S(1)}, u32[]{:S(2)}, u32[]{:S(2)}) collective-permute-start(f32[512,128]{1,0:T(8,128)S(1)} %copy-done.2), channel_id=1, source_target_pairs={{0,48},{1,49},{2,50},{3,51},{4,0},{5,1},{6,2},{7,3},{8,16},{9,17},... | collective-permute-start | bytes 786440 | tf_op jit(solution)/shard_map/ppermute | solution.py:203
  187.4 25.6 %collective-permute-start.8 = (f32[512,128]{1,0:T(8,128)S(1)}, f32[512,128]{1,0:T(8,128)S(1)}, u32[]{:S(2)}, u32[]{:S(2)}) collective-permute-start(f32[512,128]{1,0:T(8,128)S(1)} %copy-done.2), channel_id=1, source_target_pairs={{0,32},{1,33},{2,34},{3,35},{4,48},{5,49},{6,50},{7,51},{8,0},{9,1... | collective-permute-start | bytes 786440 | tf_op jit(solution)/shard_map/ppermute | solution.py:203
  188.7 45.3 %collective-permute-start.7 = (f32[512,128]{1,0:T(8,128)S(1)}, f32[512,128]{1,0:T(8,128)S(1)}, u32[]{:S(2)}, u32[]{:S(2)}) collective-permute-start(f32[512,128]{1,0:T(8,128)S(1)} %copy-done.2), channel_id=1, source_target_pairs={{0,16},{1,17},{2,18},{3,19},{4,32},{5,33},{6,34},{7,35},{8,48},{9,... | collective-permute-start | bytes 786440 | tf_op jit(solution)/shard_map/ppermute | solution.py:203
  188.9 45.2 %collective-permute-start.6 = (f32[512,128]{1,0:T(8,128)S(1)}, f32[512,128]{1,0:T(8,128)S(1)}, u32[]{:S(2)}, u32[]{:S(2)}) collective-permute-start(f32[512,128]{1,0:T(8,128)S(1)} %copy-done.2), channel_id=1, source_target_pairs={{0,0},{1,1},{2,2},{3,3},{4,16},{5,17},{6,18},{7,19},{8,32},{9,33},... | collective-permute-start | bytes 786440 | tf_op jit(solution)/shard_map/ppermute | solution.py:203
  234.0 2.2 copy-start
  236.2 2.2 copy-start.1
Sparse Core Ops, SparseCore 0:
  21.5 51.2 all-gather.3
  100.8 56.7 all-gather.5

commit v2 on v1

v2 whole, which is shorter than its diff:
```python
import functools

import jax
import jax.numpy as jnp
from jax import lax
from jax.experimental import pallas as pl
from jax.experimental.pallas import tpu as pltpu
from jax.sharding import PartitionSpec as P

HI = lax.Precision.HIGHEST
B = 128
Q = 8
RING = 4
SHIFT = (0, -1, 1, 2)


def dot6(a, b):
    return jnp.dot(a, b, precision=HI, preferred_element_type=jnp.float32)


def sweep_block(a):
    n = B // Q
    rows = [a[Q * i:Q * i + Q, :] for i in range(n)]
    lane = lax.broadcasted_iota(jnp.int32, (Q, B), 1)
    sub = lax.broadcasted_iota(jnp.int32, (Q, B), 0)
    for p in range(n):
        r = rows[p]
        cols = [jnp.broadcast_to(r[:, Q * p + j:Q * p + j + 1], (Q, B)) for j in range(Q)]
        for k in range(Q):
            inv = 1.0 / jnp.broadcast_to(cols[k][k:k + 1, :], (Q, B))
            scaled = cols[k] * inv
            new = []
            for j in range(Q):
                if j == k:
                    new.append(jnp.where(sub == k, -inv, scaled))
                else:
                    row = jnp.broadcast_to(cols[j][k:k + 1, :], (Q, B))
                    new.append(jnp.where(sub == k, row * inv, cols[j] - scaled * row))
            row = jnp.broadcast_to(r[k:k + 1, :], (Q, B))
            r = jnp.where(sub == k, row * inv, r - scaled * row)
            cols = new
        for j in range(Q):
            r = jnp.where(lane == Q * p + j, cols[j], r)
        inside = (lane >= Q * p) & (lane < Q * p + Q)
        splat = [jnp.broadcast_to(r[j:j + 1, :], (Q, B)) for j in range(Q)]
        for b in [(p + 1 + i) % n for i in range(n - 1)]:
            old = rows[b]
            acc = jnp.where(inside, 0.0, old)
            for j in range(Q):
                acc = acc - jnp.broadcast_to(old[:, Q * p + j:Q * p + j + 1], (Q, B)) * splat[j]
            rows[b] = acc
        rows[p] = r
    return jnp.concatenate(rows, axis=0)


def inverse_kernel(at_ref, own_ref, other_ref, noise_ref, out_ref):
    m = out_ref.shape[0]
    half = m // 2
    n = m // B
    g = at_ref[0]
    for source, start in ((own_ref, g * half), (other_ref, (1 - g) * half)):
        row_id = lax.broadcasted_iota(jnp.int32, (half, m), 0) + start
        col_id = lax.broadcasted_iota(jnp.int32, (half, m), 1)
        value = source[...] + jnp.where(row_id == col_id, noise_ref[...], 0.0)
        out_ref[pl.ds(pl.multiple_of(start, half), half), :] = value

    def step(k, carry):
        at = pl.ds(pl.multiple_of(k * B, B), B)
        neg = sweep_block(out_ref[at, at])
        strip = out_ref[at, :]
        left = out_ref[:, at]
        col = lax.broadcasted_iota(jnp.int32, (B, m), 1)
        here = (col >= k * B) & (col < k * B + B)
        t = jnp.where(here, jnp.concatenate([neg] * n, axis=1), -dot6(neg, strip))
        big = lax.broadcasted_iota(jnp.int32, (m, m), 1)
        keep = jnp.where((big >= k * B) & (big < k * B + B), 0.0, out_ref[...])
        out_ref[...] = keep - dot6(left, t)
        out_ref[at, :] = t
        return carry

    lax.fori_loop(0, n, step, 0)


VMEM = pl.BlockSpec(memory_space=pltpu.VMEM)
SMEM = pl.BlockSpec(memory_space=pltpu.SMEM)
PARAMS = pltpu.CompilerParams(vmem_limit_bytes=40 * 2**20)


def negative_inverse(at, own, other, noise):
    m = noise.shape[1]
    return pl.pallas_call(
        inverse_kernel,
        out_shape=jax.ShapeDtypeStruct((m, m), jnp.float32),
        in_specs=[SMEM, VMEM, VMEM, VMEM],
        out_specs=VMEM,
        compiler_params=PARAMS,
        cost_estimate=pl.CostEstimate(flops=20 * 10**9, bytes_accessed=2 * 2**20, transcendentals=0),
        name="inverse",
    )(at, own, other, noise)


def split(a):
    high = a.astype(jnp.bfloat16)
    return high, (a - high.astype(jnp.float32)).astype(jnp.bfloat16)


def split3(a):
    high = a.astype(jnp.bfloat16)
    rest = a - high.astype(jnp.float32)
    return (high, *split(rest))


def mul(a, b):
    return jnp.dot(a, b, preferred_element_type=jnp.float32)


def split_kernel(a_ref, *outs):
    for out, value in zip(outs, split3(a_ref[...])):
        out[...] = value


def split_array(a):
    rows, cols = a.shape
    spec = pl.BlockSpec((rows // 4, cols), lambda i: (i, 0))
    return pl.pallas_call(
        split_kernel,
        grid=(4,),
        out_shape=(jax.ShapeDtypeStruct(a.shape, jnp.bfloat16),) * 3,
        in_specs=[spec],
        out_specs=(spec,) * 3,
        compiler_params=PARAMS,
        name="split",
    )(a)


def product(chunks, parts):
    left = jnp.concatenate([c[...] for c in chunks], axis=0)
    ph, pm, pl_ = parts
    step = 512
    total = None
    for k in range(0, left.shape[1], step):
        jh, jm, jl = split3(left[:, k:k + step])
        h, mid, low = ph[k:k + step, :], pm[k:k + step, :], pl_[k:k + step, :]
        term = mul(jh, h) + ((mul(jh, mid) + mul(jm, h)) + (mul(jh, low) + mul(jm, mid) + mul(jl, h)))
        total = term if total is None else total + term
    return total


def product_kernel(n, *refs):
    refs[n + 3][...] = product(refs[:n], refs[n:n + 3])


def multiply(chunks, parts):
    rows = sum(c.shape[0] for c in chunks)
    cols = parts[0].shape[1]
    work = 12 * rows * cols * parts[0].shape[0]
    return pl.pallas_call(
        functools.partial(product_kernel, len(chunks)),
        out_shape=jax.ShapeDtypeStruct((rows, cols), jnp.float32),
        in_specs=[VMEM] * (len(chunks) + 3),
        out_specs=VMEM,
        compiler_params=PARAMS,
        cost_estimate=pl.CostEstimate(flops=work, bytes_accessed=8 * 2**20, transcendentals=0),
        name="multiply",
    )(*chunks, *parts)


def runs(y, x, own):
    def start(half, dy, dx):
        spot = lax.rem(y + (dy + RING), RING) * RING + lax.rem(x + (dx + RING), RING)
        return (half * RING * RING + spot) * own

    first = lambda step: [start(0, SHIFT[step], d) for d in SHIFT]
    second = lambda step: [start(1, d, SHIFT[step]) for d in SHIFT]
    early = first(0) + second(0)
    middle = first(1) + first(2) + second(1) + second(2)
    late = first(3) + second(3)
    return early, middle, late


def last_kernel(at_ref, c0, c1, c2, c3, ph, pm, pl_, early_ref, middle_ref, out_ref, late_ref):
    late_ref[...] = product((c0, c1, c2, c3), (ph, pm, pl_))
    own = out_ref.shape[1] // (2 * RING * RING)
    z = at_ref[1]
    for ref, starts in zip((early_ref, middle_ref, late_ref), runs(at_ref[2], at_ref[3], own)):
        for i, start in enumerate(starts):
            rows = pl.ds(pl.multiple_of(start, own), own)
            for j in range(RING):
                lanes = pl.ds(pl.multiple_of(lax.rem(z + j, RING) * B, B), B)
                out_ref[j, rows, :] = ref[i * own:(i + 1) * own, lanes]


def multiply_last(at, chunks, parts, early, middle):
    rows = sum(c.shape[0] for c in chunks)
    cols = parts[0].shape[1]
    m = rows + early.shape[0] + middle.shape[0]
    return pl.pallas_call(
        last_kernel,
        out_shape=jax.ShapeDtypeStruct((RING, m, B), jnp.float32),
        in_specs=[SMEM] + [VMEM] * 9,
        out_specs=VMEM,
        scratch_shapes=[pltpu.VMEM((rows, cols), jnp.float32)],
        compiler_params=PARAMS,
        name="multiply_last",
    )(at, *chunks, *parts, early, middle)


def pick_kernel(at_ref, *refs):
    out_ref = refs[-1]
    own = out_ref.shape[0] // (2 * RING * RING)
    starts = sum(runs(at_ref[2], at_ref[3], own), [])
    i = 0
    for ref in refs[:-1]:
        for r in range(0, ref.shape[0], own):
            out_ref[pl.ds(pl.multiple_of(starts[i], own), own), :] = ref[r:r + own, :]
            i += 1


def pick(at, chunks):
    m = sum(c.shape[0] for c in chunks)
    block = lambda rows: pl.BlockSpec((rows, B), lambda i, at: (0, at[3] * RING + at[2]))
    return pl.pallas_call(
        pick_kernel,
        out_shape=jax.ShapeDtypeStruct((m, B), jnp.float32),
        grid_spec=pltpu.PrefetchScalarGridSpec(
            num_scalar_prefetch=1,
            grid=(1,),
            in_specs=[block(c.shape[0]) for c in chunks],
            out_specs=pl.BlockSpec((m, B), lambda i, at: (0, 0)),
        ),
        compiler_params=PARAMS,
        name="pick",
    )(at, *chunks)


def gram_kernel(at_ref, r0, r1, r2, r3, jac_ref, piece_ref, turned_ref, own_ref, other_ref):
    piece = (r0[...] + r1[...]) + (r2[...] + r3[...])
    piece_ref[...] = piece
    turned_ref[...] = piece.T
    half = own_ref.shape[0]
    for out, start in ((own_ref, at_ref[0] * half), (other_ref, (1 - at_ref[0]) * half)):
        out[...] = lax.dot_general(
            piece_ref[pl.ds(pl.multiple_of(start, half), half), :],
            jac_ref[...],
            (((1,), (1,)), ((), ())),
            precision=HI,
            preferred_element_type=jnp.float32,
        )


def gram(at, came, jac):
    m = jac.shape[0]
    shape = lambda *s: jax.ShapeDtypeStruct(s, jnp.float32)
    return pl.pallas_call(
        gram_kernel,
        out_shape=(shape(m, B), shape(B, m), shape(m // 2, m), shape(m // 2, m)),
        in_specs=[SMEM] + [VMEM] * 5,
        out_specs=(VMEM,) * 4,
        compiler_params=PARAMS,
        name="gram",
    )(at, *came, jac)


def final_kernel(at_ref, neg_ref, innov_ref, p0, p1, p2, p3, rows_ref, cov_ref, new_ref, delta_ref, yh, yl, u):
    @pl.when(pl.program_id(0) == 0)
    def _():
        neg = neg_ref[...]
        for j, piece in enumerate((p0, p1, p2, p3)):
            place = lax.rem(at_ref[1] + (RING - j), RING)
            at = pl.ds(pl.multiple_of(place * B, B), B)
            yh[:, at], yl[:, at] = split(dot6(neg, piece[...]))
        u[...] = jnp.broadcast_to(-jnp.sum(neg * innov_ref[...], axis=0, keepdims=True), u.shape)

    for b in range(RING):
        at = slice(b * B, b * B + B)
        rows = rows_ref[b, 0]
        high, low = split(rows)
        change = mul(high, yh[...]) + (mul(high, yl[...]) + mul(low, yh[...]))
        new_ref[at, :] = (cov_ref[at, :] + change) * (1 / 0.98)
        delta = lax.dot_general(
            u[...], rows, (((1,), (1,)), ((), ())), precision=HI, preferred_element_type=jnp.float32
        )
        delta_ref[0, :, at] = delta[0:1, :]


def finish(at, neg, innovation, pieces, prod_rows, covariance):
    m = neg.shape[0]
    rows_dev, cols_dev = covariance.shape
    rows = rows_dev // RING
    whole = lambda *shape: pl.BlockSpec(shape, lambda i: (0,) * len(shape))
    new, delta = pl.pallas_call(
        final_kernel,
        grid=(RING,),
        out_shape=(
            jax.ShapeDtypeStruct((rows_dev, cols_dev), jnp.float32),
            jax.ShapeDtypeStruct((RING, 1, rows), jnp.float32),
        ),
        in_specs=[
            SMEM,
            whole(m, m),
            whole(m, 1),
            *[whole(m, B)] * 4,
            pl.BlockSpec((RING, 1, B, m), lambda i: (0, i, 0, 0)),
            pl.BlockSpec((rows, cols_dev), lambda i: (i, 0)),
        ],
        out_specs=(
            pl.BlockSpec((rows, cols_dev), lambda i: (i, 0)),
            pl.BlockSpec((1, 1, rows), lambda i: (i, 0, 0)),
        ),
        scratch_shapes=[
            pltpu.VMEM((m, cols_dev), jnp.bfloat16),
            pltpu.VMEM((m, cols_dev), jnp.bfloat16),
            pltpu.VMEM((8, m), jnp.float32),
        ],
        compiler_params=PARAMS,
        name="finish",
    )(at, neg, innovation, *pieces, prod_rows.reshape(RING, RING, B, m), covariance)
    return delta.reshape(rows_dev), new


def exchange(value, axes):
    return lax.all_to_all(value, axes, split_axis=0, concat_axis=0, tiled=True)


def shifted(value, axis, by):
    if axis == "row":
        return lax.ppermute(value, "row", [(i, (i + by) % RING) for i in range(RING)])
    spots = [(y, x) for y in range(RING) for x in range(RING)]
    if axis == "x":
        perm = [(y * RING + x, y * RING + (x + by) % RING) for y, x in spots]
    else:
        perm = [(y * RING + x, (y + by) % RING * RING + x) for y, x in spots]
    return lax.ppermute(value, "col", perm)


def tie(*values):
    return lax.optimization_barrier(values)


def both_ways(first, second, axes):
    near = tie(*[shifted(v, axis, by) for v, axis in zip((first, second), axes) for by in (1, -1)])
    h = first.shape[0] // 2
    far = [
        shifted(near[0][:h], axes[0], 1),
        shifted(near[1][h:], axes[0], -1),
        shifted(near[2][:h], axes[1], 1),
        shifted(near[3][h:], axes[1], -1),
    ]
    return near, far


def per_device(jacobian, covariance, noise, innovation):
    m = noise.shape[0]
    mine = jacobian.shape[0]
    rows_dev, cols_dev = covariance.shape
    g, z, col = lax.axis_index("grp"), lax.axis_index("row"), lax.axis_index("col")
    at = jnp.stack([g, z, col // RING, lax.rem(col, RING)]).astype(jnp.int32)
    reorder = lambda v: v.reshape(2, 4, 16, mine).transpose(0, 2, 1, 3).reshape(m)
    noise, innovation = reorder(noise), reorder(innovation)

    sent = jacobian.reshape(mine, 8, rows_dev).transpose(1, 0, 2)
    got = exchange(sent, ("grp", "row")).reshape(8 * mine, rows_dev)
    parts = split_array(covariance)
    half = 4 * mine
    a, b = got[:half], got[half:]
    near, far = both_ways(a, b, ("x", "y"))
    far = tie(*far)
    a4 = jnp.concatenate([a, near[0], near[1], far[0], far[1]], axis=0)
    b4 = jnp.concatenate([b, near[2], near[3], far[2], far[3]], axis=0)
    a4, b4 = tie(a4, b4)
    near, far = both_ways(a4, b4, ("y", "x"))
    early = multiply([a4, b4], parts)
    middle = multiply(near, parts)
    out = multiply_last(at, far, parts, early, middle)

    spots = [(a, b, x) for a in range(RING) for b in range(RING) for x in range(RING)]
    number = lambda a, b, x: (a * RING + b) * RING + x
    came = []
    for j in range(RING):
        perm = [(number(a, b, x), number(b, (a + j) % RING, x)) for a, b, x in spots]
        came.append(lax.ppermute(out[j], ("row", "col"), perm))
    jac = pick(at, [a4, b4, *near, *far])
    piece, turned, own, other = gram(at, came, jac)
    prod_rows = lax.all_gather(turned, "col", axis=0)

    swap = [(0, 1), (1, 0)]
    h = m // 2
    own = own + lax.ppermute(other, "grp", swap)
    perm = [(number(a, b, x), number(b, a, x)) for a, b, x in spots]
    home = lax.ppermute(piece, ("row", "col"), perm)
    summed = exchange(own.reshape(64, h // 64, m), ("row", "col"))
    share = jnp.sum(summed, axis=0, keepdims=True)
    own = exchange(jnp.broadcast_to(share, (64, h // 64, m)), ("row", "col")).reshape(h, m)
    own, home = tie(own, home)
    other = lax.ppermute(own, "grp", swap)
    pieces = [home] + [shifted(home, "row", d) for d in (1, 2, 3)]
    neg = negative_inverse(at, own, other, noise.reshape(1, m))
    return finish(at, neg, innovation.reshape(m, 1), pieces, prod_rows, covariance)


def solution(mesh):
    in_specs = (P(("grp", "row", "col"), None), P(("grp", "row"), "col"), P(), P())
    out_specs = (P(("grp", "row")), P(("grp", "row"), "col"))
    return jax.shard_map(
        per_device, mesh=mesh, in_specs=in_specs, out_specs=out_specs, check_vma=False
    )
```

time: 262 us -> 210 us (0.80); the launches traced: 258 us -> 209 us
  waiting for transfers between devices: 97.9 us -> 24.3 us
  starting transfers between devices: 19.6 us -> 61.3 us
  blocking collectives: 69.9 us -> 38.5 us
  Pallas kernels: 36.1 us -> 50 us
  local copies, waits for them, and re-layouts: 7.97 us -> 20.1 us
  matrix products: 11.1 us -> 0 us
    all_gather x2 -> x1, waiting for transfers between devices: 51.3 us -> 0.02 us  [per_device(): prod_rows = lax.all_gather(turned, 'col', axis=0)]
    ppermute x8 -> x24, starting transfers between devices: 10.8 us -> 42.7 us  [the longest x16 22.2 us: shifted(): return lax.ppermute(value, 'col', perm)]
    all_to_all x4 -> x2, blocking collectives: 69.9 us -> 38.5 us  [exchange(): return lax.all_to_all(value, axes, split_axis=0, concat_axis=0, tiled=True)]
    ppermute x8 -> x24, waiting for transfers between devices: 30.7 us -> 10 us  [the longest x4 5.69 us: per_device(): came.append(lax.ppermute(out[j], ('row', 'col'), perm))]
    pallas_call x2 -> x8, Pallas kernels: 36.1 us -> 50 us  [the longest x1 23.9 us: negative_inverse(): pl.pallas_call(inverse_kernel, out_shape=jax.ShapeDtypeStruct((m, m), jnp...]
    dot_general x2 -> x0, matrix products: 11.1 us -> none  [the longest x1 9.26 us: per_device(): jnp.dot(jac_rows, covariance, precision=HI, preferred_element_type=jnp.fl...]
    unnamed x12 -> x29, local copies, waits for them, and re-layouts: 4.4 us -> 14.3 us
    ppermute x1, starting transfers between devices: 1.8 us -> 7.44 us  [per_device(): own = own + lax.ppermute(other, 'grp', swap)]
  transfers between devices with their start and end apart: 13 -> 28, of which waited for: 6 -> 7; matrix products, arithmetic and copies ran while one was open for 2% -> 2% of each run, Pallas kernels for 9% -> 16%
where the time goes in v2:
time: 210 us; the launch traced here: 209 us
  starting transfers between devices  61.3 us (29%)
  Pallas kernels  50 us (24%)
  blocking collectives  38.5 us (18%)
  waiting for transfers between devices  24.3 us (12%)
  local copies, waits for them, and re-layouts  20.1 us (10%)
  between operations  14.5 us (7%)
    all_to_all x2, blocking collectives, exchange(): return lax.all_to_all(value, axes, split_axis=0, concat_axis=0, tiled=True)  38.5 us
    pallas_call x1, Pallas kernels, negative_inverse(): pl.pallas_call(inverse_kernel, out_shape=jax.ShapeDtypeStruct((m, m), jnp...  23.9 us
    ppermute x16, starting transfers between devices, shifted(): return lax.ppermute(value, 'col', perm)  22.2 us
    unnamed x29, local copies, waits for them, and re-layouts  14.3 us
    all_to_all x1, waiting for transfers between devices, exchange(): return lax.all_to_all(value, axes, split_axis=0, concat_axis=0, tiled=True)  12.7 us
    pallas_call x1, Pallas kernels, finish(): pl.pallas_call(final_kernel, grid=(RING,), out_shape=(jax.ShapeDtypeStruc...  12.3 us
    ppermute x3, starting transfers between devices, shifted(): lax.ppermute(value, 'row', [(i, (i + by) % RING) for i in range(RING)])  12 us
    ppermute x4, starting transfers between devices, per_device(): came.append(lax.ppermute(out[j], ('row', 'col'), perm))  7.78 us
  transfers between devices with their start and end apart: 28, of which 7 were waited for; matrix products, arithmetic and copies ran while one was open for 2% of the time, Pallas kernels for 16%

profile of v2, /device:TPU:1, one launch (start us, length us, event | category | flops | bytes accessed | tf_op | source)
XLA Modules:
  0.0 208.9 jit_solution(17858740473220484606)
XLA Ops:
  7.2 13.4 %all_to_all.15 = f32[8,4,2048]{2,1,0:T(4,128)S(1)} all-to-all(f32[8,4,2048]{2,1,0:T(4,128)} %bitcast.20), channel_id=1, replica_groups=mesh['grp'=2,'row'=4,'col'=16] {'grp','row'}, dimensions={0} | all-to-all | bytes 524288 | tf_op jit(solution)/shard_map/all_to_all | solution.py:322
  26.7 2.3 %collective-permute-done.2 = f32[16,2048]{1,0:T(8,128)S(1)} collective-permute-done((f32[16,2048]{1,0:T(8,128)S(1)}, f32[16,2048]{1,0:T(8,128)S(1)}, u32[]{:S(2)}, u32[]{:S(2)}) %collective-permute-start.2) | collective-permute-done | bytes 131104 | tf_op jit(solution)/shard_map/ppermute | solution.py:333
  29.1 2.7 %collective-permute-start.5 = (f32[8,2048]{1,0:T(8,128)S(1)}, f32[8,2048]{1,0:T(8,128)S(1)}, u32[]{:S(2)}, u32[]{:S(2)}) collective-permute-start(f32[8,2048]{1,0:T(8,128)S(1)} %slice.53), channel_id=1, source_target_pairs={{0,3},{1,0},{2,1},{3,2},{4,7},{5,4},{6,5},{7,6},{8,11},{9,8},{10,9... | collective-permute-start | bytes 196616 | tf_op jit(solution)/shard_map/ppermute | solution.py:333
  36.3 2.7 %collective-permute-start.11 = (f32[64,2048]{1,0:T(8,128)S(1)}, f32[64,2048]{1,0:T(8,128)}, u32[]{:S(2)}, u32[]{:S(2)}) collective-permute-start(f32[64,2048]{1,0:T(8,128)S(1)} %constant_dynamic-update-slice_fusion.5.refs_1_), channel_id=1, source_target_pairs={{0,3},{1,0},{2,1},{3,2},{4,7},{5,4},{6,5},{7,6},{8,11},{9,8},{10,9... | collective-permute-start | bytes 1572872 | tf_op jit(solution)/shard_map/ppermute | solution.py:333
  41.7 2.2 %copy-done = f32[2048,512]{1,0:T(8,128)S(1)} copy-done((f32[2048,512]{1,0:T(8,128)S(1)}, f32[2048,512]{1,0:T(8,128)}, u32[]{:S(2)}) %copy-start) | copy-done | bytes 4194328
  54.8 2.7 %collective-permute-start.13 = (f32[32,2048]{1,0:T(8,128)S(1)}, f32[32,2048]{1,0:T(8,128)S(1)}, u32[]{:S(2)}, u32[]{:S(2)}) collective-permute-start(f32[32,2048]{1,0:T(8,128)S(1)} %slice.57), channel_id=1, source_target_pairs={{0,12},{1,13},{2,14},{3,15},{4,0},{5,1},{6,2},{7,3},{8,4},{9,5},{1... | collective-permute-start | bytes 786440 | tf_op jit(solution)/shard_map/ppermute | solution.py:333
  59.5 2.9 %collective-permute-start.15 = (f32[32,2048]{1,0:T(8,128)S(1)}, f32[32,2048]{1,0:T(8,128)S(1)}, u32[]{:S(2)}, u32[]{:S(2)}) collective-permute-start(f32[32,2048]{1,0:T(8,128)S(1)} %slice.59), channel_id=1, source_target_pairs={{0,3},{1,0},{2,1},{3,2},{4,7},{5,4},{6,5},{7,6},{8,11},{9,8},{10,9... | collective-permute-start | bytes 786440 | tf_op jit(solution)/shard_map/ppermute | solution.py:333
  62.4 4.9 %multiply.3.middle_ref = f32[256,512]{1,0:T(8,128)S(1)} custom-call(f32[64,2048]{1,0:T(8,128)} %collective-permute-done.8.refs_0_.refs_2_, f32[64,2048]{1,0:T(8,128)} %collective-permute-done.9.refs_1_.refs_3_, f32[64,2048]{1,0:T(8,128)} %collective-permute-done.10.refs_2_.refs_4_, f32[64,2048]{1,0:T(8,128)} %collective-permute-done.11.refs_3_.refs_5_, ...), custom_call_target="tpu_custom_call" | custom-call | flops 3221225472 | bytes 8388608 | tf_op jit(solution)/shard_map/multiply/pallas_call | solution.py:157
  67.4 2.4 %multiply_last.1 = f32[4,512,128]{2,1,0:T(8,128)S(1)} custom-call(s32[4]{0:T(128)S(1)} %pad_add_fusion.at_ref, f32[32,2048]{1,0:T(8,128)S(1)} %collective-permute-done.12.c0.refs_6_, f32[32,2048]{1,0:T(8,128)S(1)} %collective-permute-done.13.c1.refs_7_, f32[32,2048]{1,0:T(8,128)S(1)} %collective-permute-done.14.c2.refs_8_, ...), custom_call_target="tpu_custom_call" | custom-call | tf_op jit(solution)/shard_map/multiply_last/pallas_call | solution.py:197
  70.5 3.0 %collective-permute-start.17 = (f32[512,128]{1,0:T(8,128)S(1)}, f32[512,128]{1,0:T(8,128)S(1)}, u32[]{:S(2)}, u32[]{:S(2)}) collective-permute-start(f32[512,128]{1,0:T(8,128)S(1)} %get-tuple-element.54), channel_id=1, source_target_pairs={{0,4},{1,5},{2,6},{3,7},{4,20},{5,21},{6,22},{7,23},{8,36},{9,37},... | collective-permute-start | bytes 786440 | tf_op jit(solution)/shard_map/ppermute | solution.py:381
  75.3 2.3 %collective-permute-start.19 = (f32[512,128]{1,0:T(8,128)S(1)}, f32[512,128]{1,0:T(8,128)S(1)}, u32[]{:S(2)}, u32[]{:S(2)}) collective-permute-start(f32[512,128]{1,0:T(8,128)S(1)} %get-tuple-element.52), channel_id=1, source_target_pairs={{0,12},{1,13},{2,14},{3,15},{4,28},{5,29},{6,30},{7,31},{8,44},{9,... | collective-permute-start | bytes 786440 | tf_op jit(solution)/shard_map/ppermute | solution.py:381
  79.1 5.4 %collective-permute-done.18.r2 = f32[512,128]{1,0:T(8,128)S(1)} collective-permute-done((f32[512,128]{1,0:T(8,128)S(1)}, f32[512,128]{1,0:T(8,128)S(1)}, u32[]{:S(2)}, u32[]{:S(2)}) %collective-permute-start.18) | collective-permute-done | bytes 262176 | tf_op jit(solution)/shard_map/ppermute | solution.py:381
  84.8 2.2 %gram.1 = (f32[512,128]{1,0:T(8,128)S(1)}, f32[128,512]{1,0:T(8,128)}, f32[256,512]{1,0:T(8,128)S(1)}, f32[256,512]{1,0:T(8,128)S(1)}) custom-call(s32[4]{0:T(128)S(1)} %pad_add_fusion.at_ref, f32[512,128]{1,0:T(8,128)S(1)} %collective-permute-done.16.r0, f32[512,128]{1,0:T(8,128)S(1)} %collective-permute-done.17.r1, ...), custom_call_target="tpu_custom_call" | custom-call | tf_op jit(solution)/shard_map/gram/pallas_call | solution.py:254
  87.0 7.4 %collective-permute-start.20 = (f32[256,512]{1,0:T(8,128)S(1)}, f32[256,512]{1,0:T(8,128)S(1)}, u32[]{:S(2)}, u32[]{:S(2)}) collective-permute-start(f32[256,512]{1,0:T(8,128)S(1)} %get-tuple-element.45), channel_id=1, source_target_pairs={{0,64},{64,0},{1,65},{65,1},{2,66},{66,2},{3,67},{67,3},{4,68},{68... | collective-permute-start | bytes 1572872 | tf_op jit(solution)/shard_map/ppermute | solution.py:388
  96.2 25.1 %all_to_all.16 = f32[64,4,512]{2,1,0:T(4,128)S(1)} all-to-all(f32[64,4,512]{2,1,0:T(4,128)S(1)} %reshape.30), channel_id=1, replica_groups=mesh['grp'=2,'row'=4,'col'=16] {'row','col'}, dimensions={0} | all-to-all | bytes 1048576 | tf_op jit(solution)/shard_map/all_to_all | solution.py:322
  122.3 4.6 %all-to-all-start.2 = ((f32[64,4,512]{2,1,0:T(4,128)}), f32[64,4,512]{2,1,0:T(4,128)S(1)}, u32[]{:S(2)}, u32[]{:S(2)}) async-start(f32[64,4,512]{2,1,0:T(4,128)} %broadcast_in_dim.2), calls=%async_computation.2 | async-start | bytes 1048576 | tf_op jit(solution)/shard_map/all_to_all | solution.py:322
  127.6 12.7 %all-to-all-done.2 = f32[64,4,512]{2,1,0:T(4,128)S(1)} async-done(((f32[64,4,512]{2,1,0:T(4,128)}), f32[64,4,512]{2,1,0:T(4,128)S(1)}, u32[]{:S(2)}, u32[]{:S(2)}) %all-to-all-start.2) | async-done | bytes 524320 | tf_op jit(solution)/shard_map/all_to_all | solution.py:322
  140.5 6.4 %collective-permute-start.22 = (f32[256,512]{1,0:T(8,128)S(1)}, f32[256,512]{1,0:T(8,128)S(1)}, u32[]{:S(2)}, u32[]{:S(2)}) collective-permute-start(f32[256,512]{1,0:T(8,128)S(1)} %reshape.31.own_ref), channel_id=1, source_target_pairs={{0,64},{64,0},{1,65},{65,1},{2,66},{66,2},{3,67},{67,3},{4,68},{68... | collective-permute-start | bytes 1572872 | tf_op jit(solution)/shard_map/ppermute | solution.py:395
  147.5 2.7 %collective-permute-start.23 = (f32[512,128]{1,0:T(8,128)S(1)}, f32[512,128]{1,0:T(8,128)S(1)}, u32[]{:S(2)}, u32[]{:S(2)}) collective-permute-start(f32[512,128]{1,0:T(8,128)S(1)} %collective-permute-done.21.p0), channel_id=1, source_target_pairs={{0,16},{16,32},{32,48},{48,0},{1,17},{17,33},{33,49},{49,1},{2,18}... | collective-permute-start | bytes 786440 | tf_op jit(solution)/shard_map/ppermute | solution.py:327
  150.2 9.3 %collective-permute-start.24 = (f32[512,128]{1,0:T(8,128)S(1)}, f32[512,128]{1,0:T(8,128)S(1)}, u32[]{:S(2)}, u32[]{:S(2)}) collective-permute-start(f32[512,128]{1,0:T(8,128)S(1)} %collective-permute-done.21.p0), channel_id=1, source_target_pairs={{0,32},{16,48},{32,0},{48,16},{1,33},{17,49},{33,1},{49,17},{2,34}... | collective-permute-start | bytes 786440 | tf_op jit(solution)/shard_map/ppermute | solution.py:327
  161.4 23.9 %inverse.1.neg_ref = f32[512,512]{1,0:T(8,128)S(1)} custom-call(s32[4]{0:T(128)S(1)} %pad_add_fusion.at_ref, f32[256,512]{1,0:T(8,128)S(1)} %reshape.31.own_ref, f32[256,512]{1,0:T(8,128)S(1)} %copy-done.8, f32[1,512]{1,0:T(1,128)S(1)} %reshape_reshape.6.noise_ref), custom_call_target="tpu_custom_call" | custom-call | flops 20000000000 | bytes 2097152 | tf_op jit(solution)/shard_map/inverse/pallas_call | solution.py:91
  185.4 2.2 %copy-done.1 = f32[2048,512]{1,0:T(8,128)S(1)} copy-done((f32[2048,512]{1,0:T(8,128)S(1)}, f32[2048,512]{1,0:T(8,128)}, u32[]{:S(2)}) %copy-start.1) | copy-done | bytes 4194328
  187.6 2.2 %copy-done.6 = f32[2048,512]{1,0:T(8,128)S(1)} copy-done((f32[2048,512]{1,0:T(8,128)S(1)}, f32[2048,512]{1,0:T(8,128)}, u32[]{:S(2)}) %copy-start.6) | copy-done | bytes 4194328
  189.8 12.3 %finish.1 = (f32[2048,512]{1,0:T(8,128)}, f32[4,1,512]{2,1,0:T(1,128)}) custom-call(s32[4]{0:T(128)S(1)} %pad_add_fusion.at_ref, f32[512,512]{1,0:T(8,128)S(1)} %inverse.1.neg_ref, f32[512,1]{1,0:T(8,128)S(1)} %reshape_reshape.8.innov_ref, f32[512,128]{1,0:T(8,128)S(1)} %collective-permute-done.21.p0, f32[512,128]{1,0:T(8,128)S(1)} %collective-permute-done.23.p1, ...), custom_call_target="tpu_custom_call" | custom-call | tf_op jit(solution)/shard_map/finish/pallas_call | solution.py:291
  (98 shorter events, 36.4 us)
Async XLA Ops:
  7.2 178.2 %all-gather.3.cloned.1.call-start = ((), (), s32[]{:S(2)}) async-start(), calls=%async_computation.3 | async-start | bytes 4456448 | tf_op jit(solution)/shard_map/all_gather | solution.py:384
  20.7 6.0 %collective-permute-start = (f32[16,2048]{1,0:T(8,128)S(1)}, f32[16,2048]{1,0:T(8,128)S(1)}, u32[]{:S(2)}, u32[]{:S(2)}) collective-permute-start(f32[16,2048]{1,0:T(8,128)S(1)} %slice.49), channel_id=1, source_target_pairs={{0,1},{1,2},{2,3},{3,0},{4,5},{5,6},{6,7},{7,4},{8,9},{9,10},{10,1... | collective-permute-start | bytes 393224 | tf_op jit(solution)/shard_map/ppermute | solution.py:333
  23.5 5.5 %collective-permute-start.2 = (f32[16,2048]{1,0:T(8,128)S(1)}, f32[16,2048]{1,0:T(8,128)S(1)}, u32[]{:S(2)}, u32[]{:S(2)}) collective-permute-start(f32[16,2048]{1,0:T(8,128)S(1)} %slice.51), channel_id=1, source_target_pairs={{0,4},{1,5},{2,6},{3,7},{4,8},{5,9},{6,10},{7,11},{8,12},{9,13},{1... | collective-permute-start | bytes 393224 | tf_op jit(solution)/shard_map/ppermute | solution.py:333
  29.0 5.5 %collective-permute-start.4 = (f32[8,2048]{1,0:T(8,128)S(1)}, f32[8,2048]{1,0:T(8,128)S(1)}, u32[]{:S(2)}, u32[]{:S(2)}) collective-permute-start(f32[8,2048]{1,0:T(8,128)S(1)} %slice.52), channel_id=1, source_target_pairs={{0,1},{1,2},{2,3},{3,0},{4,5},{5,6},{6,7},{7,4},{8,9},{9,10},{10,1... | collective-permute-start | bytes 196616 | tf_op jit(solution)/shard_map/ppermute | solution.py:333
  29.1 5.4 %collective-permute-start.5 = (f32[8,2048]{1,0:T(8,128)S(1)}, f32[8,2048]{1,0:T(8,128)S(1)}, u32[]{:S(2)}, u32[]{:S(2)}) collective-permute-start(f32[8,2048]{1,0:T(8,128)S(1)} %slice.53), channel_id=1, source_target_pairs={{0,3},{1,0},{2,1},{3,2},{4,7},{5,4},{6,5},{7,6},{8,11},{9,8},{10,9... | collective-permute-start | bytes 196616 | tf_op jit(solution)/shard_map/ppermute | solution.py:333
  36.3 16.4 %collective-permute-start.10 = (f32[64,2048]{1,0:T(8,128)S(1)}, f32[64,2048]{1,0:T(8,128)}, u32[]{:S(2)}, u32[]{:S(2)}) collective-permute-start(f32[64,2048]{1,0:T(8,128)S(1)} %constant_dynamic-update-slice_fusion.5.refs_1_), channel_id=1, source_target_pairs={{0,1},{1,2},{2,3},{3,0},{4,5},{5,6},{6,7},{7,4},{8,9},{9,10},{10,1... | collective-permute-start | bytes 1572872 | tf_op jit(solution)/shard_map/ppermute | solution.py:333
  36.3 16.3 %collective-permute-start.11 = (f32[64,2048]{1,0:T(8,128)S(1)}, f32[64,2048]{1,0:T(8,128)}, u32[]{:S(2)}, u32[]{:S(2)}) collective-permute-start(f32[64,2048]{1,0:T(8,128)S(1)} %constant_dynamic-update-slice_fusion.5.refs_1_), channel_id=1, source_target_pairs={{0,3},{1,0},{2,1},{3,2},{4,7},{5,4},{6,5},{7,6},{8,11},{9,8},{10,9... | collective-permute-start | bytes 1572872 | tf_op jit(solution)/shard_map/ppermute | solution.py:333
  39.0 13.7 %collective-permute-start.8 = (f32[64,2048]{1,0:T(8,128)S(1)}, f32[64,2048]{1,0:T(8,128)}, u32[]{:S(2)}, u32[]{:S(2)}) collective-permute-start(f32[64,2048]{1,0:T(8,128)S(1)} %constant_dynamic-update-slice_fusion.refs_0_), channel_id=1, source_target_pairs={{0,4},{1,5},{2,6},{3,7},{4,8},{5,9},{6,10},{7,11},{8,12},{9,13},{1... | collective-permute-start | bytes 1572872 | tf_op jit(solution)/shard_map/ppermute | solution.py:333
  40.3 12.4 %collective-permute-start.9 = (f32[64,2048]{1,0:T(8,128)S(1)}, f32[64,2048]{1,0:T(8,128)}, u32[]{:S(2)}, u32[]{:S(2)}) collective-permute-start(f32[64,2048]{1,0:T(8,128)S(1)} %constant_dynamic-update-slice_fusion.refs_0_), channel_id=1, source_target_pairs={{0,12},{1,13},{2,14},{3,15},{4,0},{5,1},{6,2},{7,3},{8,4},{9,5},{1... | collective-permute-start | bytes 1572872 | tf_op jit(solution)/shard_map/ppermute | solution.py:333
  53.7 13.7 %collective-permute-start.12 = (f32[32,2048]{1,0:T(8,128)S(1)}, f32[32,2048]{1,0:T(8,128)S(1)}, u32[]{:S(2)}, u32[]{:S(2)}) collective-permute-start(f32[32,2048]{1,0:T(8,128)S(1)} %slice.56), channel_id=1, source_target_pairs={{0,4},{1,5},{2,6},{3,7},{4,8},{5,9},{6,10},{7,11},{8,12},{9,13},{1... | collective-permute-start | bytes 786440 | tf_op jit(solution)/shard_map/ppermute | solution.py:333
  54.8 12.6 %collective-permute-start.13 = (f32[32,2048]{1,0:T(8,128)S(1)}, f32[32,2048]{1,0:T(8,128)S(1)}, u32[]{:S(2)}, u32[]{:S(2)}) collective-permute-start(f32[32,2048]{1,0:T(8,128)S(1)} %slice.57), channel_id=1, source_target_pairs={{0,12},{1,13},{2,14},{3,15},{4,0},{5,1},{6,2},{7,3},{8,4},{9,5},{1... | collective-permute-start | bytes 786440 | tf_op jit(solution)/shard_map/ppermute | solution.py:333
  58.4 8.9 %collective-permute-start.14 = (f32[32,2048]{1,0:T(8,128)S(1)}, f32[32,2048]{1,0:T(8,128)S(1)}, u32[]{:S(2)}, u32[]{:S(2)}) collective-permute-start(f32[32,2048]{1,0:T(8,128)S(1)} %slice.58), channel_id=1, source_target_pairs={{0,1},{1,2},{2,3},{3,0},{4,5},{5,6},{6,7},{7,4},{8,9},{9,10},{10,1... | collective-permute-start | bytes 786440 | tf_op jit(solution)/shard_map/ppermute | solution.py:333
  59.5 7.9 %collective-permute-start.15 = (f32[32,2048]{1,0:T(8,128)S(1)}, f32[32,2048]{1,0:T(8,128)S(1)}, u32[]{:S(2)}, u32[]{:S(2)}) collective-permute-start(f32[32,2048]{1,0:T(8,128)S(1)} %slice.59), channel_id=1, source_target_pairs={{0,3},{1,0},{2,1},{3,2},{4,7},{5,4},{6,5},{7,6},{8,11},{9,8},{10,9... | collective-permute-start | bytes 786440 | tf_op jit(solution)/shard_map/ppermute | solution.py:333
  69.8 9.2 %collective-permute-start.16 = (f32[512,128]{1,0:T(8,128)S(1)}, f32[512,128]{1,0:T(8,128)S(1)}, u32[]{:S(2)}, u32[]{:S(2)}) collective-permute-start(f32[512,128]{1,0:T(8,128)S(1)} %get-tuple-element.55), channel_id=1, source_target_pairs={{0,0},{1,1},{2,2},{3,3},{4,16},{5,17},{6,18},{7,19},{8,32},{9,33},... | collective-permute-start | bytes 786440 | tf_op jit(solution)/shard_map/ppermute | solution.py:381
  70.5 8.5 %collective-permute-start.17 = (f32[512,128]{1,0:T(8,128)S(1)}, f32[512,128]{1,0:T(8,128)S(1)}, u32[]{:S(2)}, u32[]{:S(2)}) collective-permute-start(f32[512,128]{1,0:T(8,128)S(1)} %get-tuple-element.54), channel_id=1, source_target_pairs={{0,4},{1,5},{2,6},{3,7},{4,20},{5,21},{6,22},{7,23},{8,36},{9,37},... | collective-permute-start | bytes 786440 | tf_op jit(solution)/shard_map/ppermute | solution.py:381
  73.6 10.9 %collective-permute-start.18 = (f32[512,128]{1,0:T(8,128)S(1)}, f32[512,128]{1,0:T(8,128)S(1)}, u32[]{:S(2)}, u32[]{:S(2)}) collective-permute-start(f32[512,128]{1,0:T(8,128)S(1)} %get-tuple-element.53), channel_id=1, source_target_pairs={{0,8},{1,9},{2,10},{3,11},{4,24},{5,25},{6,26},{7,27},{8,40},{9,41... | collective-permute-start | bytes 786440 | tf_op jit(solution)/shard_map/ppermute | solution.py:381
  75.3 9.4 %collective-permute-start.19 = (f32[512,128]{1,0:T(8,128)S(1)}, f32[512,128]{1,0:T(8,128)S(1)}, u32[]{:S(2)}, u32[]{:S(2)}) collective-permute-start(f32[512,128]{1,0:T(8,128)S(1)} %get-tuple-element.52), channel_id=1, source_target_pairs={{0,12},{1,13},{2,14},{3,15},{4,28},{5,29},{6,30},{7,31},{8,44},{9,... | collective-permute-start | bytes 786440 | tf_op jit(solution)/shard_map/ppermute | solution.py:381
  87.0 9.0 %collective-permute-start.20 = (f32[256,512]{1,0:T(8,128)S(1)}, f32[256,512]{1,0:T(8,128)S(1)}, u32[]{:S(2)}, u32[]{:S(2)}) collective-permute-start(f32[256,512]{1,0:T(8,128)S(1)} %get-tuple-element.45), channel_id=1, source_target_pairs={{0,64},{64,0},{1,65},{65,1},{2,66},{66,2},{3,67},{67,3},{4,68},{68... | collective-permute-start | bytes 1572872 | tf_op jit(solution)/shard_map/ppermute | solution.py:388
  122.3 18.1 %all-to-all-start.2 = ((f32[64,4,512]{2,1,0:T(4,128)}), f32[64,4,512]{2,1,0:T(4,128)S(1)}, u32[]{:S(2)}, u32[]{:S(2)}) async-start(f32[64,4,512]{2,1,0:T(4,128)} %broadcast_in_dim.2), calls=%async_computation.2 | async-start | bytes 1048576 | tf_op jit(solution)/shard_map/all_to_all | solution.py:322
  126.9 13.6 %collective-permute-start.21 = (f32[512,128]{1,0:T(8,128)S(1)}, f32[512,128]{1,0:T(8,128)S(1)}, u32[]{:S(2)}, u32[]{:S(2)}) collective-permute-start(f32[512,128]{1,0:T(8,128)S(1)} %get-tuple-element.46), channel_id=1, source_target_pairs={{0,0},{1,1},{2,2},{3,3},{4,16},{5,17},{6,18},{7,19},{8,32},{9,33},... | collective-permute-start | bytes 786440 | tf_op jit(solution)/shard_map/ppermute | solution.py:390
  140.5 19.0 %collective-permute-start.22 = (f32[256,512]{1,0:T(8,128)S(1)}, f32[256,512]{1,0:T(8,128)S(1)}, u32[]{:S(2)}, u32[]{:S(2)}) collective-permute-start(f32[256,512]{1,0:T(8,128)S(1)} %reshape.31.own_ref), channel_id=1, source_target_pairs={{0,64},{64,0},{1,65},{65,1},{2,66},{66,2},{3,67},{67,3},{4,68},{68... | collective-permute-start | bytes 1572872 | tf_op jit(solution)/shard_map/ppermute | solution.py:395
  147.5 37.8 %collective-permute-start.23 = (f32[512,128]{1,0:T(8,128)S(1)}, f32[512,128]{1,0:T(8,128)S(1)}, u32[]{:S(2)}, u32[]{:S(2)}) collective-permute-start(f32[512,128]{1,0:T(8,128)S(1)} %collective-permute-done.21.p0), channel_id=1, source_target_pairs={{0,16},{16,32},{32,48},{48,0},{1,17},{17,33},{33,49},{49,1},{2,18}... | collective-permute-start | bytes 786440 | tf_op jit(solution)/shard_map/ppermute | solution.py:327
  150.2 35.1 %collective-permute-start.24 = (f32[512,128]{1,0:T(8,128)S(1)}, f32[512,128]{1,0:T(8,128)S(1)}, u32[]{:S(2)}, u32[]{:S(2)}) collective-permute-start(f32[512,128]{1,0:T(8,128)S(1)} %collective-permute-done.21.p0), channel_id=1, source_target_pairs={{0,32},{16,48},{32,0},{48,16},{1,33},{17,49},{33,1},{49,17},{2,34}... | collective-permute-start | bytes 786440 | tf_op jit(solution)/shard_map/ppermute | solution.py:327
  159.5 25.8 %collective-permute-start.25 = (f32[512,128]{1,0:T(8,128)S(1)}, f32[512,128]{1,0:T(8,128)S(1)}, u32[]{:S(2)}, u32[]{:S(2)}) collective-permute-start(f32[512,128]{1,0:T(8,128)S(1)} %collective-permute-done.21.p0), channel_id=1, source_target_pairs={{0,48},{16,0},{32,16},{48,32},{1,49},{17,1},{33,17},{49,33},{2,50}... | collective-permute-start | bytes 786440 | tf_op jit(solution)/shard_map/ppermute | solution.py:327
  (15 other events, 166.8 us)
Sparse Core Ops, SparseCore 0:
  87.1 78.1 all-gather.2

commit v3 on v2

--- a/solution.py
+++ b/solution.py
@@ -53,16 +53,21 @@
     return jnp.concatenate(rows, axis=0)
 
 
-def inverse_kernel(at_ref, own_ref, other_ref, noise_ref, out_ref):
+def inverse_kernel(at_ref, own_ref, other_ref, noise_ref, innov_ref, out_ref, u_ref):
     m = out_ref.shape[0]
     half = m // 2
     n = m // B
     g = at_ref[0]
-    for source, start in ((own_ref, g * half), (other_ref, (1 - g) * half)):
-        row_id = lax.broadcasted_iota(jnp.int32, (half, m), 0) + start
-        col_id = lax.broadcasted_iota(jnp.int32, (half, m), 1)
-        value = source[...] + jnp.where(row_id == col_id, noise_ref[...], 0.0)
-        out_ref[pl.ds(pl.multiple_of(start, half), half), :] = value
+
+    def system():
+        for source, start in ((own_ref, g * half), (other_ref, (1 - g) * half)):
+            row_id = lax.broadcasted_iota(jnp.int32, (half, m), 0) + start
+            col_id = lax.broadcasted_iota(jnp.int32, (half, m), 1)
+            at = pl.ds(pl.multiple_of(start, half), half)
+            yield at, row_id == col_id, source[...] + jnp.where(row_id == col_id, noise_ref[...], 0.0)
+
+    for at, _, value in system():
+        out_ref[at, :] = value
 
     def step(k, carry):
         at = pl.ds(pl.multiple_of(k * B, B), B)
@@ -80,23 +85,37 @@
 
     lax.fori_loop(0, n, step, 0)
 
+    def solve(row):
+        total = jnp.zeros((1, m), jnp.float32)
+        for at, diagonal, _ in system():
+            column = jnp.sum(jnp.where(diagonal, row, 0.0), axis=1, keepdims=True)
+            total = total - jnp.sum(out_ref[at, :] * column, axis=0, keepdims=True)
+        return total
+
+    first = solve(innov_ref[...])
+    rest = innov_ref[...]
+    for _, diagonal, value in system():
+        column = jnp.sum(jnp.where(diagonal, first, 0.0), axis=1, keepdims=True)
+        rest = rest - jnp.sum(value * column, axis=0, keepdims=True)
+    u_ref[...] = first + solve(rest)
+
 
 VMEM = pl.BlockSpec(memory_space=pltpu.VMEM)
 SMEM = pl.BlockSpec(memory_space=pltpu.SMEM)
-PARAMS = pltpu.CompilerParams(vmem_limit_bytes=40 * 2**20)
-
-
-def negative_inverse(at, own, other, noise):
+PARAMS = pltpu.CompilerParams(vmem_limit_bytes=20 * 2**20)
+
+
+def negative_inverse(at, own, other, noise, innovation):
     m = noise.shape[1]
     return pl.pallas_call(
         inverse_kernel,
-        out_shape=jax.ShapeDtypeStruct((m, m), jnp.float32),
-        in_specs=[SMEM, VMEM, VMEM, VMEM],
-        out_specs=VMEM,
-        compiler_params=PARAMS,
+        out_shape=(jax.ShapeDtypeStruct((m, m), jnp.float32), jax.ShapeDtypeStruct((1, m), jnp.float32)),
+        in_specs=[SMEM] + [VMEM] * 4,
+        out_specs=(VMEM, VMEM),
+        compiler_params=pltpu.CompilerParams(vmem_limit_bytes=16 * 2**20),
         cost_estimate=pl.CostEstimate(flops=20 * 10**9, bytes_accessed=2 * 2**20, transcendentals=0),
         name="inverse",
-    )(at, own, other, noise)
+    )(at, own, other, noise, innovation)
 
 
 def split(a):
@@ -261,61 +280,82 @@
     )(at, *came, jac)
 
 
-def final_kernel(at_ref, neg_ref, innov_ref, p0, p1, p2, p3, rows_ref, cov_ref, new_ref, delta_ref, yh, yl, u):
-    @pl.when(pl.program_id(0) == 0)
-    def _():
-        neg = neg_ref[...]
-        for j, piece in enumerate((p0, p1, p2, p3)):
-            place = lax.rem(at_ref[1] + (RING - j), RING)
-            at = pl.ds(pl.multiple_of(place * B, B), B)
-            yh[:, at], yl[:, at] = split(dot6(neg, piece[...]))
-        u[...] = jnp.broadcast_to(-jnp.sum(neg * innov_ref[...], axis=0, keepdims=True), u.shape)
-
-    for b in range(RING):
-        at = slice(b * B, b * B + B)
-        rows = rows_ref[b, 0]
+def final_kernel(
+    at_ref, neg_ref, u_ref, p0, p1, p2, p3, rows_hbm, cov_hbm, new_hbm, delta_ref, cols, yh, yl, rows_ref, cov_ref, new_ref, sems
+):
+    count = cov_ref.shape[0]
+    size = cov_ref.shape[1]
+    block = lambda i: pl.ds(i * size, size)
+    get_rows = [pltpu.make_async_copy(rows_hbm.at[:, i], rows_ref.at[i], sems.at[0, i]) for i in range(count)]
+    get_cov = [pltpu.make_async_copy(cov_hbm.at[block(i)], cov_ref.at[i], sems.at[1, i]) for i in range(count)]
+    put_new = [pltpu.make_async_copy(new_ref.at[i], new_hbm.at[block(i)], sems.at[2, i]) for i in range(count)]
+    for i in range(count):
+        get_rows[i].start()
+        get_cov[i].start()
+    for j, piece in enumerate((p0, p1, p2, p3)):
+        place = lax.rem(at_ref[1] + (RING - j), RING)
+        cols[:, pl.ds(pl.multiple_of(place * B, B), B)] = piece[...]
+    yh[...], yl[...] = split(dot6(neg_ref[...], cols[...]))
+    for i in range(count):
+        get_rows[i].wait()
+        rows = rows_ref[i].reshape(size, cols.shape[0])
         high, low = split(rows)
         change = mul(high, yh[...]) + (mul(high, yl[...]) + mul(low, yh[...]))
-        new_ref[at, :] = (cov_ref[at, :] + change) * (1 / 0.98)
-        delta = lax.dot_general(
-            u[...], rows, (((1,), (1,)), ((), ())), precision=HI, preferred_element_type=jnp.float32
-        )
-        delta_ref[0, :, at] = delta[0:1, :]
-
-
-def finish(at, neg, innovation, pieces, prod_rows, covariance):
+        get_cov[i].wait()
+        new_ref[i] = (cov_ref[i] + change) * (1 / 0.98)
+        put_new[i].start()
+        scaled = rows * u_ref[...]
+        lanes = sum(scaled[:, k:k + B] for k in range(0, rows.shape[1], B))
+        for b in range(0, size, B):
+            delta_ref[:, i * size + b:i * size + b + B] = jnp.sum(lanes[b:b + B, :].T, axis=0, keepdims=True)
+    for i in range(count):
+        put_new[i].wait()
+
+
+def finish(at, neg, u, pieces, prod_rows, covariance):
     m = neg.shape[0]
     rows_dev, cols_dev = covariance.shape
     rows = rows_dev // RING
-    whole = lambda *shape: pl.BlockSpec(shape, lambda i: (0,) * len(shape))
+    hbm = pl.BlockSpec(memory_space=pltpu.HBM)
     new, delta = pl.pallas_call(
         final_kernel,
-        grid=(RING,),
         out_shape=(
             jax.ShapeDtypeStruct((rows_dev, cols_dev), jnp.float32),
-            jax.ShapeDtypeStruct((RING, 1, rows), jnp.float32),
+            jax.ShapeDtypeStruct((1, rows_dev), jnp.float32),
         ),
-        in_specs=[
-            SMEM,
-            whole(m, m),
-            whole(m, 1),
-            *[whole(m, B)] * 4,
-            pl.BlockSpec((RING, 1, B, m), lambda i: (0, i, 0, 0)),
-            pl.BlockSpec((rows, cols_dev), lambda i: (i, 0)),
-        ],
-        out_specs=(
-            pl.BlockSpec((rows, cols_dev), lambda i: (i, 0)),
-            pl.BlockSpec((1, 1, rows), lambda i: (i, 0, 0)),
-        ),
+        in_specs=[SMEM] + [VMEM] * 6 + [hbm, hbm],
+        out_specs=(hbm, VMEM),
         scratch_shapes=[
+            pltpu.VMEM((m, cols_dev), jnp.float32),
             pltpu.VMEM((m, cols_dev), jnp.bfloat16),
             pltpu.VMEM((m, cols_dev), jnp.bfloat16),
-            pltpu.VMEM((8, m), jnp.float32),
+            pltpu.VMEM((RING, RING, B, m), jnp.float32),
+            pltpu.VMEM((RING, rows, cols_dev), jnp.float32),
+            pltpu.VMEM((RING, rows, cols_dev), jnp.float32),
+            pltpu.SemaphoreType.DMA((3, RING)),
         ],
-        compiler_params=PARAMS,
+        compiler_params=pltpu.CompilerParams(vmem_limit_bytes=50 * 2**20),
         name="finish",
-    )(at, neg, innovation, *pieces, prod_rows.reshape(RING, RING, B, m), covariance)
+    )(at, neg, u, *pieces, prod_rows.reshape(RING, RING, B, m), covariance)
     return delta.reshape(rows_dev), new
+
+
+def halve_kernel(n0, n1, n2, n3, f0, f1, f2, f3):
+    h = f0.shape[0]
+    for near, far, start in ((n0, f0, 0), (n1, f1, h), (n2, f2, 0), (n3, f3, h)):
+        far[...] = near[start:start + h, :]
+
+
+def halves(near):
+    rows, cols = near[0].shape
+    return pl.pallas_call(
+        halve_kernel,
+        out_shape=(jax.ShapeDtypeStruct((rows // 2, cols), jnp.float32),) * 4,
+        in_specs=[VMEM] * 4,
+        out_specs=(VMEM,) * 4,
+        compiler_params=PARAMS,
+        name="halves",
+    )(*near)
 
 
 def exchange(value, axes):
@@ -339,13 +379,8 @@
 
 def both_ways(first, second, axes):
     near = tie(*[shifted(v, axis, by) for v, axis in zip((first, second), axes) for by in (1, -1)])
-    h = first.shape[0] // 2
-    far = [
-        shifted(near[0][:h], axes[0], 1),
-        shifted(near[1][h:], axes[0], -1),
-        shifted(near[2][:h], axes[1], 1),
-        shifted(near[3][h:], axes[1], -1),
-    ]
+    part = halves(near)
+    far = [shifted(part[i], axes[i // 2], (1, -1)[i % 2]) for i in range(4)]
     return near, far
 
 
@@ -381,7 +416,6 @@
         came.append(lax.ppermute(out[j], ("row", "col"), perm))
     jac = pick(at, [a4, b4, *near, *far])
     piece, turned, own, other = gram(at, came, jac)
-    prod_rows = lax.all_gather(turned, "col", axis=0)
 
     swap = [(0, 1), (1, 0)]
     h = m // 2
@@ -389,13 +423,14 @@
     perm = [(number(a, b, x), number(b, a, x)) for a, b, x in spots]
     home = lax.ppermute(piece, ("row", "col"), perm)
     summed = exchange(own.reshape(64, h // 64, m), ("row", "col"))
-    share = jnp.sum(summed, axis=0, keepdims=True)
+    share, turned = tie(jnp.sum(summed, axis=0, keepdims=True), turned)
+    prod_rows = lax.all_gather(turned, "col", axis=0)
     own = exchange(jnp.broadcast_to(share, (64, h // 64, m)), ("row", "col")).reshape(h, m)
     own, home = tie(own, home)
     other = lax.ppermute(own, "grp", swap)
     pieces = [home] + [shifted(home, "row", d) for d in (1, 2, 3)]
-    neg = negative_inverse(at, own, other, noise.reshape(1, m))
-    return finish(at, neg, innovation.reshape(m, 1), pieces, prod_rows, covariance)
+    neg, u = negative_inverse(at, own, other, noise.reshape(1, m), innovation.reshape(1, m))
+    return finish(at, neg, u, pieces, prod_rows, covariance)
 
 
 def solution(mesh):

time: 210 us -> 194 us (0.924)
  local copies, waits for them, and re-layouts: 20.1 us -> 11.8 us
  blocking collectives: 38.5 us -> 34.7 us
    unnamed x29, local copies, waits for them, and re-layouts: 14.3 us -> 9.95 us
    slice x8 -> x0, local copies, waits for them, and re-layouts: 3.9 us -> none  [the longest x2 0.98 us: both_ways(): near[0][:h]]
    all_to_all x2, blocking collectives: 38.5 us -> 34.7 us  [exchange(): return lax.all_to_all(value, axes, split_axis=0, concat_axis=0, tiled=True)]
    pallas_call x2 -> x4, Pallas kernels: 36.2 us -> 35.8 us  [the longest x1 24.6 us: negative_inverse(): pl.pallas_call(inverse_kernel, out_shape=(jax.ShapeDtypeStruct((m, m), jn...]
  transfers between devices with their start and end apart: 28 -> 28, of which waited for: 7 -> 7; matrix products, arithmetic and copies ran while one was open for 2% -> 1% of each run, Pallas kernels for 16% -> 17%
where the time goes in v3:
time: 194 us
  starting transfers between devices  60 us (31%)
  Pallas kernels  49.6 us (26%)
  blocking collectives  34.7 us (18%)
  waiting for transfers between devices  22.8 us (12%)
  between operations  14.4 us (7%)
  local copies, waits for them, and re-layouts  11.8 us (6%)
    all_to_all x2, blocking collectives, exchange(): return lax.all_to_all(value, axes, split_axis=0, concat_axis=0, tiled=True)  34.7 us
    pallas_call x1, Pallas kernels, negative_inverse(): pl.pallas_call(inverse_kernel, out_shape=(jax.ShapeDtypeStruct((m, m), jn...  24.6 us
    ppermute x16, starting transfers between devices, shifted(): return lax.ppermute(value, 'col', perm)  21.9 us
    ppermute x3, starting transfers between devices, shifted(): lax.ppermute(value, 'row', [(i, (i + by) % RING) for i in range(RING)])  12.4 us
    all_to_all x1, waiting for transfers between devices, exchange(): return lax.all_to_all(value, axes, split_axis=0, concat_axis=0, tiled=True)  11.2 us
    unnamed x29, local copies, waits for them, and re-layouts  9.95 us
    pallas_call x1, Pallas kernels, finish(): pl.pallas_call(final_kernel, out_shape=(jax.ShapeDtypeStruct((rows_dev, c...  9.55 us
    ppermute x4, starting transfers between devices, per_device(): came.append(lax.ppermute(out[j], ('row', 'col'), perm))  7.76 us
  transfers between devices with their start and end apart: 28, of which 7 were waited for; matrix products, arithmetic and copies ran while one was open for 1% of the time, Pallas kernels for 17%

profile of v3, /device:TPU:1, one launch (start us, length us, event | category | flops | bytes accessed | tf_op | source)
XLA Modules:
  0.0 193.6 jit_solution(12133902257083042727)
XLA Ops:
  7.2 13.4 %all_to_all.15 = f32[8,4,2048]{2,1,0:T(4,128)S(1)} all-to-all(f32[8,4,2048]{2,1,0:T(4,128)} %bitcast.22), channel_id=1, replica_groups=mesh['grp'=2,'row'=4,'col'=16] {'grp','row'}, dimensions={0} | all-to-all | bytes 524288 | tf_op jit(solution)/shard_map/all_to_all | solution.py:362
  26.7 2.3 %collective-permute-done.2.n2 = f32[16,2048]{1,0:T(8,128)S(1)} collective-permute-done((f32[16,2048]{1,0:T(8,128)S(1)}, f32[16,2048]{1,0:T(8,128)S(1)}, u32[]{:S(2)}, u32[]{:S(2)}) %collective-permute-start.2) | collective-permute-done | bytes 131104 | tf_op jit(solution)/shard_map/ppermute | solution.py:373
  29.1 2.7 %collective-permute-start.5 = (f32[8,2048]{1,0:T(8,128)S(1)}, f32[8,2048]{1,0:T(8,128)S(1)}, u32[]{:S(2)}, u32[]{:S(2)}) collective-permute-start(f32[8,2048]{1,0:T(8,128)S(1)} %get-tuple-element.44), channel_id=1, source_target_pairs={{0,3},{1,0},{2,1},{3,2},{4,7},{5,4},{6,5},{7,6},{8,11},{9,8},{10,9... | collective-permute-start | bytes 196616 | tf_op jit(solution)/shard_map/ppermute | solution.py:373
  36.3 2.7 %collective-permute-start.11 = (f32[64,2048]{1,0:T(8,128)S(1)}, f32[64,2048]{1,0:T(8,128)}, u32[]{:S(2)}, u32[]{:S(2)}) collective-permute-start(f32[64,2048]{1,0:T(8,128)S(1)} %constant_dynamic-update-slice_fusion.5.refs_1_), channel_id=1, source_target_pairs={{0,3},{1,0},{2,1},{3,2},{4,7},{5,4},{6,5},{7,6},{8,11},{9,8},{10,9... | collective-permute-start | bytes 1572872 | tf_op jit(solution)/shard_map/ppermute | solution.py:373
  41.7 2.2 %copy-done = f32[2048,512]{1,0:T(8,128)S(1)} copy-done((f32[2048,512]{1,0:T(8,128)S(1)}, f32[2048,512]{1,0:T(8,128)}, u32[]{:S(2)}) %copy-start) | copy-done | bytes 4194328
  50.8 1.8 multiply.2.early_ref
  54.4 2.6 %collective-permute-start.13 = (f32[32,2048]{1,0:T(8,128)S(1)}, f32[32,2048]{1,0:T(8,128)S(1)}, u32[]{:S(2)}, u32[]{:S(2)}) collective-permute-start(f32[32,2048]{1,0:T(8,128)S(1)} %get-tuple-element.58), channel_id=1, source_target_pairs={{0,12},{1,13},{2,14},{3,15},{4,0},{5,1},{6,2},{7,3},{8,4},{9,5},{1... | collective-permute-start | bytes 786440 | tf_op jit(solution)/shard_map/ppermute | solution.py:373
  57.0 2.7 %collective-permute-start.15 = (f32[32,2048]{1,0:T(8,128)S(1)}, f32[32,2048]{1,0:T(8,128)S(1)}, u32[]{:S(2)}, u32[]{:S(2)}) collective-permute-start(f32[32,2048]{1,0:T(8,128)S(1)} %get-tuple-element.60), channel_id=1, source_target_pairs={{0,3},{1,0},{2,1},{3,2},{4,7},{5,4},{6,5},{7,6},{8,11},{9,8},{10,9... | collective-permute-start | bytes 786440 | tf_op jit(solution)/shard_map/ppermute | solution.py:373
  59.7 5.0 %multiply.3.middle_ref = f32[256,512]{1,0:T(8,128)S(1)} custom-call(f32[64,2048]{1,0:T(8,128)} %collective-permute-done.8.n0.refs_0_.refs_2_, f32[64,2048]{1,0:T(8,128)} %collective-permute-done.9.n1.refs_1_.refs_3_, f32[64,2048]{1,0:T(8,128)} %collective-permute-done.10.n2.refs_2_.refs_4_, f32[64,2048]{1,0:T(8,128)} %collective-permute-done.11.n3.refs_3_.refs_5_, ...), custom_call_target="tpu_custom_call" | custom-call | flops 3221225472 | bytes 8388608 | tf_op jit(solution)/shard_map/multiply/pallas_call | solution.py:176
  64.7 2.4 %multiply_last.1 = f32[4,512,128]{2,1,0:T(8,128)S(1)} custom-call(s32[4]{0:T(128)S(1)} %pad_add_fusion.at_ref, f32[32,2048]{1,0:T(8,128)S(1)} %collective-permute-done.12.c0.refs_6_, f32[32,2048]{1,0:T(8,128)S(1)} %collective-permute-done.13.c1.refs_7_, f32[32,2048]{1,0:T(8,128)S(1)} %collective-permute-done.14.c2.refs_8_, ...), custom_call_target="tpu_custom_call" | custom-call | tf_op jit(solution)/shard_map/multiply_last/pallas_call | solution.py:216
  67.9 3.0 %collective-permute-start.17 = (f32[512,128]{1,0:T(8,128)S(1)}, f32[512,128]{1,0:T(8,128)S(1)}, u32[]{:S(2)}, u32[]{:S(2)}) collective-permute-start(f32[512,128]{1,0:T(8,128)S(1)} %get-tuple-element.78), channel_id=1, source_target_pairs={{0,4},{1,5},{2,6},{3,7},{4,20},{5,21},{6,22},{7,23},{8,36},{9,37},... | collective-permute-start | bytes 786440 | tf_op jit(solution)/shard_map/ppermute | solution.py:416
  70.9 1.7 collective-permute-start.18
  72.7 2.3 %collective-permute-start.19 = (f32[512,128]{1,0:T(8,128)S(1)}, f32[512,128]{1,0:T(8,128)S(1)}, u32[]{:S(2)}, u32[]{:S(2)}) collective-permute-start(f32[512,128]{1,0:T(8,128)S(1)} %get-tuple-element.76), channel_id=1, source_target_pairs={{0,12},{1,13},{2,14},{3,15},{4,28},{5,29},{6,30},{7,31},{8,44},{9,... | collective-permute-start | bytes 786440 | tf_op jit(solution)/shard_map/ppermute | solution.py:416
  76.4 5.4 %collective-permute-done.18.r2 = f32[512,128]{1,0:T(8,128)S(1)} collective-permute-done((f32[512,128]{1,0:T(8,128)S(1)}, f32[512,128]{1,0:T(8,128)S(1)}, u32[]{:S(2)}, u32[]{:S(2)}) %collective-permute-start.18) | collective-permute-done | bytes 262176 | tf_op jit(solution)/shard_map/ppermute | solution.py:416
  82.1 2.2 %gram.1 = (f32[512,128]{1,0:T(8,128)S(1)}, f32[128,512]{1,0:T(8,128)}, f32[256,512]{1,0:T(8,128)S(1)}, f32[256,512]{1,0:T(8,128)S(1)}) custom-call(s32[4]{0:T(128)S(1)} %pad_add_fusion.at_ref, f32[512,128]{1,0:T(8,128)S(1)} %collective-permute-done.16.r0, f32[512,128]{1,0:T(8,128)S(1)} %collective-permute-done.17.r1, ...), custom_call_target="tpu_custom_call" | custom-call | tf_op jit(solution)/shard_map/gram/pallas_call | solution.py:273
  84.3 7.4 %collective-permute-start.20 = (f32[256,512]{1,0:T(8,128)S(1)}, f32[256,512]{1,0:T(8,128)S(1)}, u32[]{:S(2)}, u32[]{:S(2)}) collective-permute-start(f32[256,512]{1,0:T(8,128)S(1)} %get-tuple-element.65), channel_id=1, source_target_pairs={{0,64},{64,0},{1,65},{65,1},{2,66},{66,2},{3,67},{67,3},{4,68},{68... | collective-permute-start | bytes 1572872 | tf_op jit(solution)/shard_map/ppermute | solution.py:422
  93.4 21.3 %all_to_all.16 = f32[64,4,512]{2,1,0:T(4,128)S(1)} all-to-all(f32[64,4,512]{2,1,0:T(4,128)S(1)} %reshape.29), channel_id=1, replica_groups=mesh['grp'=2,'row'=4,'col'=16] {'row','col'}, dimensions={0} | all-to-all | bytes 1048576 | tf_op jit(solution)/shard_map/all_to_all | solution.py:362
  115.7 4.6 %all-to-all-start.2 = ((f32[64,4,512]{2,1,0:T(4,128)}), f32[64,4,512]{2,1,0:T(4,128)S(1)}, u32[]{:S(2)}, u32[]{:S(2)}) async-start(f32[64,4,512]{2,1,0:T(4,128)} %broadcast_in_dim.12), calls=%async_computation.2 | async-start | bytes 1048576 | tf_op jit(solution)/shard_map/all_to_all | solution.py:362
  121.1 11.2 %all-to-all-done.2 = f32[64,4,512]{2,1,0:T(4,128)S(1)} async-done(((f32[64,4,512]{2,1,0:T(4,128)}), f32[64,4,512]{2,1,0:T(4,128)S(1)}, u32[]{:S(2)}, u32[]{:S(2)}) %all-to-all-start.2) | async-done | bytes 524320 | tf_op jit(solution)/shard_map/all_to_all | solution.py:362
  132.5 5.2 %collective-permute-start.22 = (f32[256,512]{1,0:T(8,128)S(1)}, f32[256,512]{1,0:T(8,128)S(1)}, u32[]{:S(2)}, u32[]{:S(2)}) collective-permute-start(f32[256,512]{1,0:T(8,128)S(1)} %reshape.30.own_ref), channel_id=1, source_target_pairs={{0,64},{64,0},{1,65},{65,1},{2,66},{66,2},{3,67},{67,3},{4,68},{68... | collective-permute-start | bytes 1572872 | tf_op jit(solution)/shard_map/ppermute | solution.py:430
  138.3 5.4 %collective-permute-start.23 = (f32[512,128]{1,0:T(8,128)S(1)}, f32[512,128]{1,0:T(8,128)S(1)}, u32[]{:S(2)}, u32[]{:S(2)}) collective-permute-start(f32[512,128]{1,0:T(8,128)S(1)} %collective-permute-done.21.p0), channel_id=1, source_target_pairs={{0,16},{16,32},{32,48},{48,0},{1,17},{17,33},{33,49},{49,1},{2,18}... | collective-permute-start | bytes 786440 | tf_op jit(solution)/shard_map/ppermute | solution.py:367
  143.6 7.0 %collective-permute-start.24 = (f32[512,128]{1,0:T(8,128)S(1)}, f32[512,128]{1,0:T(8,128)S(1)}, u32[]{:S(2)}, u32[]{:S(2)}) collective-permute-start(f32[512,128]{1,0:T(8,128)S(1)} %collective-permute-done.21.p0), channel_id=1, source_target_pairs={{0,32},{16,48},{32,0},{48,16},{1,33},{17,49},{33,1},{49,17},{2,34}... | collective-permute-start | bytes 786440 | tf_op jit(solution)/shard_map/ppermute | solution.py:367
  152.5 24.6 %inverse.1 = (f32[512,512]{1,0:T(8,128)S(1)}, f32[1,512]{1,0:T(1,128)S(1)}) custom-call(s32[4]{0:T(128)S(1)} %pad_add_fusion.at_ref, f32[256,512]{1,0:T(8,128)S(1)} %reshape.30.own_ref, f32[256,512]{1,0:T(8,128)S(1)} %copy-done.8, f32[1,512]{1,0:T(1,128)S(1)} %reshape_reshape.6.noise_ref, f32[1,512]{1,0:T(1,128)S(1)} %reshape_reshape.7.innov_ref), custom_call_target="tpu_custom_call" | custom-call | flops 20000000000 | bytes 2097152 | tf_op jit(solution)/shard_map/inverse/pallas_call | solution.py:110
  177.2 9.5 %finish.1 = (f32[2048,512]{1,0:T(8,128)}, f32[1,2048]{1,0:T(1,128)}) custom-call(s32[4]{0:T(128)S(1)} %pad_add_fusion.at_ref, f32[512,512]{1,0:T(8,128)S(1)} %get-tuple-element.70.neg_ref, f32[1,512]{1,0:T(1,128)S(1)} %get-tuple-element.71.u_ref, f32[512,128]{1,0:T(8,128)S(1)} %collective-permute-done.21.p0, f32[512,128]{1,0:T(8,128)S(1)} %collective-permute-done.23.p1, ...), custom_call_target="tpu_custom_call" | custom-call | tf_op jit(solution)/shard_map/finish/pallas_call | solution.py:320
  (92 shorter events, 30.5 us)
Async XLA Ops:
  7.2 170.0 %all-gather.3.cloned.1.call-start = ((), (), s32[]{:S(2)}) async-start(), calls=%async_computation.3 | async-start | bytes 4456448 | tf_op jit(solution)/shard_map/all_gather | solution.py:427
  20.7 6.0 %collective-permute-start = (f32[16,2048]{1,0:T(8,128)S(1)}, f32[16,2048]{1,0:T(8,128)S(1)}, u32[]{:S(2)}, u32[]{:S(2)}) collective-permute-start(f32[16,2048]{1,0:T(8,128)S(1)} %slice.25), channel_id=1, source_target_pairs={{0,1},{1,2},{2,3},{3,0},{4,5},{5,6},{6,7},{7,4},{8,9},{9,10},{10,1... | collective-permute-start | bytes 393224 | tf_op jit(solution)/shard_map/ppermute | solution.py:373
  23.5 5.5 %collective-permute-start.2 = (f32[16,2048]{1,0:T(8,128)S(1)}, f32[16,2048]{1,0:T(8,128)S(1)}, u32[]{:S(2)}, u32[]{:S(2)}) collective-permute-start(f32[16,2048]{1,0:T(8,128)S(1)} %slice.27), channel_id=1, source_target_pairs={{0,4},{1,5},{2,6},{3,7},{4,8},{5,9},{6,10},{7,11},{8,12},{9,13},{1... | collective-permute-start | bytes 393224 | tf_op jit(solution)/shard_map/ppermute | solution.py:373
  29.0 5.5 %collective-permute-start.4 = (f32[8,2048]{1,0:T(8,128)S(1)}, f32[8,2048]{1,0:T(8,128)S(1)}, u32[]{:S(2)}, u32[]{:S(2)}) collective-permute-start(f32[8,2048]{1,0:T(8,128)S(1)} %get-tuple-element.43), channel_id=1, source_target_pairs={{0,1},{1,2},{2,3},{3,0},{4,5},{5,6},{6,7},{7,4},{8,9},{9,10},{10,1... | collective-permute-start | bytes 196616 | tf_op jit(solution)/shard_map/ppermute | solution.py:373
  29.1 5.4 %collective-permute-start.5 = (f32[8,2048]{1,0:T(8,128)S(1)}, f32[8,2048]{1,0:T(8,128)S(1)}, u32[]{:S(2)}, u32[]{:S(2)}) collective-permute-start(f32[8,2048]{1,0:T(8,128)S(1)} %get-tuple-element.44), channel_id=1, source_target_pairs={{0,3},{1,0},{2,1},{3,2},{4,7},{5,4},{6,5},{7,6},{8,11},{9,8},{10,9... | collective-permute-start | bytes 196616 | tf_op jit(solution)/shard_map/ppermute | solution.py:373
  36.2 16.4 %collective-permute-start.10 = (f32[64,2048]{1,0:T(8,128)S(1)}, f32[64,2048]{1,0:T(8,128)}, u32[]{:S(2)}, u32[]{:S(2)}) collective-permute-start(f32[64,2048]{1,0:T(8,128)S(1)} %constant_dynamic-update-slice_fusion.5.refs_1_), channel_id=1, source_target_pairs={{0,1},{1,2},{2,3},{3,0},{4,5},{5,6},{6,7},{7,4},{8,9},{9,10},{10,1... | collective-permute-start | bytes 1572872 | tf_op jit(solution)/shard_map/ppermute | solution.py:373
  36.3 16.3 %collective-permute-start.11 = (f32[64,2048]{1,0:T(8,128)S(1)}, f32[64,2048]{1,0:T(8,128)}, u32[]{:S(2)}, u32[]{:S(2)}) collective-permute-start(f32[64,2048]{1,0:T(8,128)S(1)} %constant_dynamic-update-slice_fusion.5.refs_1_), channel_id=1, source_target_pairs={{0,3},{1,0},{2,1},{3,2},{4,7},{5,4},{6,5},{7,6},{8,11},{9,8},{10,9... | collective-permute-start | bytes 1572872 | tf_op jit(solution)/shard_map/ppermute | solution.py:373
  39.0 13.7 %collective-permute-start.8 = (f32[64,2048]{1,0:T(8,128)S(1)}, f32[64,2048]{1,0:T(8,128)}, u32[]{:S(2)}, u32[]{:S(2)}) collective-permute-start(f32[64,2048]{1,0:T(8,128)S(1)} %constant_dynamic-update-slice_fusion.refs_0_), channel_id=1, source_target_pairs={{0,4},{1,5},{2,6},{3,7},{4,8},{5,9},{6,10},{7,11},{8,12},{9,13},{1... | collective-permute-start | bytes 1572872 | tf_op jit(solution)/shard_map/ppermute | solution.py:373
  40.2 12.4 %collective-permute-start.9 = (f32[64,2048]{1,0:T(8,128)S(1)}, f32[64,2048]{1,0:T(8,128)}, u32[]{:S(2)}, u32[]{:S(2)}) collective-permute-start(f32[64,2048]{1,0:T(8,128)S(1)} %constant_dynamic-update-slice_fusion.refs_0_), channel_id=1, source_target_pairs={{0,12},{1,13},{2,14},{3,15},{4,0},{5,1},{6,2},{7,3},{8,4},{9,5},{1... | collective-permute-start | bytes 1572872 | tf_op jit(solution)/shard_map/ppermute | solution.py:373
  54.3 10.4 %collective-permute-start.12 = (f32[32,2048]{1,0:T(8,128)S(1)}, f32[32,2048]{1,0:T(8,128)S(1)}, u32[]{:S(2)}, u32[]{:S(2)}) collective-permute-start(f32[32,2048]{1,0:T(8,128)S(1)} %get-tuple-element.57), channel_id=1, source_target_pairs={{0,4},{1,5},{2,6},{3,7},{4,8},{5,9},{6,10},{7,11},{8,12},{9,13},{1... | collective-permute-start | bytes 786440 | tf_op jit(solution)/shard_map/ppermute | solution.py:373
  54.4 10.3 %collective-permute-start.13 = (f32[32,2048]{1,0:T(8,128)S(1)}, f32[32,2048]{1,0:T(8,128)S(1)}, u32[]{:S(2)}, u32[]{:S(2)}) collective-permute-start(f32[32,2048]{1,0:T(8,128)S(1)} %get-tuple-element.58), channel_id=1, source_target_pairs={{0,12},{1,13},{2,14},{3,15},{4,0},{5,1},{6,2},{7,3},{8,4},{9,5},{1... | collective-permute-start | bytes 786440 | tf_op jit(solution)/shard_map/ppermute | solution.py:373
  57.0 7.7 %collective-permute-start.14 = (f32[32,2048]{1,0:T(8,128)S(1)}, f32[32,2048]{1,0:T(8,128)S(1)}, u32[]{:S(2)}, u32[]{:S(2)}) collective-permute-start(f32[32,2048]{1,0:T(8,128)S(1)} %get-tuple-element.59), channel_id=1, source_target_pairs={{0,1},{1,2},{2,3},{3,0},{4,5},{5,6},{6,7},{7,4},{8,9},{9,10},{10,1... | collective-permute-start | bytes 786440 | tf_op jit(solution)/shard_map/ppermute | solution.py:373
  57.0 7.7 %collective-permute-start.15 = (f32[32,2048]{1,0:T(8,128)S(1)}, f32[32,2048]{1,0:T(8,128)S(1)}, u32[]{:S(2)}, u32[]{:S(2)}) collective-permute-start(f32[32,2048]{1,0:T(8,128)S(1)} %get-tuple-element.60), channel_id=1, source_target_pairs={{0,3},{1,0},{2,1},{3,2},{4,7},{5,4},{6,5},{7,6},{8,11},{9,8},{10,9... | collective-permute-start | bytes 786440 | tf_op jit(solution)/shard_map/ppermute | solution.py:373
  67.2 9.2 %collective-permute-start.16 = (f32[512,128]{1,0:T(8,128)S(1)}, f32[512,128]{1,0:T(8,128)S(1)}, u32[]{:S(2)}, u32[]{:S(2)}) collective-permute-start(f32[512,128]{1,0:T(8,128)S(1)} %get-tuple-element.79), channel_id=1, source_target_pairs={{0,0},{1,1},{2,2},{3,3},{4,16},{5,17},{6,18},{7,19},{8,32},{9,33},... | collective-permute-start | bytes 786440 | tf_op jit(solution)/shard_map/ppermute | solution.py:416
  67.9 8.5 %collective-permute-start.17 = (f32[512,128]{1,0:T(8,128)S(1)}, f32[512,128]{1,0:T(8,128)S(1)}, u32[]{:S(2)}, u32[]{:S(2)}) collective-permute-start(f32[512,128]{1,0:T(8,128)S(1)} %get-tuple-element.78), channel_id=1, source_target_pairs={{0,4},{1,5},{2,6},{3,7},{4,20},{5,21},{6,22},{7,23},{8,36},{9,37},... | collective-permute-start | bytes 786440 | tf_op jit(solution)/shard_map/ppermute | solution.py:416
  70.9 10.9 %collective-permute-start.18 = (f32[512,128]{1,0:T(8,128)S(1)}, f32[512,128]{1,0:T(8,128)S(1)}, u32[]{:S(2)}, u32[]{:S(2)}) collective-permute-start(f32[512,128]{1,0:T(8,128)S(1)} %get-tuple-element.77), channel_id=1, source_target_pairs={{0,8},{1,9},{2,10},{3,11},{4,24},{5,25},{6,26},{7,27},{8,40},{9,41... | collective-permute-start | bytes 786440 | tf_op jit(solution)/shard_map/ppermute | solution.py:416
  72.7 9.4 %collective-permute-start.19 = (f32[512,128]{1,0:T(8,128)S(1)}, f32[512,128]{1,0:T(8,128)S(1)}, u32[]{:S(2)}, u32[]{:S(2)}) collective-permute-start(f32[512,128]{1,0:T(8,128)S(1)} %get-tuple-element.76), channel_id=1, source_target_pairs={{0,12},{1,13},{2,14},{3,15},{4,28},{5,29},{6,30},{7,31},{8,44},{9,... | collective-permute-start | bytes 786440 | tf_op jit(solution)/shard_map/ppermute | solution.py:416
  84.3 8.9 %collective-permute-start.20 = (f32[256,512]{1,0:T(8,128)S(1)}, f32[256,512]{1,0:T(8,128)S(1)}, u32[]{:S(2)}, u32[]{:S(2)}) collective-permute-start(f32[256,512]{1,0:T(8,128)S(1)} %get-tuple-element.65), channel_id=1, source_target_pairs={{0,64},{64,0},{1,65},{65,1},{2,66},{66,2},{3,67},{67,3},{4,68},{68... | collective-permute-start | bytes 1572872 | tf_op jit(solution)/shard_map/ppermute | solution.py:422
  115.7 16.6 %all-to-all-start.2 = ((f32[64,4,512]{2,1,0:T(4,128)}), f32[64,4,512]{2,1,0:T(4,128)S(1)}, u32[]{:S(2)}, u32[]{:S(2)}) async-start(f32[64,4,512]{2,1,0:T(4,128)} %broadcast_in_dim.12), calls=%async_computation.2 | async-start | bytes 1048576 | tf_op jit(solution)/shard_map/all_to_all | solution.py:362
  120.4 12.1 %collective-permute-start.21 = (f32[512,128]{1,0:T(8,128)S(1)}, f32[512,128]{1,0:T(8,128)S(1)}, u32[]{:S(2)}, u32[]{:S(2)}) collective-permute-start(f32[512,128]{1,0:T(8,128)S(1)} %get-tuple-element.68), channel_id=1, source_target_pairs={{0,0},{1,1},{2,2},{3,3},{4,16},{5,17},{6,18},{7,19},{8,32},{9,33},... | collective-permute-start | bytes 786440 | tf_op jit(solution)/shard_map/ppermute | solution.py:424
  132.5 18.2 %collective-permute-start.22 = (f32[256,512]{1,0:T(8,128)S(1)}, f32[256,512]{1,0:T(8,128)S(1)}, u32[]{:S(2)}, u32[]{:S(2)}) collective-permute-start(f32[256,512]{1,0:T(8,128)S(1)} %reshape.30.own_ref), channel_id=1, source_target_pairs={{0,64},{64,0},{1,65},{65,1},{2,66},{66,2},{3,67},{67,3},{4,68},{68... | collective-permute-start | bytes 1572872 | tf_op jit(solution)/shard_map/ppermute | solution.py:430
  138.3 38.9 %collective-permute-start.23 = (f32[512,128]{1,0:T(8,128)S(1)}, f32[512,128]{1,0:T(8,128)S(1)}, u32[]{:S(2)}, u32[]{:S(2)}) collective-permute-start(f32[512,128]{1,0:T(8,128)S(1)} %collective-permute-done.21.p0), channel_id=1, source_target_pairs={{0,16},{16,32},{32,48},{48,0},{1,17},{17,33},{33,49},{49,1},{2,18}... | collective-permute-start | bytes 786440 | tf_op jit(solution)/shard_map/ppermute | solution.py:367
  143.6 33.5 %collective-permute-start.24 = (f32[512,128]{1,0:T(8,128)S(1)}, f32[512,128]{1,0:T(8,128)S(1)}, u32[]{:S(2)}, u32[]{:S(2)}) collective-permute-start(f32[512,128]{1,0:T(8,128)S(1)} %collective-permute-done.21.p0), channel_id=1, source_target_pairs={{0,32},{16,48},{32,0},{48,16},{1,33},{17,49},{33,1},{49,17},{2,34}... | collective-permute-start | bytes 786440 | tf_op jit(solution)/shard_map/ppermute | solution.py:367
  150.7 26.5 %collective-permute-start.25 = (f32[512,128]{1,0:T(8,128)S(1)}, f32[512,128]{1,0:T(8,128)S(1)}, u32[]{:S(2)}, u32[]{:S(2)}) collective-permute-start(f32[512,128]{1,0:T(8,128)S(1)} %collective-permute-done.21.p0), channel_id=1, source_target_pairs={{0,48},{16,0},{32,16},{48,32},{1,49},{17,1},{33,17},{49,33},{2,50}... | collective-permute-start | bytes 786440 | tf_op jit(solution)/shard_map/ppermute | solution.py:367
  (15 other events, 167.0 us)
Sparse Core Ops, SparseCore 0:
  115.0 56.1 all-gather.2

commit v4 on v3

--- a/solution.py
+++ b/solution.py
@@ -27,7 +27,9 @@
         r = rows[p]
         cols = [jnp.broadcast_to(r[:, Q * p + j:Q * p + j + 1], (Q, B)) for j in range(Q)]
         for k in range(Q):
-            inv = 1.0 / jnp.broadcast_to(cols[k][k:k + 1, :], (Q, B))
+            pivot = jnp.broadcast_to(cols[k][k:k + 1, :], (Q, B))
+            inv = pl.reciprocal(pivot, approx=True)
+            inv = inv * (2.0 - pivot * inv)
             scaled = cols[k] * inv
             new = []
             for j in range(Q):
@@ -53,51 +55,55 @@
     return jnp.concatenate(rows, axis=0)
 
 
-def inverse_kernel(at_ref, own_ref, other_ref, noise_ref, innov_ref, out_ref, u_ref):
+def sweep_all(out_ref, diag_ref, left_ref, turn_ref):
+    m = out_ref.shape[0]
+    n = m // B
+    place = lambda k: pl.ds(pl.multiple_of(k * B, B), B)
+    diag_ref[...] = out_ref[:B, :B]
+    left_ref[...] = jnp.zeros_like(left_ref)
+    turn_ref[...] = jnp.zeros_like(turn_ref)
+
+    def update(k):
+        last = place(jnp.maximum(k - 1, 0))
+        lane = lax.broadcasted_iota(jnp.int32, (m, m), 1)
+        inside = (lane >= (k - 1) * B) & (lane < k * B)
+        out_ref[...] = jnp.where(inside, 0.0, out_ref[...]) - dot6(left_ref[...], turn_ref[...])
+        out_ref[last, :] = jnp.where(k > 0, turn_ref[...], out_ref[last, :])
+
+    def step(k, carry):
+        neg = sweep_block(diag_ref[...])
+        update(k)
+        at, after = place(k), place(jnp.minimum(k + 1, n - 1))
+        lane = lax.broadcasted_iota(jnp.int32, (B, m), 1)
+        here = (lane >= k * B) & (lane < k * B + B)
+        turn_ref[...] = jnp.where(here, jnp.concatenate([neg] * n, axis=1), -dot6(neg, out_ref[at, :]))
+        left_ref[...] = out_ref[:, at]
+        diag_ref[...] = out_ref[after, after] - dot6(left_ref[after, :], turn_ref[:, after])
+        return carry
+
+    lax.fori_loop(0, n, step, 0)
+    update(n)
+
+
+def inverse_kernel(at_ref, own_ref, other_ref, noise_ref, innov_ref, out_ref, u_ref, s_ref, *scratch):
     m = out_ref.shape[0]
     half = m // 2
-    n = m // B
     g = at_ref[0]
-
-    def system():
-        for source, start in ((own_ref, g * half), (other_ref, (1 - g) * half)):
-            row_id = lax.broadcasted_iota(jnp.int32, (half, m), 0) + start
-            col_id = lax.broadcasted_iota(jnp.int32, (half, m), 1)
-            at = pl.ds(pl.multiple_of(start, half), half)
-            yield at, row_id == col_id, source[...] + jnp.where(row_id == col_id, noise_ref[...], 0.0)
-
-    for at, _, value in system():
-        out_ref[at, :] = value
-
-    def step(k, carry):
-        at = pl.ds(pl.multiple_of(k * B, B), B)
-        neg = sweep_block(out_ref[at, at])
-        strip = out_ref[at, :]
-        left = out_ref[:, at]
-        col = lax.broadcasted_iota(jnp.int32, (B, m), 1)
-        here = (col >= k * B) & (col < k * B + B)
-        t = jnp.where(here, jnp.concatenate([neg] * n, axis=1), -dot6(neg, strip))
-        big = lax.broadcasted_iota(jnp.int32, (m, m), 1)
-        keep = jnp.where((big >= k * B) & (big < k * B + B), 0.0, out_ref[...])
-        out_ref[...] = keep - dot6(left, t)
-        out_ref[at, :] = t
-        return carry
-
-    lax.fori_loop(0, n, step, 0)
-
-    def solve(row):
-        total = jnp.zeros((1, m), jnp.float32)
-        for at, diagonal, _ in system():
-            column = jnp.sum(jnp.where(diagonal, row, 0.0), axis=1, keepdims=True)
-            total = total - jnp.sum(out_ref[at, :] * column, axis=0, keepdims=True)
-        return total
-
-    first = solve(innov_ref[...])
-    rest = innov_ref[...]
-    for _, diagonal, value in system():
-        column = jnp.sum(jnp.where(diagonal, first, 0.0), axis=1, keepdims=True)
-        rest = rest - jnp.sum(value * column, axis=0, keepdims=True)
-    u_ref[...] = first + solve(rest)
+    s_ref[pl.ds(pl.multiple_of(g * half, half), half), :] = own_ref[...]
+    s_ref[pl.ds(pl.multiple_of((1 - g) * half, half), half), :] = other_ref[...]
+    diagonal = lax.broadcasted_iota(jnp.int32, (m, m), 0) == lax.broadcasted_iota(jnp.int32, (m, m), 1)
+    s_ref[...] = s_ref[...] + jnp.where(diagonal, noise_ref[...], 0.0)
+    out_ref[...] = s_ref[...]
+    sweep_all(out_ref, *scratch)
+
+    def apply(matrix_ref, row):
+        column = jnp.broadcast_to(row, (B, m)).T
+        parts = [jnp.sum(matrix_ref[:, i:i + B] * column, axis=0, keepdims=True) for i in range(0, m, B)]
+        return jnp.concatenate(parts, axis=1)
+
+    first = -apply(out_ref, innov_ref[...])
+    rest = innov_ref[...] - apply(s_ref, first)
+    u_ref[...] = first - apply(out_ref, rest)
 
 
 VMEM = pl.BlockSpec(memory_space=pltpu.VMEM)
@@ -112,8 +118,9 @@
         out_shape=(jax.ShapeDtypeStruct((m, m), jnp.float32), jax.ShapeDtypeStruct((1, m), jnp.float32)),
         in_specs=[SMEM] + [VMEM] * 4,
         out_specs=(VMEM, VMEM),
+        scratch_shapes=[pltpu.VMEM(s, jnp.float32) for s in ((m, m), (B, B), (m, B), (B, m))],
         compiler_params=pltpu.CompilerParams(vmem_limit_bytes=16 * 2**20),
-        cost_estimate=pl.CostEstimate(flops=20 * 10**9, bytes_accessed=2 * 2**20, transcendentals=0),
+        cost_estimate=pl.CostEstimate(flops=25 * 10**9, bytes_accessed=2 * 2**20, transcendentals=0),
         name="inverse",
     )(at, own, other, noise, innovation)
 
@@ -341,18 +348,19 @@
 
 
 def halve_kernel(n0, n1, n2, n3, f0, f1, f2, f3):
-    h = f0.shape[0]
-    for near, far, start in ((n0, f0, 0), (n1, f1, h), (n2, f2, 0), (n3, f3, h)):
-        far[...] = near[start:start + h, :]
+    for near, far in ((n0, f0), (n1, f1), (n2, f2), (n3, f3)):
+        far[...] = near[...]
 
 
 def halves(near):
     rows, cols = near[0].shape
+    block = lambda which: pl.BlockSpec((rows // 2, cols), lambda i: (which, 0))
     return pl.pallas_call(
         halve_kernel,
+        grid=(1,),
         out_shape=(jax.ShapeDtypeStruct((rows // 2, cols), jnp.float32),) * 4,
-        in_specs=[VMEM] * 4,
-        out_specs=(VMEM,) * 4,
+        in_specs=[block(0), block(1), block(0), block(1)],
+        out_specs=(block(0),) * 4,
         compiler_params=PARAMS,
         name="halves",
     )(*near)

time: 194 us -> 191 us (0.985)
  Pallas kernels: 49.6 us -> 45.9 us
    pallas_call x1, Pallas kernels: 24.6 us -> 21.3 us  [negative_inverse(): pl.pallas_call(inverse_kernel, out_shape=(jax.ShapeDtypeStruct((m, m), jn...]
  transfers between devices with their start and end apart: 28 -> 28, of which waited for: 7 -> 7; matrix products, arithmetic and copies ran while one was open for 1% -> 1% of each run, Pallas kernels for 17% -> 16%
where the time goes in v4:
time: 191 us; the launch traced here: 190 us
  starting transfers between devices  60 us (31%)
  Pallas kernels  45.9 us (24%)
  blocking collectives  34.7 us (18%)
  waiting for transfers between devices  22.8 us (12%)
  between operations  14.4 us (8%)
  local copies, waits for them, and re-layouts  11.8 us (6%)
    all_to_all x2, blocking collectives, exchange(): return lax.all_to_all(value, axes, split_axis=0, concat_axis=0, tiled=True)  34.7 us
    ppermute x16, starting transfers between devices, shifted(): return lax.ppermute(value, 'col', perm)  21.9 us
    pallas_call x1, Pallas kernels, negative_inverse(): pl.pallas_call(inverse_kernel, out_shape=(jax.ShapeDtypeStruct((m, m), jn...  21.3 us
    ppermute x3, starting transfers between devices, shifted(): lax.ppermute(value, 'row', [(i, (i + by) % RING) for i in range(RING)])  12.4 us
    all_to_all x1, waiting for transfers between devices, exchange(): return lax.all_to_all(value, axes, split_axis=0, concat_axis=0, tiled=True)  11.2 us
    unnamed x29, local copies, waits for them, and re-layouts  9.95 us
    pallas_call x1, Pallas kernels, finish(): pl.pallas_call(final_kernel, out_shape=(jax.ShapeDtypeStruct((rows_dev, c...  9.54 us
    ppermute x4, starting transfers between devices, per_device(): came.append(lax.ppermute(out[j], ('row', 'col'), perm))  7.77 us
  transfers between devices with their start and end apart: 28, of which 7 were waited for; matrix products, arithmetic and copies ran while one was open for 1% of the time, Pallas kernels for 16%

profile of v4, /device:TPU:1, one launch (start us, length us, event | category | flops | bytes accessed | tf_op | source)
XLA Modules:
  0.0 189.9 jit_solution(250168970404107142)
XLA Ops:
  7.2 13.4 %all_to_all.15 = f32[8,4,2048]{2,1,0:T(4,128)S(1)} all-to-all(f32[8,4,2048]{2,1,0:T(4,128)} %bitcast.22), channel_id=1, replica_groups=mesh['grp'=2,'row'=4,'col'=16] {'grp','row'}, dimensions={0} | all-to-all | bytes 524288 | tf_op jit(solution)/shard_map/all_to_all | solution.py:370
  26.7 2.3 %collective-permute-done.2.n2 = f32[16,2048]{1,0:T(8,128)S(1)} collective-permute-done((f32[16,2048]{1,0:T(8,128)S(1)}, f32[16,2048]{1,0:T(8,128)S(1)}, u32[]{:S(2)}, u32[]{:S(2)}) %collective-permute-start.2) | collective-permute-done | bytes 131104 | tf_op jit(solution)/shard_map/ppermute | solution.py:381
  29.1 2.7 %collective-permute-start.5 = (f32[8,2048]{1,0:T(8,128)S(1)}, f32[8,2048]{1,0:T(8,128)S(1)}, u32[]{:S(2)}, u32[]{:S(2)}) collective-permute-start(f32[8,2048]{1,0:T(8,128)S(1)} %get-tuple-element.44), channel_id=1, source_target_pairs={{0,3},{1,0},{2,1},{3,2},{4,7},{5,4},{6,5},{7,6},{8,11},{9,8},{10,9... | collective-permute-start | bytes 196616 | tf_op jit(solution)/shard_map/ppermute | solution.py:381
  36.3 2.7 %collective-permute-start.11 = (f32[64,2048]{1,0:T(8,128)S(1)}, f32[64,2048]{1,0:T(8,128)}, u32[]{:S(2)}, u32[]{:S(2)}) collective-permute-start(f32[64,2048]{1,0:T(8,128)S(1)} %constant_dynamic-update-slice_fusion.5.refs_1_), channel_id=1, source_target_pairs={{0,3},{1,0},{2,1},{3,2},{4,7},{5,4},{6,5},{7,6},{8,11},{9,8},{10,9... | collective-permute-start | bytes 1572872 | tf_op jit(solution)/shard_map/ppermute | solution.py:381
  41.7 2.2 %copy-done = f32[2048,512]{1,0:T(8,128)S(1)} copy-done((f32[2048,512]{1,0:T(8,128)S(1)}, f32[2048,512]{1,0:T(8,128)}, u32[]{:S(2)}) %copy-start) | copy-done | bytes 4194328
  50.8 1.8 multiply.2.early_ref
  54.0 2.6 %collective-permute-start.13 = (f32[32,2048]{1,0:T(8,128)S(1)}, f32[32,2048]{1,0:T(8,128)S(1)}, u32[]{:S(2)}, u32[]{:S(2)}) collective-permute-start(f32[32,2048]{1,0:T(8,128)S(1)} %get-tuple-element.58), channel_id=1, source_target_pairs={{0,12},{1,13},{2,14},{3,15},{4,0},{5,1},{6,2},{7,3},{8,4},{9,5},{1... | collective-permute-start | bytes 786440 | tf_op jit(solution)/shard_map/ppermute | solution.py:381
  56.7 2.7 %collective-permute-start.15 = (f32[32,2048]{1,0:T(8,128)S(1)}, f32[32,2048]{1,0:T(8,128)S(1)}, u32[]{:S(2)}, u32[]{:S(2)}) collective-permute-start(f32[32,2048]{1,0:T(8,128)S(1)} %get-tuple-element.60), channel_id=1, source_target_pairs={{0,3},{1,0},{2,1},{3,2},{4,7},{5,4},{6,5},{7,6},{8,11},{9,8},{10,9... | collective-permute-start | bytes 786440 | tf_op jit(solution)/shard_map/ppermute | solution.py:381
  59.4 5.0 %multiply.3.middle_ref = f32[256,512]{1,0:T(8,128)S(1)} custom-call(f32[64,2048]{1,0:T(8,128)} %collective-permute-done.8.n0.refs_0_.refs_2_, f32[64,2048]{1,0:T(8,128)} %collective-permute-done.9.n1.refs_1_.refs_3_, f32[64,2048]{1,0:T(8,128)} %collective-permute-done.10.n2.refs_2_.refs_4_, f32[64,2048]{1,0:T(8,128)} %collective-permute-done.11.n3.refs_3_.refs_5_, ...), custom_call_target="tpu_custom_call" | custom-call | flops 3221225472 | bytes 8388608 | tf_op jit(solution)/shard_map/multiply/pallas_call | solution.py:183
  64.4 2.4 %multiply_last.1 = f32[4,512,128]{2,1,0:T(8,128)S(1)} custom-call(s32[4]{0:T(128)S(1)} %pad_add_fusion.at_ref, f32[32,2048]{1,0:T(8,128)S(1)} %collective-permute-done.12.c0.refs_6_, f32[32,2048]{1,0:T(8,128)S(1)} %collective-permute-done.13.c1.refs_7_, f32[32,2048]{1,0:T(8,128)S(1)} %collective-permute-done.14.c2.refs_8_, ...), custom_call_target="tpu_custom_call" | custom-call | tf_op jit(solution)/shard_map/multiply_last/pallas_call | solution.py:223
  67.6 3.0 %collective-permute-start.17 = (f32[512,128]{1,0:T(8,128)S(1)}, f32[512,128]{1,0:T(8,128)S(1)}, u32[]{:S(2)}, u32[]{:S(2)}) collective-permute-start(f32[512,128]{1,0:T(8,128)S(1)} %get-tuple-element.78), channel_id=1, source_target_pairs={{0,4},{1,5},{2,6},{3,7},{4,20},{5,21},{6,22},{7,23},{8,36},{9,37},... | collective-permute-start | bytes 786440 | tf_op jit(solution)/shard_map/ppermute | solution.py:424
  70.6 1.7 collective-permute-start.18
  72.3 2.3 %collective-permute-start.19 = (f32[512,128]{1,0:T(8,128)S(1)}, f32[512,128]{1,0:T(8,128)S(1)}, u32[]{:S(2)}, u32[]{:S(2)}) collective-permute-start(f32[512,128]{1,0:T(8,128)S(1)} %get-tuple-element.76), channel_id=1, source_target_pairs={{0,12},{1,13},{2,14},{3,15},{4,28},{5,29},{6,30},{7,31},{8,44},{9,... | collective-permute-start | bytes 786440 | tf_op jit(solution)/shard_map/ppermute | solution.py:424
  76.1 5.4 %collective-permute-done.18.r2 = f32[512,128]{1,0:T(8,128)S(1)} collective-permute-done((f32[512,128]{1,0:T(8,128)S(1)}, f32[512,128]{1,0:T(8,128)S(1)}, u32[]{:S(2)}, u32[]{:S(2)}) %collective-permute-start.18) | collective-permute-done | bytes 262176 | tf_op jit(solution)/shard_map/ppermute | solution.py:424
  81.7 2.2 %gram.1 = (f32[512,128]{1,0:T(8,128)S(1)}, f32[128,512]{1,0:T(8,128)}, f32[256,512]{1,0:T(8,128)S(1)}, f32[256,512]{1,0:T(8,128)S(1)}) custom-call(s32[4]{0:T(128)S(1)} %pad_add_fusion.at_ref, f32[512,128]{1,0:T(8,128)S(1)} %collective-permute-done.16.r0, f32[512,128]{1,0:T(8,128)S(1)} %collective-permute-done.17.r1, ...), custom_call_target="tpu_custom_call" | custom-call | tf_op jit(solution)/shard_map/gram/pallas_call | solution.py:280
  83.9 7.4 %collective-permute-start.20 = (f32[256,512]{1,0:T(8,128)S(1)}, f32[256,512]{1,0:T(8,128)S(1)}, u32[]{:S(2)}, u32[]{:S(2)}) collective-permute-start(f32[256,512]{1,0:T(8,128)S(1)} %get-tuple-element.65), channel_id=1, source_target_pairs={{0,64},{64,0},{1,65},{65,1},{2,66},{66,2},{3,67},{67,3},{4,68},{68... | collective-permute-start | bytes 1572872 | tf_op jit(solution)/shard_map/ppermute | solution.py:430
  93.1 21.3 %all_to_all.16 = f32[64,4,512]{2,1,0:T(4,128)S(1)} all-to-all(f32[64,4,512]{2,1,0:T(4,128)S(1)} %reshape.29), channel_id=1, replica_groups=mesh['grp'=2,'row'=4,'col'=16] {'row','col'}, dimensions={0} | all-to-all | bytes 1048576 | tf_op jit(solution)/shard_map/all_to_all | solution.py:370
  115.4 4.6 %all-to-all-start.2 = ((f32[64,4,512]{2,1,0:T(4,128)}), f32[64,4,512]{2,1,0:T(4,128)S(1)}, u32[]{:S(2)}, u32[]{:S(2)}) async-start(f32[64,4,512]{2,1,0:T(4,128)} %broadcast_in_dim.12), calls=%async_computation.2 | async-start | bytes 1048576 | tf_op jit(solution)/shard_map/all_to_all | solution.py:370
  120.7 11.2 %all-to-all-done.2 = f32[64,4,512]{2,1,0:T(4,128)S(1)} async-done(((f32[64,4,512]{2,1,0:T(4,128)}), f32[64,4,512]{2,1,0:T(4,128)S(1)}, u32[]{:S(2)}, u32[]{:S(2)}) %all-to-all-start.2) | async-done | bytes 524320 | tf_op jit(solution)/shard_map/all_to_all | solution.py:370
  132.2 5.2 %collective-permute-start.22 = (f32[256,512]{1,0:T(8,128)S(1)}, f32[256,512]{1,0:T(8,128)S(1)}, u32[]{:S(2)}, u32[]{:S(2)}) collective-permute-start(f32[256,512]{1,0:T(8,128)S(1)} %reshape.30.own_ref), channel_id=1, source_target_pairs={{0,64},{64,0},{1,65},{65,1},{2,66},{66,2},{3,67},{67,3},{4,68},{68... | collective-permute-start | bytes 1572872 | tf_op jit(solution)/shard_map/ppermute | solution.py:438
  137.9 5.4 %collective-permute-start.23 = (f32[512,128]{1,0:T(8,128)S(1)}, f32[512,128]{1,0:T(8,128)S(1)}, u32[]{:S(2)}, u32[]{:S(2)}) collective-permute-start(f32[512,128]{1,0:T(8,128)S(1)} %collective-permute-done.21.p0), channel_id=1, source_target_pairs={{0,16},{16,32},{32,48},{48,0},{1,17},{17,33},{33,49},{49,1},{2,18}... | collective-permute-start | bytes 786440 | tf_op jit(solution)/shard_map/ppermute | solution.py:375
  143.3 7.0 %collective-permute-start.24 = (f32[512,128]{1,0:T(8,128)S(1)}, f32[512,128]{1,0:T(8,128)S(1)}, u32[]{:S(2)}, u32[]{:S(2)}) collective-permute-start(f32[512,128]{1,0:T(8,128)S(1)} %collective-permute-done.21.p0), channel_id=1, source_target_pairs={{0,32},{16,48},{32,0},{48,16},{1,33},{17,49},{33,1},{49,17},{2,34}... | collective-permute-start | bytes 786440 | tf_op jit(solution)/shard_map/ppermute | solution.py:375
  152.2 21.3 %inverse.1 = (f32[512,512]{1,0:T(8,128)S(1)}, f32[1,512]{1,0:T(1,128)S(1)}) custom-call(s32[4]{0:T(128)S(1)} %pad_add_fusion.at_ref, f32[256,512]{1,0:T(8,128)S(1)} %reshape.30.own_ref, f32[256,512]{1,0:T(8,128)S(1)} %copy-done.8, f32[1,512]{1,0:T(1,128)S(1)} %reshape_reshape.6.noise_ref, f32[1,512]{1,0:T(1,128)S(1)} %reshape_reshape.7.innov_ref), custom_call_target="tpu_custom_call" | custom-call | flops 24999999488 | bytes 2097152 | tf_op jit(solution)/shard_map/inverse/pallas_call | solution.py:116
  173.5 9.5 %finish.1 = (f32[2048,512]{1,0:T(8,128)}, f32[1,2048]{1,0:T(1,128)}) custom-call(s32[4]{0:T(128)S(1)} %pad_add_fusion.at_ref, f32[512,512]{1,0:T(8,128)S(1)} %get-tuple-element.70.neg_ref, f32[1,512]{1,0:T(1,128)S(1)} %get-tuple-element.71.u_ref, f32[512,128]{1,0:T(8,128)S(1)} %collective-permute-done.21.p0, f32[512,128]{1,0:T(8,128)S(1)} %collective-permute-done.23.p1, ...), custom_call_target="tpu_custom_call" | custom-call | tf_op jit(solution)/shard_map/finish/pallas_call | solution.py:327
  (92 shorter events, 30.1 us)
Async XLA Ops:
  7.2 166.3 %all-gather.3.cloned.1.call-start = ((), (), s32[]{:S(2)}) async-start(), calls=%async_computation.3 | async-start | bytes 4456448 | tf_op jit(solution)/shard_map/all_gather | solution.py:435
  20.7 6.0 %collective-permute-start = (f32[16,2048]{1,0:T(8,128)S(1)}, f32[16,2048]{1,0:T(8,128)S(1)}, u32[]{:S(2)}, u32[]{:S(2)}) collective-permute-start(f32[16,2048]{1,0:T(8,128)S(1)} %slice.25), channel_id=1, source_target_pairs={{0,1},{1,2},{2,3},{3,0},{4,5},{5,6},{6,7},{7,4},{8,9},{9,10},{10,1... | collective-permute-start | bytes 393224 | tf_op jit(solution)/shard_map/ppermute | solution.py:381
  23.5 5.5 %collective-permute-start.2 = (f32[16,2048]{1,0:T(8,128)S(1)}, f32[16,2048]{1,0:T(8,128)S(1)}, u32[]{:S(2)}, u32[]{:S(2)}) collective-permute-start(f32[16,2048]{1,0:T(8,128)S(1)} %slice.27), channel_id=1, source_target_pairs={{0,4},{1,5},{2,6},{3,7},{4,8},{5,9},{6,10},{7,11},{8,12},{9,13},{1... | collective-permute-start | bytes 393224 | tf_op jit(solution)/shard_map/ppermute | solution.py:381
  29.0 5.5 %collective-permute-start.4 = (f32[8,2048]{1,0:T(8,128)S(1)}, f32[8,2048]{1,0:T(8,128)S(1)}, u32[]{:S(2)}, u32[]{:S(2)}) collective-permute-start(f32[8,2048]{1,0:T(8,128)S(1)} %get-tuple-element.43), channel_id=1, source_target_pairs={{0,1},{1,2},{2,3},{3,0},{4,5},{5,6},{6,7},{7,4},{8,9},{9,10},{10,1... | collective-permute-start | bytes 196616 | tf_op jit(solution)/shard_map/ppermute | solution.py:381
  29.1 5.4 %collective-permute-start.5 = (f32[8,2048]{1,0:T(8,128)S(1)}, f32[8,2048]{1,0:T(8,128)S(1)}, u32[]{:S(2)}, u32[]{:S(2)}) collective-permute-start(f32[8,2048]{1,0:T(8,128)S(1)} %get-tuple-element.44), channel_id=1, source_target_pairs={{0,3},{1,0},{2,1},{3,2},{4,7},{5,4},{6,5},{7,6},{8,11},{9,8},{10,9... | collective-permute-start | bytes 196616 | tf_op jit(solution)/shard_map/ppermute | solution.py:381
  36.2 16.4 %collective-permute-start.10 = (f32[64,2048]{1,0:T(8,128)S(1)}, f32[64,2048]{1,0:T(8,128)}, u32[]{:S(2)}, u32[]{:S(2)}) collective-permute-start(f32[64,2048]{1,0:T(8,128)S(1)} %constant_dynamic-update-slice_fusion.5.refs_1_), channel_id=1, source_target_pairs={{0,1},{1,2},{2,3},{3,0},{4,5},{5,6},{6,7},{7,4},{8,9},{9,10},{10,1... | collective-permute-start | bytes 1572872 | tf_op jit(solution)/shard_map/ppermute | solution.py:381
  36.3 16.3 %collective-permute-start.11 = (f32[64,2048]{1,0:T(8,128)S(1)}, f32[64,2048]{1,0:T(8,128)}, u32[]{:S(2)}, u32[]{:S(2)}) collective-permute-start(f32[64,2048]{1,0:T(8,128)S(1)} %constant_dynamic-update-slice_fusion.5.refs_1_), channel_id=1, source_target_pairs={{0,3},{1,0},{2,1},{3,2},{4,7},{5,4},{6,5},{7,6},{8,11},{9,8},{10,9... | collective-permute-start | bytes 1572872 | tf_op jit(solution)/shard_map/ppermute | solution.py:381
  39.0 13.7 %collective-permute-start.8 = (f32[64,2048]{1,0:T(8,128)S(1)}, f32[64,2048]{1,0:T(8,128)}, u32[]{:S(2)}, u32[]{:S(2)}) collective-permute-start(f32[64,2048]{1,0:T(8,128)S(1)} %constant_dynamic-update-slice_fusion.refs_0_), channel_id=1, source_target_pairs={{0,4},{1,5},{2,6},{3,7},{4,8},{5,9},{6,10},{7,11},{8,12},{9,13},{1... | collective-permute-start | bytes 1572872 | tf_op jit(solution)/shard_map/ppermute | solution.py:381
  40.2 12.4 %collective-permute-start.9 = (f32[64,2048]{1,0:T(8,128)S(1)}, f32[64,2048]{1,0:T(8,128)}, u32[]{:S(2)}, u32[]{:S(2)}) collective-permute-start(f32[64,2048]{1,0:T(8,128)S(1)} %constant_dynamic-update-slice_fusion.refs_0_), channel_id=1, source_target_pairs={{0,12},{1,13},{2,14},{3,15},{4,0},{5,1},{6,2},{7,3},{8,4},{9,5},{1... | collective-permute-start | bytes 1572872 | tf_op jit(solution)/shard_map/ppermute | solution.py:381
  53.9 10.4 %collective-permute-start.12 = (f32[32,2048]{1,0:T(8,128)S(1)}, f32[32,2048]{1,0:T(8,128)S(1)}, u32[]{:S(2)}, u32[]{:S(2)}) collective-permute-start(f32[32,2048]{1,0:T(8,128)S(1)} %get-tuple-element.57), channel_id=1, source_target_pairs={{0,4},{1,5},{2,6},{3,7},{4,8},{5,9},{6,10},{7,11},{8,12},{9,13},{1... | collective-permute-start | bytes 786440 | tf_op jit(solution)/shard_map/ppermute | solution.py:381
  54.0 10.3 %collective-permute-start.13 = (f32[32,2048]{1,0:T(8,128)S(1)}, f32[32,2048]{1,0:T(8,128)S(1)}, u32[]{:S(2)}, u32[]{:S(2)}) collective-permute-start(f32[32,2048]{1,0:T(8,128)S(1)} %get-tuple-element.58), channel_id=1, source_target_pairs={{0,12},{1,13},{2,14},{3,15},{4,0},{5,1},{6,2},{7,3},{8,4},{9,5},{1... | collective-permute-start | bytes 786440 | tf_op jit(solution)/shard_map/ppermute | solution.py:381
  56.7 7.7 %collective-permute-start.14 = (f32[32,2048]{1,0:T(8,128)S(1)}, f32[32,2048]{1,0:T(8,128)S(1)}, u32[]{:S(2)}, u32[]{:S(2)}) collective-permute-start(f32[32,2048]{1,0:T(8,128)S(1)} %get-tuple-element.59), channel_id=1, source_target_pairs={{0,1},{1,2},{2,3},{3,0},{4,5},{5,6},{6,7},{7,4},{8,9},{9,10},{10,1... | collective-permute-start | bytes 786440 | tf_op jit(solution)/shard_map/ppermute | solution.py:381
  56.7 7.7 %collective-permute-start.15 = (f32[32,2048]{1,0:T(8,128)S(1)}, f32[32,2048]{1,0:T(8,128)S(1)}, u32[]{:S(2)}, u32[]{:S(2)}) collective-permute-start(f32[32,2048]{1,0:T(8,128)S(1)} %get-tuple-element.60), channel_id=1, source_target_pairs={{0,3},{1,0},{2,1},{3,2},{4,7},{5,4},{6,5},{7,6},{8,11},{9,8},{10,9... | collective-permute-start | bytes 786440 | tf_op jit(solution)/shard_map/ppermute | solution.py:381
  66.9 9.2 %collective-permute-start.16 = (f32[512,128]{1,0:T(8,128)S(1)}, f32[512,128]{1,0:T(8,128)S(1)}, u32[]{:S(2)}, u32[]{:S(2)}) collective-permute-start(f32[512,128]{1,0:T(8,128)S(1)} %get-tuple-element.79), channel_id=1, source_target_pairs={{0,0},{1,1},{2,2},{3,3},{4,16},{5,17},{6,18},{7,19},{8,32},{9,33},... | collective-permute-start | bytes 786440 | tf_op jit(solution)/shard_map/ppermute | solution.py:424
  67.6 8.5 %collective-permute-start.17 = (f32[512,128]{1,0:T(8,128)S(1)}, f32[512,128]{1,0:T(8,128)S(1)}, u32[]{:S(2)}, u32[]{:S(2)}) collective-permute-start(f32[512,128]{1,0:T(8,128)S(1)} %get-tuple-element.78), channel_id=1, source_target_pairs={{0,4},{1,5},{2,6},{3,7},{4,20},{5,21},{6,22},{7,23},{8,36},{9,37},... | collective-permute-start | bytes 786440 | tf_op jit(solution)/shard_map/ppermute | solution.py:424
  70.6 10.9 %collective-permute-start.18 = (f32[512,128]{1,0:T(8,128)S(1)}, f32[512,128]{1,0:T(8,128)S(1)}, u32[]{:S(2)}, u32[]{:S(2)}) collective-permute-start(f32[512,128]{1,0:T(8,128)S(1)} %get-tuple-element.77), channel_id=1, source_target_pairs={{0,8},{1,9},{2,10},{3,11},{4,24},{5,25},{6,26},{7,27},{8,40},{9,41... | collective-permute-start | bytes 786440 | tf_op jit(solution)/shard_map/ppermute | solution.py:424
  72.3 9.4 %collective-permute-start.19 = (f32[512,128]{1,0:T(8,128)S(1)}, f32[512,128]{1,0:T(8,128)S(1)}, u32[]{:S(2)}, u32[]{:S(2)}) collective-permute-start(f32[512,128]{1,0:T(8,128)S(1)} %get-tuple-element.76), channel_id=1, source_target_pairs={{0,12},{1,13},{2,14},{3,15},{4,28},{5,29},{6,30},{7,31},{8,44},{9,... | collective-permute-start | bytes 786440 | tf_op jit(solution)/shard_map/ppermute | solution.py:424
  83.9 8.9 %collective-permute-start.20 = (f32[256,512]{1,0:T(8,128)S(1)}, f32[256,512]{1,0:T(8,128)S(1)}, u32[]{:S(2)}, u32[]{:S(2)}) collective-permute-start(f32[256,512]{1,0:T(8,128)S(1)} %get-tuple-element.65), channel_id=1, source_target_pairs={{0,64},{64,0},{1,65},{65,1},{2,66},{66,2},{3,67},{67,3},{4,68},{68... | collective-permute-start | bytes 1572872 | tf_op jit(solution)/shard_map/ppermute | solution.py:430
  115.4 16.6 %all-to-all-start.2 = ((f32[64,4,512]{2,1,0:T(4,128)}), f32[64,4,512]{2,1,0:T(4,128)S(1)}, u32[]{:S(2)}, u32[]{:S(2)}) async-start(f32[64,4,512]{2,1,0:T(4,128)} %broadcast_in_dim.12), calls=%async_computation.2 | async-start | bytes 1048576 | tf_op jit(solution)/shard_map/all_to_all | solution.py:370
  120.0 12.1 %collective-permute-start.21 = (f32[512,128]{1,0:T(8,128)S(1)}, f32[512,128]{1,0:T(8,128)S(1)}, u32[]{:S(2)}, u32[]{:S(2)}) collective-permute-start(f32[512,128]{1,0:T(8,128)S(1)} %get-tuple-element.68), channel_id=1, source_target_pairs={{0,0},{1,1},{2,2},{3,3},{4,16},{5,17},{6,18},{7,19},{8,32},{9,33},... | collective-permute-start | bytes 786440 | tf_op jit(solution)/shard_map/ppermute | solution.py:432
  132.2 18.2 %collective-permute-start.22 = (f32[256,512]{1,0:T(8,128)S(1)}, f32[256,512]{1,0:T(8,128)S(1)}, u32[]{:S(2)}, u32[]{:S(2)}) collective-permute-start(f32[256,512]{1,0:T(8,128)S(1)} %reshape.30.own_ref), channel_id=1, source_target_pairs={{0,64},{64,0},{1,65},{65,1},{2,66},{66,2},{3,67},{67,3},{4,68},{68... | collective-permute-start | bytes 1572872 | tf_op jit(solution)/shard_map/ppermute | solution.py:438
  137.9 35.5 %collective-permute-start.23 = (f32[512,128]{1,0:T(8,128)S(1)}, f32[512,128]{1,0:T(8,128)S(1)}, u32[]{:S(2)}, u32[]{:S(2)}) collective-permute-start(f32[512,128]{1,0:T(8,128)S(1)} %collective-permute-done.21.p0), channel_id=1, source_target_pairs={{0,16},{16,32},{32,48},{48,0},{1,17},{17,33},{33,49},{49,1},{2,18}... | collective-permute-start | bytes 786440 | tf_op jit(solution)/shard_map/ppermute | solution.py:375
  143.3 30.2 %collective-permute-start.24 = (f32[512,128]{1,0:T(8,128)S(1)}, f32[512,128]{1,0:T(8,128)S(1)}, u32[]{:S(2)}, u32[]{:S(2)}) collective-permute-start(f32[512,128]{1,0:T(8,128)S(1)} %collective-permute-done.21.p0), channel_id=1, source_target_pairs={{0,32},{16,48},{32,0},{48,16},{1,33},{17,49},{33,1},{49,17},{2,34}... | collective-permute-start | bytes 786440 | tf_op jit(solution)/shard_map/ppermute | solution.py:375
  150.3 23.1 %collective-permute-start.25 = (f32[512,128]{1,0:T(8,128)S(1)}, f32[512,128]{1,0:T(8,128)S(1)}, u32[]{:S(2)}, u32[]{:S(2)}) collective-permute-start(f32[512,128]{1,0:T(8,128)S(1)} %collective-permute-done.21.p0), channel_id=1, source_target_pairs={{0,48},{16,0},{32,16},{48,32},{1,49},{17,1},{33,17},{49,33},{2,50}... | collective-permute-start | bytes 786440 | tf_op jit(solution)/shard_map/ppermute | solution.py:375
  (15 other events, 166.3 us)
Sparse Core Ops, SparseCore 0:
  114.7 56.1 all-gather.2

commit v5 on v4

--- a/solution.py
+++ b/solution.py
@@ -341,7 +341,7 @@
             pltpu.VMEM((RING, rows, cols_dev), jnp.float32),
             pltpu.SemaphoreType.DMA((3, RING)),
         ],
-        compiler_params=pltpu.CompilerParams(vmem_limit_bytes=50 * 2**20),
+        compiler_params=pltpu.CompilerParams(vmem_limit_bytes=52 * 2**20),
         name="finish",
     )(at, neg, u, *pieces, prod_rows.reshape(RING, RING, B, m), covariance)
     return delta.reshape(rows_dev), new
@@ -431,8 +431,9 @@
     perm = [(number(a, b, x), number(b, a, x)) for a, b, x in spots]
     home = lax.ppermute(piece, ("row", "col"), perm)
     summed = exchange(own.reshape(64, h // 64, m), ("row", "col"))
-    share, turned = tie(jnp.sum(summed, axis=0, keepdims=True), turned)
+    summed, turned = tie(summed, turned)
     prod_rows = lax.all_gather(turned, "col", axis=0)
+    share = jnp.sum(summed, axis=0, keepdims=True)
     own = exchange(jnp.broadcast_to(share, (64, h // 64, m)), ("row", "col")).reshape(h, m)
     own, home = tie(own, home)
     other = lax.ppermute(own, "grp", swap)

time: 191 us -> 190 us (level)
    unnamed x29 -> x27, local copies, waits for them, and re-layouts: 9.95 us -> 9.11 us
where the time goes in v5:
time: 190 us
  starting transfers between devices  59.8 us (31%)
  Pallas kernels  46.5 us (24%)
  blocking collectives  34.7 us (18%)
  waiting for transfers between devices  22.9 us (12%)
  between operations  14.4 us (8%)
  local copies, waits for them, and re-layouts  11 us (6%)
    all_to_all x2, blocking collectives, exchange(): return lax.all_to_all(value, axes, split_axis=0, concat_axis=0, tiled=True)  34.7 us
    ppermute x16, starting transfers between devices, shifted(): return lax.ppermute(value, 'col', perm)  21.9 us
    pallas_call x1, Pallas kernels, negative_inverse(): pl.pallas_call(inverse_kernel, out_shape=(jax.ShapeDtypeStruct((m, m), jn...  21.4 us
    ppermute x3, starting transfers between devices, shifted(): lax.ppermute(value, 'row', [(i, (i + by) % RING) for i in range(RING)])  12.4 us
    all_to_all x1, waiting for transfers between devices, exchange(): return lax.all_to_all(value, axes, split_axis=0, concat_axis=0, tiled=True)  11.4 us
    pallas_call x1, Pallas kernels, finish(): pl.pallas_call(final_kernel, out_shape=(jax.ShapeDtypeStruct((rows_dev, c...  10 us
    unnamed x27, local copies, waits for them, and re-layouts  9.11 us
    ppermute x4, starting transfers between devices, per_device(): came.append(lax.ppermute(out[j], ('row', 'col'), perm))  7.78 us
  transfers between devices with their start and end apart: 28, of which 7 were waited for; matrix products, arithmetic and copies ran while one was open for 1% of the time, Pallas kernels for 16%

profile of v5, /device:TPU:1, one launch (start us, length us, event | category | flops | bytes accessed | tf_op | source)
XLA Modules:
  0.0 189.6 jit_solution(8521380515808871333)
XLA Ops:
  7.2 13.4 %all_to_all.15 = f32[8,4,2048]{2,1,0:T(4,128)S(1)} all-to-all(f32[8,4,2048]{2,1,0:T(4,128)} %bitcast.20), channel_id=1, replica_groups=mesh['grp'=2,'row'=4,'col'=16] {'grp','row'}, dimensions={0} | all-to-all | bytes 524288 | tf_op jit(solution)/shard_map/all_to_all | solution.py:370
  26.7 2.3 %collective-permute-done.2.n2 = f32[16,2048]{1,0:T(8,128)S(1)} collective-permute-done((f32[16,2048]{1,0:T(8,128)S(1)}, f32[16,2048]{1,0:T(8,128)S(1)}, u32[]{:S(2)}, u32[]{:S(2)}) %collective-permute-start.2) | collective-permute-done | bytes 131104 | tf_op jit(solution)/shard_map/ppermute | solution.py:381
  29.1 2.7 %collective-permute-start.5 = (f32[8,2048]{1,0:T(8,128)S(1)}, f32[8,2048]{1,0:T(8,128)S(1)}, u32[]{:S(2)}, u32[]{:S(2)}) collective-permute-start(f32[8,2048]{1,0:T(8,128)S(1)} %get-tuple-element.44), channel_id=1, source_target_pairs={{0,3},{1,0},{2,1},{3,2},{4,7},{5,4},{6,5},{7,6},{8,11},{9,8},{10,9... | collective-permute-start | bytes 196616 | tf_op jit(solution)/shard_map/ppermute | solution.py:381
  36.3 2.7 %collective-permute-start.11 = (f32[64,2048]{1,0:T(8,128)S(1)}, f32[64,2048]{1,0:T(8,128)}, u32[]{:S(2)}, u32[]{:S(2)}) collective-permute-start(f32[64,2048]{1,0:T(8,128)S(1)} %constant_dynamic-update-slice_fusion.5.refs_1_), channel_id=1, source_target_pairs={{0,3},{1,0},{2,1},{3,2},{4,7},{5,4},{6,5},{7,6},{8,11},{9,8},{10,9... | collective-permute-start | bytes 1572872 | tf_op jit(solution)/shard_map/ppermute | solution.py:381
  41.7 2.2 %copy-done = f32[2048,512]{1,0:T(8,128)S(1)} copy-done((f32[2048,512]{1,0:T(8,128)S(1)}, f32[2048,512]{1,0:T(8,128)}, u32[]{:S(2)}) %copy-start) | copy-done | bytes 4194328
  50.8 1.8 multiply.2.early_ref
  54.0 2.6 %collective-permute-start.13 = (f32[32,2048]{1,0:T(8,128)S(1)}, f32[32,2048]{1,0:T(8,128)S(1)}, u32[]{:S(2)}, u32[]{:S(2)}) collective-permute-start(f32[32,2048]{1,0:T(8,128)S(1)} %get-tuple-element.58), channel_id=1, source_target_pairs={{0,12},{1,13},{2,14},{3,15},{4,0},{5,1},{6,2},{7,3},{8,4},{9,5},{1... | collective-permute-start | bytes 786440 | tf_op jit(solution)/shard_map/ppermute | solution.py:381
  56.7 2.7 %collective-permute-start.15 = (f32[32,2048]{1,0:T(8,128)S(1)}, f32[32,2048]{1,0:T(8,128)S(1)}, u32[]{:S(2)}, u32[]{:S(2)}) collective-permute-start(f32[32,2048]{1,0:T(8,128)S(1)} %get-tuple-element.60), channel_id=1, source_target_pairs={{0,3},{1,0},{2,1},{3,2},{4,7},{5,4},{6,5},{7,6},{8,11},{9,8},{10,9... | collective-permute-start | bytes 786440 | tf_op jit(solution)/shard_map/ppermute | solution.py:381
  59.4 5.0 %multiply.3.middle_ref = f32[256,512]{1,0:T(8,128)S(1)} custom-call(f32[64,2048]{1,0:T(8,128)} %collective-permute-done.8.n0.refs_0_.refs_2_, f32[64,2048]{1,0:T(8,128)} %collective-permute-done.9.n1.refs_1_.refs_3_, f32[64,2048]{1,0:T(8,128)} %collective-permute-done.10.n2.refs_2_.refs_4_, f32[64,2048]{1,0:T(8,128)} %collective-permute-done.11.n3.refs_3_.refs_5_, ...), custom_call_target="tpu_custom_call" | custom-call | flops 3221225472 | bytes 8388608 | tf_op jit(solution)/shard_map/multiply/pallas_call | solution.py:183
  64.4 2.4 %multiply_last.1 = f32[4,512,128]{2,1,0:T(8,128)S(1)} custom-call(s32[4]{0:T(128)S(1)} %pad_add_fusion.at_ref, f32[32,2048]{1,0:T(8,128)S(1)} %collective-permute-done.12.c0.refs_6_, f32[32,2048]{1,0:T(8,128)S(1)} %collective-permute-done.13.c1.refs_7_, f32[32,2048]{1,0:T(8,128)S(1)} %collective-permute-done.14.c2.refs_8_, ...), custom_call_target="tpu_custom_call" | custom-call | tf_op jit(solution)/shard_map/multiply_last/pallas_call | solution.py:223
  67.6 3.0 %collective-permute-start.17 = (f32[512,128]{1,0:T(8,128)S(1)}, f32[512,128]{1,0:T(8,128)S(1)}, u32[]{:S(2)}, u32[]{:S(2)}) collective-permute-start(f32[512,128]{1,0:T(8,128)S(1)} %get-tuple-element.78), channel_id=1, source_target_pairs={{0,4},{1,5},{2,6},{3,7},{4,20},{5,21},{6,22},{7,23},{8,36},{9,37},... | collective-permute-start | bytes 786440 | tf_op jit(solution)/shard_map/ppermute | solution.py:424
  70.6 1.7 collective-permute-start.18
  72.3 2.3 %collective-permute-start.19 = (f32[512,128]{1,0:T(8,128)S(1)}, f32[512,128]{1,0:T(8,128)S(1)}, u32[]{:S(2)}, u32[]{:S(2)}) collective-permute-start(f32[512,128]{1,0:T(8,128)S(1)} %get-tuple-element.76), channel_id=1, source_target_pairs={{0,12},{1,13},{2,14},{3,15},{4,28},{5,29},{6,30},{7,31},{8,44},{9,... | collective-permute-start | bytes 786440 | tf_op jit(solution)/shard_map/ppermute | solution.py:424
  76.1 5.4 %collective-permute-done.18.r2 = f32[512,128]{1,0:T(8,128)S(1)} collective-permute-done((f32[512,128]{1,0:T(8,128)S(1)}, f32[512,128]{1,0:T(8,128)S(1)}, u32[]{:S(2)}, u32[]{:S(2)}) %collective-permute-start.18) | collective-permute-done | bytes 262176 | tf_op jit(solution)/shard_map/ppermute | solution.py:424
  81.7 2.2 %gram.1 = (f32[512,128]{1,0:T(8,128)S(1)}, f32[128,512]{1,0:T(8,128)}, f32[256,512]{1,0:T(8,128)S(1)}, f32[256,512]{1,0:T(8,128)S(1)}) custom-call(s32[4]{0:T(128)S(1)} %pad_add_fusion.at_ref, f32[512,128]{1,0:T(8,128)S(1)} %collective-permute-done.16.r0, f32[512,128]{1,0:T(8,128)S(1)} %collective-permute-done.17.r1, ...), custom_call_target="tpu_custom_call" | custom-call | tf_op jit(solution)/shard_map/gram/pallas_call | solution.py:280
  83.9 7.4 %collective-permute-start.20 = (f32[256,512]{1,0:T(8,128)S(1)}, f32[256,512]{1,0:T(8,128)S(1)}, u32[]{:S(2)}, u32[]{:S(2)}) collective-permute-start(f32[256,512]{1,0:T(8,128)S(1)} %get-tuple-element.65), channel_id=1, source_target_pairs={{0,64},{64,0},{1,65},{65,1},{2,66},{66,2},{3,67},{67,3},{4,68},{68... | collective-permute-start | bytes 1572872 | tf_op jit(solution)/shard_map/ppermute | solution.py:430
  93.1 21.3 %all_to_all.16 = f32[64,4,512]{2,1,0:T(4,128)S(1)} all-to-all(f32[64,4,512]{2,1,0:T(4,128)S(1)} %reshape.30), channel_id=1, replica_groups=mesh['grp'=2,'row'=4,'col'=16] {'row','col'}, dimensions={0} | all-to-all | bytes 1048576 | tf_op jit(solution)/shard_map/all_to_all | solution.py:370
  115.4 4.6 %all-to-all-start.2 = ((f32[64,4,512]{2,1,0:T(4,128)}), f32[64,4,512]{2,1,0:T(4,128)S(1)}, u32[]{:S(2)}, u32[]{:S(2)}) async-start(f32[64,4,512]{2,1,0:T(4,128)} %broadcast_in_dim.2), calls=%async_computation.2 | async-start | bytes 1048576 | tf_op jit(solution)/shard_map/all_to_all | solution.py:370
  120.7 11.4 %all-to-all-done.2 = f32[64,4,512]{2,1,0:T(4,128)S(1)} async-done(((f32[64,4,512]{2,1,0:T(4,128)}), f32[64,4,512]{2,1,0:T(4,128)S(1)}, u32[]{:S(2)}, u32[]{:S(2)}) %all-to-all-start.2) | async-done | bytes 524320 | tf_op jit(solution)/shard_map/all_to_all | solution.py:370
  132.3 5.0 %collective-permute-start.22 = (f32[256,512]{1,0:T(8,128)S(1)}, f32[256,512]{1,0:T(8,128)S(1)}, u32[]{:S(2)}, u32[]{:S(2)}) collective-permute-start(f32[256,512]{1,0:T(8,128)S(1)} %reshape.31.own_ref), channel_id=1, source_target_pairs={{0,64},{64,0},{1,65},{65,1},{2,66},{66,2},{3,67},{67,3},{4,68},{68... | collective-permute-start | bytes 1572872 | tf_op jit(solution)/shard_map/ppermute | solution.py:439
  137.9 5.4 %collective-permute-start.23 = (f32[512,128]{1,0:T(8,128)S(1)}, f32[512,128]{1,0:T(8,128)S(1)}, u32[]{:S(2)}, u32[]{:S(2)}) collective-permute-start(f32[512,128]{1,0:T(8,128)S(1)} %collective-permute-done.21.p0), channel_id=1, source_target_pairs={{0,16},{16,32},{32,48},{48,0},{1,17},{17,33},{33,49},{49,1},{2,18}... | collective-permute-start | bytes 786440 | tf_op jit(solution)/shard_map/ppermute | solution.py:375
  143.3 7.0 %collective-permute-start.24 = (f32[512,128]{1,0:T(8,128)S(1)}, f32[512,128]{1,0:T(8,128)S(1)}, u32[]{:S(2)}, u32[]{:S(2)}) collective-permute-start(f32[512,128]{1,0:T(8,128)S(1)} %collective-permute-done.21.p0), channel_id=1, source_target_pairs={{0,32},{16,48},{32,0},{48,16},{1,33},{17,49},{33,1},{49,17},{2,34}... | collective-permute-start | bytes 786440 | tf_op jit(solution)/shard_map/ppermute | solution.py:375
  150.3 21.4 %inverse.1 = (f32[512,512]{1,0:T(8,128)S(1)}, f32[1,512]{1,0:T(1,128)S(1)}) custom-call(s32[4]{0:T(128)S(1)} %pad_add_fusion.at_ref, f32[256,512]{1,0:T(8,128)S(1)} %reshape.31.own_ref, f32[256,512]{1,0:T(8,128)S(1)} %collective-permute-done.22.other_ref, f32[1,512]{1,0:T(1,128)S(1)} %reshape_reshape.6.noise_ref, f32[1,512]{1,0:T(1,128)S(1)} %reshape_reshape.7.innov_ref), custom_call_target="tpu_custom_call" | custom-call | flops 24999999488 | bytes 2097152 | tf_op jit(solution)/shard_map/inverse/pallas_call | solution.py:116
  172.7 10.0 %finish.1 = (f32[2048,512]{1,0:T(8,128)}, f32[1,2048]{1,0:T(1,128)}) custom-call(s32[4]{0:T(128)S(1)} %pad_add_fusion.at_ref, f32[512,512]{1,0:T(8,128)} %copy-done.7, f32[1,512]{1,0:T(1,128)S(1)} %get-tuple-element.71.u_ref, f32[512,128]{1,0:T(8,128)S(1)} %collective-permute-done.21.p0, f32[512,128]{1,0:T(8,128)S(1)} %collective-permute-done.23.p1, ...), custom_call_target="tpu_custom_call" | custom-call | tf_op jit(solution)/shard_map/finish/pallas_call | solution.py:327
  (90 shorter events, 29.3 us)
Async XLA Ops:
  7.2 165.5 %all-gather.3.cloned.1.call-start = ((), (), s32[]{:S(2)}) async-start(), calls=%async_computation.3 | async-start | bytes 4456448 | tf_op jit(solution)/shard_map/all_gather | solution.py:435
  20.7 6.0 %collective-permute-start = (f32[16,2048]{1,0:T(8,128)S(1)}, f32[16,2048]{1,0:T(8,128)S(1)}, u32[]{:S(2)}, u32[]{:S(2)}) collective-permute-start(f32[16,2048]{1,0:T(8,128)S(1)} %slice.25), channel_id=1, source_target_pairs={{0,1},{1,2},{2,3},{3,0},{4,5},{5,6},{6,7},{7,4},{8,9},{9,10},{10,1... | collective-permute-start | bytes 393224 | tf_op jit(solution)/shard_map/ppermute | solution.py:381
  23.5 5.5 %collective-permute-start.2 = (f32[16,2048]{1,0:T(8,128)S(1)}, f32[16,2048]{1,0:T(8,128)S(1)}, u32[]{:S(2)}, u32[]{:S(2)}) collective-permute-start(f32[16,2048]{1,0:T(8,128)S(1)} %slice.27), channel_id=1, source_target_pairs={{0,4},{1,5},{2,6},{3,7},{4,8},{5,9},{6,10},{7,11},{8,12},{9,13},{1... | collective-permute-start | bytes 393224 | tf_op jit(solution)/shard_map/ppermute | solution.py:381
  29.0 5.5 %collective-permute-start.4 = (f32[8,2048]{1,0:T(8,128)S(1)}, f32[8,2048]{1,0:T(8,128)S(1)}, u32[]{:S(2)}, u32[]{:S(2)}) collective-permute-start(f32[8,2048]{1,0:T(8,128)S(1)} %get-tuple-element.43), channel_id=1, source_target_pairs={{0,1},{1,2},{2,3},{3,0},{4,5},{5,6},{6,7},{7,4},{8,9},{9,10},{10,1... | collective-permute-start | bytes 196616 | tf_op jit(solution)/shard_map/ppermute | solution.py:381
  29.1 5.4 %collective-permute-start.5 = (f32[8,2048]{1,0:T(8,128)S(1)}, f32[8,2048]{1,0:T(8,128)S(1)}, u32[]{:S(2)}, u32[]{:S(2)}) collective-permute-start(f32[8,2048]{1,0:T(8,128)S(1)} %get-tuple-element.44), channel_id=1, source_target_pairs={{0,3},{1,0},{2,1},{3,2},{4,7},{5,4},{6,5},{7,6},{8,11},{9,8},{10,9... | collective-permute-start | bytes 196616 | tf_op jit(solution)/shard_map/ppermute | solution.py:381
  36.2 16.4 %collective-permute-start.10 = (f32[64,2048]{1,0:T(8,128)S(1)}, f32[64,2048]{1,0:T(8,128)}, u32[]{:S(2)}, u32[]{:S(2)}) collective-permute-start(f32[64,2048]{1,0:T(8,128)S(1)} %constant_dynamic-update-slice_fusion.5.refs_1_), channel_id=1, source_target_pairs={{0,1},{1,2},{2,3},{3,0},{4,5},{5,6},{6,7},{7,4},{8,9},{9,10},{10,1... | collective-permute-start | bytes 1572872 | tf_op jit(solution)/shard_map/ppermute | solution.py:381
  36.3 16.3 %collective-permute-start.11 = (f32[64,2048]{1,0:T(8,128)S(1)}, f32[64,2048]{1,0:T(8,128)}, u32[]{:S(2)}, u32[]{:S(2)}) collective-permute-start(f32[64,2048]{1,0:T(8,128)S(1)} %constant_dynamic-update-slice_fusion.5.refs_1_), channel_id=1, source_target_pairs={{0,3},{1,0},{2,1},{3,2},{4,7},{5,4},{6,5},{7,6},{8,11},{9,8},{10,9... | collective-permute-start | bytes 1572872 | tf_op jit(solution)/shard_map/ppermute | solution.py:381
  39.0 13.7 %collective-permute-start.8 = (f32[64,2048]{1,0:T(8,128)S(1)}, f32[64,2048]{1,0:T(8,128)}, u32[]{:S(2)}, u32[]{:S(2)}) collective-permute-start(f32[64,2048]{1,0:T(8,128)S(1)} %constant_dynamic-update-slice_fusion.refs_0_), channel_id=1, source_target_pairs={{0,4},{1,5},{2,6},{3,7},{4,8},{5,9},{6,10},{7,11},{8,12},{9,13},{1... | collective-permute-start | bytes 1572872 | tf_op jit(solution)/shard_map/ppermute | solution.py:381
  40.2 12.4 %collective-permute-start.9 = (f32[64,2048]{1,0:T(8,128)S(1)}, f32[64,2048]{1,0:T(8,128)}, u32[]{:S(2)}, u32[]{:S(2)}) collective-permute-start(f32[64,2048]{1,0:T(8,128)S(1)} %constant_dynamic-update-slice_fusion.refs_0_), channel_id=1, source_target_pairs={{0,12},{1,13},{2,14},{3,15},{4,0},{5,1},{6,2},{7,3},{8,4},{9,5},{1... | collective-permute-start | bytes 1572872 | tf_op jit(solution)/shard_map/ppermute | solution.py:381
  53.9 10.4 %collective-permute-start.12 = (f32[32,2048]{1,0:T(8,128)S(1)}, f32[32,2048]{1,0:T(8,128)S(1)}, u32[]{:S(2)}, u32[]{:S(2)}) collective-permute-start(f32[32,2048]{1,0:T(8,128)S(1)} %get-tuple-element.57), channel_id=1, source_target_pairs={{0,4},{1,5},{2,6},{3,7},{4,8},{5,9},{6,10},{7,11},{8,12},{9,13},{1... | collective-permute-start | bytes 786440 | tf_op jit(solution)/shard_map/ppermute | solution.py:381
  54.0 10.3 %collective-permute-start.13 = (f32[32,2048]{1,0:T(8,128)S(1)}, f32[32,2048]{1,0:T(8,128)S(1)}, u32[]{:S(2)}, u32[]{:S(2)}) collective-permute-start(f32[32,2048]{1,0:T(8,128)S(1)} %get-tuple-element.58), channel_id=1, source_target_pairs={{0,12},{1,13},{2,14},{3,15},{4,0},{5,1},{6,2},{7,3},{8,4},{9,5},{1... | collective-permute-start | bytes 786440 | tf_op jit(solution)/shard_map/ppermute | solution.py:381
  56.7 7.7 %collective-permute-start.14 = (f32[32,2048]{1,0:T(8,128)S(1)}, f32[32,2048]{1,0:T(8,128)S(1)}, u32[]{:S(2)}, u32[]{:S(2)}) collective-permute-start(f32[32,2048]{1,0:T(8,128)S(1)} %get-tuple-element.59), channel_id=1, source_target_pairs={{0,1},{1,2},{2,3},{3,0},{4,5},{5,6},{6,7},{7,4},{8,9},{9,10},{10,1... | collective-permute-start | bytes 786440 | tf_op jit(solution)/shard_map/ppermute | solution.py:381
  56.7 7.7 %collective-permute-start.15 = (f32[32,2048]{1,0:T(8,128)S(1)}, f32[32,2048]{1,0:T(8,128)S(1)}, u32[]{:S(2)}, u32[]{:S(2)}) collective-permute-start(f32[32,2048]{1,0:T(8,128)S(1)} %get-tuple-element.60), channel_id=1, source_target_pairs={{0,3},{1,0},{2,1},{3,2},{4,7},{5,4},{6,5},{7,6},{8,11},{9,8},{10,9... | collective-permute-start | bytes 786440 | tf_op jit(solution)/shard_map/ppermute | solution.py:381
  66.9 9.2 %collective-permute-start.16 = (f32[512,128]{1,0:T(8,128)S(1)}, f32[512,128]{1,0:T(8,128)S(1)}, u32[]{:S(2)}, u32[]{:S(2)}) collective-permute-start(f32[512,128]{1,0:T(8,128)S(1)} %get-tuple-element.79), channel_id=1, source_target_pairs={{0,0},{1,1},{2,2},{3,3},{4,16},{5,17},{6,18},{7,19},{8,32},{9,33},... | collective-permute-start | bytes 786440 | tf_op jit(solution)/shard_map/ppermute | solution.py:424
  67.6 8.5 %collective-permute-start.17 = (f32[512,128]{1,0:T(8,128)S(1)}, f32[512,128]{1,0:T(8,128)S(1)}, u32[]{:S(2)}, u32[]{:S(2)}) collective-permute-start(f32[512,128]{1,0:T(8,128)S(1)} %get-tuple-element.78), channel_id=1, source_target_pairs={{0,4},{1,5},{2,6},{3,7},{4,20},{5,21},{6,22},{7,23},{8,36},{9,37},... | collective-permute-start | bytes 786440 | tf_op jit(solution)/shard_map/ppermute | solution.py:424
  70.6 10.9 %collective-permute-start.18 = (f32[512,128]{1,0:T(8,128)S(1)}, f32[512,128]{1,0:T(8,128)S(1)}, u32[]{:S(2)}, u32[]{:S(2)}) collective-permute-start(f32[512,128]{1,0:T(8,128)S(1)} %get-tuple-element.77), channel_id=1, source_target_pairs={{0,8},{1,9},{2,10},{3,11},{4,24},{5,25},{6,26},{7,27},{8,40},{9,41... | collective-permute-start | bytes 786440 | tf_op jit(solution)/shard_map/ppermute | solution.py:424
  72.3 9.4 %collective-permute-start.19 = (f32[512,128]{1,0:T(8,128)S(1)}, f32[512,128]{1,0:T(8,128)S(1)}, u32[]{:S(2)}, u32[]{:S(2)}) collective-permute-start(f32[512,128]{1,0:T(8,128)S(1)} %get-tuple-element.76), channel_id=1, source_target_pairs={{0,12},{1,13},{2,14},{3,15},{4,28},{5,29},{6,30},{7,31},{8,44},{9,... | collective-permute-start | bytes 786440 | tf_op jit(solution)/shard_map/ppermute | solution.py:424
  83.9 8.9 %collective-permute-start.20 = (f32[256,512]{1,0:T(8,128)S(1)}, f32[256,512]{1,0:T(8,128)S(1)}, u32[]{:S(2)}, u32[]{:S(2)}) collective-permute-start(f32[256,512]{1,0:T(8,128)S(1)} %get-tuple-element.65), channel_id=1, source_target_pairs={{0,64},{64,0},{1,65},{65,1},{2,66},{66,2},{3,67},{67,3},{4,68},{68... | collective-permute-start | bytes 1572872 | tf_op jit(solution)/shard_map/ppermute | solution.py:430
  115.4 16.7 %all-to-all-start.2 = ((f32[64,4,512]{2,1,0:T(4,128)}), f32[64,4,512]{2,1,0:T(4,128)S(1)}, u32[]{:S(2)}, u32[]{:S(2)}) async-start(f32[64,4,512]{2,1,0:T(4,128)} %broadcast_in_dim.2), calls=%async_computation.2 | async-start | bytes 1048576 | tf_op jit(solution)/shard_map/all_to_all | solution.py:370
  120.1 12.3 %collective-permute-start.21 = (f32[512,128]{1,0:T(8,128)S(1)}, f32[512,128]{1,0:T(8,128)S(1)}, u32[]{:S(2)}, u32[]{:S(2)}) collective-permute-start(f32[512,128]{1,0:T(8,128)S(1)} %get-tuple-element.68), channel_id=1, source_target_pairs={{0,0},{1,1},{2,2},{3,3},{4,16},{5,17},{6,18},{7,19},{8,32},{9,33},... | collective-permute-start | bytes 786440 | tf_op jit(solution)/shard_map/ppermute | solution.py:432
  132.3 18.0 %collective-permute-start.22 = (f32[256,512]{1,0:T(8,128)S(1)}, f32[256,512]{1,0:T(8,128)S(1)}, u32[]{:S(2)}, u32[]{:S(2)}) collective-permute-start(f32[256,512]{1,0:T(8,128)S(1)} %reshape.31.own_ref), channel_id=1, source_target_pairs={{0,64},{64,0},{1,65},{65,1},{2,66},{66,2},{3,67},{67,3},{4,68},{68... | collective-permute-start | bytes 1572872 | tf_op jit(solution)/shard_map/ppermute | solution.py:439
  137.9 34.8 %collective-permute-start.23 = (f32[512,128]{1,0:T(8,128)S(1)}, f32[512,128]{1,0:T(8,128)S(1)}, u32[]{:S(2)}, u32[]{:S(2)}) collective-permute-start(f32[512,128]{1,0:T(8,128)S(1)} %collective-permute-done.21.p0), channel_id=1, source_target_pairs={{0,16},{16,32},{32,48},{48,0},{1,17},{17,33},{33,49},{49,1},{2,18}... | collective-permute-start | bytes 786440 | tf_op jit(solution)/shard_map/ppermute | solution.py:375
  143.3 29.4 %collective-permute-start.24 = (f32[512,128]{1,0:T(8,128)S(1)}, f32[512,128]{1,0:T(8,128)S(1)}, u32[]{:S(2)}, u32[]{:S(2)}) collective-permute-start(f32[512,128]{1,0:T(8,128)S(1)} %collective-permute-done.21.p0), channel_id=1, source_target_pairs={{0,32},{16,48},{32,0},{48,16},{1,33},{17,49},{33,1},{49,17},{2,34}... | collective-permute-start | bytes 786440 | tf_op jit(solution)/shard_map/ppermute | solution.py:375
  150.3 22.4 %collective-permute-start.25 = (f32[512,128]{1,0:T(8,128)S(1)}, f32[512,128]{1,0:T(8,128)S(1)}, u32[]{:S(2)}, u32[]{:S(2)}) collective-permute-start(f32[512,128]{1,0:T(8,128)S(1)} %collective-permute-done.21.p0), channel_id=1, source_target_pairs={{0,48},{16,0},{32,16},{48,32},{1,49},{17,1},{33,17},{49,33},{2,50}... | collective-permute-start | bytes 786440 | tf_op jit(solution)/shard_map/ppermute | solution.py:375
  (14 other events, 165.3 us)
Sparse Core Ops, SparseCore 0:
  114.6 56.2 all-gather.2

commit v6 on v5

--- a/solution.py
+++ b/solution.py
@@ -406,10 +406,9 @@
     parts = split_array(covariance)
     half = 4 * mine
     a, b = got[:half], got[half:]
-    near, far = both_ways(a, b, ("x", "y"))
-    far = tie(*far)
-    a4 = jnp.concatenate([a, near[0], near[1], far[0], far[1]], axis=0)
-    b4 = jnp.concatenate([b, near[2], near[3], far[2], far[3]], axis=0)
+    came = tie(*[shifted(v, axis, by) for v, axis in ((a, "x"), (b, "y")) for by in (1, -1, 2)])
+    a4 = jnp.concatenate([a, *came[:3]], axis=0)
+    b4 = jnp.concatenate([b, *came[3:]], axis=0)
     a4, b4 = tie(a4, b4)
     near, far = both_ways(a4, b4, ("y", "x"))
     early = multiply([a4, b4], parts)

time: 190 us -> 186 us (0.979)
  starting transfers between devices: 59.8 us -> 54.1 us
  waiting for transfers between devices: 22.9 us -> 24.9 us
    ppermute x1, starting transfers between devices: 7.4 us -> 4.16 us  [per_device(): own = own + lax.ppermute(other, 'grp', swap)]
    ppermute x16 -> x14, starting transfers between devices: 21.9 us -> 19.7 us  [shifted(): return lax.ppermute(value, 'col', perm)]
    ppermute x16 -> x14, waiting for transfers between devices: 4.29 us -> 5.34 us  [shifted(): return lax.ppermute(value, 'col', perm)]
    unnamed x27 -> x20, local copies, waits for them, and re-layouts: 9.11 us -> 9.06 us
  transfers between devices with their start and end apart: 28 -> 26, of which waited for: 7 -> 6; matrix products, arithmetic and copies ran while one was open for 1% -> 1% of each run, Pallas kernels for 16% -> 16%
where the time goes in v6:
time: 186 us
  starting transfers between devices  54.1 us (29%)
  Pallas kernels  46.5 us (25%)
  blocking collectives  34.7 us (19%)
  waiting for transfers between devices  24.9 us (13%)
  between operations  14.4 us (8%)
  local copies, waits for them, and re-layouts  10.9 us (6%)
    all_to_all x2, blocking collectives, exchange(): return lax.all_to_all(value, axes, split_axis=0, concat_axis=0, tiled=True)  34.7 us
    pallas_call x1, Pallas kernels, negative_inverse(): pl.pallas_call(inverse_kernel, out_shape=(jax.ShapeDtypeStruct((m, m), jn...  21.4 us
    ppermute x14, starting transfers between devices, shifted(): return lax.ppermute(value, 'col', perm)  19.7 us
    ppermute x3, starting transfers between devices, shifted(): lax.ppermute(value, 'row', [(i, (i + by) % RING) for i in range(RING)])  12.4 us
    all_to_all x1, waiting for transfers between devices, exchange(): return lax.all_to_all(value, axes, split_axis=0, concat_axis=0, tiled=True)  11.4 us
    pallas_call x1, Pallas kernels, finish(): pl.pallas_call(final_kernel, out_shape=(jax.ShapeDtypeStruct((rows_dev, c...  10 us
    unnamed x20, local copies, waits for them, and re-layouts  9.06 us
    ppermute x4, starting transfers between devices, per_device(): came.append(lax.ppermute(out[j], ('row', 'col'), perm))  7.52 us
  transfers between devices with their start and end apart: 26, of which 6 were waited for; matrix products, arithmetic and copies ran while one was open for 1% of the time, Pallas kernels for 16%

profile of v6, /device:TPU:1, one launch (start us, length us, event | category | flops | bytes accessed | tf_op | source)
XLA Modules:
  0.0 185.9 jit_solution(6166459453013997195)
XLA Ops:
  7.2 13.4 %all_to_all.15 = f32[8,4,2048]{2,1,0:T(4,128)S(1)} all-to-all(f32[8,4,2048]{2,1,0:T(4,128)} %bitcast.20), channel_id=1, replica_groups=mesh['grp'=2,'row'=4,'col'=16] {'grp','row'}, dimensions={0} | all-to-all | bytes 524288 | tf_op jit(solution)/shard_map/all_to_all | solution.py:370
  27.9 1.7 collective-permute-start.5
  30.5 4.4 %collective-permute-done.5 = f32[16,2048]{1,0:T(8,128)S(1)} collective-permute-done((f32[16,2048]{1,0:T(8,128)S(1)}, f32[16,2048]{1,0:T(8,128)S(1)}, u32[]{:S(2)}, u32[]{:S(2)}) %collective-permute-start.5) | collective-permute-done | bytes 131104 | tf_op jit(solution)/shard_map/ppermute | solution.py:381
  35.1 2.7 %collective-permute-start.7 = (f32[64,2048]{1,0:T(8,128)S(1)}, f32[64,2048]{1,0:T(8,128)}, u32[]{:S(2)}, u32[]{:S(2)}) collective-permute-start(f32[64,2048]{1,0:T(8,128)S(1)} %get-tuple-element.39.refs_0_), channel_id=1, source_target_pairs={{0,12},{1,13},{2,14},{3,15},{4,0},{5,1},{6,2},{7,3},{8,4},{9,5},{1... | collective-permute-start | bytes 1572872 | tf_op jit(solution)/shard_map/ppermute | solution.py:381
  38.1 2.4 %collective-permute-start.9 = (f32[64,2048]{1,0:T(8,128)S(1)}, f32[64,2048]{1,0:T(8,128)}, u32[]{:S(2)}, u32[]{:S(2)}) collective-permute-start(f32[64,2048]{1,0:T(8,128)S(1)} %get-tuple-element.40.refs_1_), channel_id=1, source_target_pairs={{0,3},{1,0},{2,1},{3,2},{4,7},{5,4},{6,5},{7,6},{8,11},{9,8},{10,9... | collective-permute-start | bytes 1572872 | tf_op jit(solution)/shard_map/ppermute | solution.py:381
  40.4 2.2 %copy-done = f32[2048,512]{1,0:T(8,128)S(1)} copy-done((f32[2048,512]{1,0:T(8,128)S(1)}, f32[2048,512]{1,0:T(8,128)}, u32[]{:S(2)}) %copy-start) | copy-done | bytes 4194328
  49.6 1.8 multiply.2.early_ref
  52.8 2.7 %collective-permute-start.11 = (f32[32,2048]{1,0:T(8,128)S(1)}, f32[32,2048]{1,0:T(8,128)S(1)}, u32[]{:S(2)}, u32[]{:S(2)}) collective-permute-start(f32[32,2048]{1,0:T(8,128)S(1)} %get-tuple-element.46), channel_id=1, source_target_pairs={{0,12},{1,13},{2,14},{3,15},{4,0},{5,1},{6,2},{7,3},{8,4},{9,5},{1... | collective-permute-start | bytes 786440 | tf_op jit(solution)/shard_map/ppermute | solution.py:381
  55.5 2.7 %collective-permute-start.13 = (f32[32,2048]{1,0:T(8,128)S(1)}, f32[32,2048]{1,0:T(8,128)S(1)}, u32[]{:S(2)}, u32[]{:S(2)}) collective-permute-start(f32[32,2048]{1,0:T(8,128)S(1)} %get-tuple-element.48), channel_id=1, source_target_pairs={{0,3},{1,0},{2,1},{3,2},{4,7},{5,4},{6,5},{7,6},{8,11},{9,8},{10,9... | collective-permute-start | bytes 786440 | tf_op jit(solution)/shard_map/ppermute | solution.py:381
  58.2 5.0 %multiply.3.middle_ref = f32[256,512]{1,0:T(8,128)S(1)} custom-call(f32[64,2048]{1,0:T(8,128)} %collective-permute-done.6.n0.refs_0_.refs_2_, f32[64,2048]{1,0:T(8,128)} %collective-permute-done.7.n1.refs_1_.refs_3_, f32[64,2048]{1,0:T(8,128)} %collective-permute-done.8.n2.refs_2_.refs_4_, f32[64,2048]{1,0:T(8,128)} %collective-permute-done.9.n3.refs_3_.refs_5_, ...), custom_call_target="tpu_custom_call" | custom-call | flops 3221225472 | bytes 8388608 | tf_op jit(solution)/shard_map/multiply/pallas_call | solution.py:183
  63.2 2.4 %multiply_last.1 = f32[4,512,128]{2,1,0:T(8,128)S(1)} custom-call(s32[4]{0:T(128)S(1)} %pad_add_fusion.at_ref, f32[32,2048]{1,0:T(8,128)S(1)} %collective-permute-done.10.c0.refs_6_, f32[32,2048]{1,0:T(8,128)S(1)} %collective-permute-done.11.c1.refs_7_, f32[32,2048]{1,0:T(8,128)S(1)} %collective-permute-done.12.c2.refs_8_, ...), custom_call_target="tpu_custom_call" | custom-call | tf_op jit(solution)/shard_map/multiply_last/pallas_call | solution.py:223
  66.4 3.2 %collective-permute-start.15 = (f32[512,128]{1,0:T(8,128)S(1)}, f32[512,128]{1,0:T(8,128)S(1)}, u32[]{:S(2)}, u32[]{:S(2)}) collective-permute-start(f32[512,128]{1,0:T(8,128)S(1)} %get-tuple-element.66), channel_id=1, source_target_pairs={{0,4},{1,5},{2,6},{3,7},{4,20},{5,21},{6,22},{7,23},{8,36},{9,37},... | collective-permute-start | bytes 786440 | tf_op jit(solution)/shard_map/ppermute | solution.py:423
  71.2 2.0 %collective-permute-start.17 = (f32[512,128]{1,0:T(8,128)S(1)}, f32[512,128]{1,0:T(8,128)S(1)}, u32[]{:S(2)}, u32[]{:S(2)}) collective-permute-start(f32[512,128]{1,0:T(8,128)S(1)} %get-tuple-element.64), channel_id=1, source_target_pairs={{0,12},{1,13},{2,14},{3,15},{4,28},{5,29},{6,30},{7,31},{8,44},{9,... | collective-permute-start | bytes 786440 | tf_op jit(solution)/shard_map/ppermute | solution.py:423
  74.6 6.4 %collective-permute-done.16.r2 = f32[512,128]{1,0:T(8,128)S(1)} collective-permute-done((f32[512,128]{1,0:T(8,128)S(1)}, f32[512,128]{1,0:T(8,128)S(1)}, u32[]{:S(2)}, u32[]{:S(2)}) %collective-permute-start.16) | collective-permute-done | bytes 262176 | tf_op jit(solution)/shard_map/ppermute | solution.py:423
  81.2 2.2 %gram.1 = (f32[512,128]{1,0:T(8,128)S(1)}, f32[128,512]{1,0:T(8,128)}, f32[256,512]{1,0:T(8,128)S(1)}, f32[256,512]{1,0:T(8,128)S(1)}) custom-call(s32[4]{0:T(128)S(1)} %pad_add_fusion.at_ref, f32[512,128]{1,0:T(8,128)S(1)} %collective-permute-done.14.r0, f32[512,128]{1,0:T(8,128)S(1)} %collective-permute-done.15.r1, ...), custom_call_target="tpu_custom_call" | custom-call | tf_op jit(solution)/shard_map/gram/pallas_call | solution.py:280
  83.4 4.2 %collective-permute-start.18 = (f32[256,512]{1,0:T(8,128)S(1)}, f32[256,512]{1,0:T(8,128)S(1)}, u32[]{:S(2)}, u32[]{:S(2)}) collective-permute-start(f32[256,512]{1,0:T(8,128)S(1)} %get-tuple-element.53), channel_id=1, source_target_pairs={{0,64},{64,0},{1,65},{65,1},{2,66},{66,2},{3,67},{67,3},{4,68},{68... | collective-permute-start | bytes 1572872 | tf_op jit(solution)/shard_map/ppermute | solution.py:429
  89.3 21.3 %all_to_all.16 = f32[64,4,512]{2,1,0:T(4,128)S(1)} all-to-all(f32[64,4,512]{2,1,0:T(4,128)S(1)} %reshape.30), channel_id=1, replica_groups=mesh['grp'=2,'row'=4,'col'=16] {'row','col'}, dimensions={0} | all-to-all | bytes 1048576 | tf_op jit(solution)/shard_map/all_to_all | solution.py:370
  111.7 4.6 %all-to-all-start.2 = ((f32[64,4,512]{2,1,0:T(4,128)}), f32[64,4,512]{2,1,0:T(4,128)S(1)}, u32[]{:S(2)}, u32[]{:S(2)}) async-start(f32[64,4,512]{2,1,0:T(4,128)} %broadcast_in_dim.2), calls=%async_computation.2 | async-start | bytes 1048576 | tf_op jit(solution)/shard_map/all_to_all | solution.py:370
  117.0 11.4 %all-to-all-done.2 = f32[64,4,512]{2,1,0:T(4,128)S(1)} async-done(((f32[64,4,512]{2,1,0:T(4,128)}), f32[64,4,512]{2,1,0:T(4,128)S(1)}, u32[]{:S(2)}, u32[]{:S(2)}) %all-to-all-start.2) | async-done | bytes 524320 | tf_op jit(solution)/shard_map/all_to_all | solution.py:370
  128.6 5.0 %collective-permute-start.20 = (f32[256,512]{1,0:T(8,128)S(1)}, f32[256,512]{1,0:T(8,128)S(1)}, u32[]{:S(2)}, u32[]{:S(2)}) collective-permute-start(f32[256,512]{1,0:T(8,128)S(1)} %reshape.31.own_ref), channel_id=1, source_target_pairs={{0,64},{64,0},{1,65},{65,1},{2,66},{66,2},{3,67},{67,3},{4,68},{68... | collective-permute-start | bytes 1572872 | tf_op jit(solution)/shard_map/ppermute | solution.py:438
  134.1 5.4 %collective-permute-start.21 = (f32[512,128]{1,0:T(8,128)S(1)}, f32[512,128]{1,0:T(8,128)S(1)}, u32[]{:S(2)}, u32[]{:S(2)}) collective-permute-start(f32[512,128]{1,0:T(8,128)S(1)} %collective-permute-done.19.p0), channel_id=1, source_target_pairs={{0,16},{16,32},{32,48},{48,0},{1,17},{17,33},{33,49},{49,1},{2,18}... | collective-permute-start | bytes 786440 | tf_op jit(solution)/shard_map/ppermute | solution.py:375
  139.5 7.0 %collective-permute-start.22 = (f32[512,128]{1,0:T(8,128)S(1)}, f32[512,128]{1,0:T(8,128)S(1)}, u32[]{:S(2)}, u32[]{:S(2)}) collective-permute-start(f32[512,128]{1,0:T(8,128)S(1)} %collective-permute-done.19.p0), channel_id=1, source_target_pairs={{0,32},{16,48},{32,0},{48,16},{1,33},{17,49},{33,1},{49,17},{2,34}... | collective-permute-start | bytes 786440 | tf_op jit(solution)/shard_map/ppermute | solution.py:375
  146.5 21.4 %inverse.1 = (f32[512,512]{1,0:T(8,128)S(1)}, f32[1,512]{1,0:T(1,128)S(1)}) custom-call(s32[4]{0:T(128)S(1)} %pad_add_fusion.at_ref, f32[256,512]{1,0:T(8,128)S(1)} %reshape.31.own_ref, f32[256,512]{1,0:T(8,128)S(1)} %collective-permute-done.20.other_ref, f32[1,512]{1,0:T(1,128)S(1)} %reshape_reshape.6.noise_ref, f32[1,512]{1,0:T(1,128)S(1)} %reshape_reshape.7.innov_ref), custom_call_target="tpu_custom_call" | custom-call | flops 24999999488 | bytes 2097152 | tf_op jit(solution)/shard_map/inverse/pallas_call | solution.py:116
  168.9 10.0 %finish.1 = (f32[2048,512]{1,0:T(8,128)}, f32[1,2048]{1,0:T(1,128)}) custom-call(s32[4]{0:T(128)S(1)} %pad_add_fusion.at_ref, f32[512,512]{1,0:T(8,128)} %copy-done.7, f32[1,512]{1,0:T(1,128)S(1)} %get-tuple-element.59.u_ref, f32[512,128]{1,0:T(8,128)S(1)} %collective-permute-done.19.p0, f32[512,128]{1,0:T(8,128)S(1)} %collective-permute-done.21.p1, ...), custom_call_target="tpu_custom_call" | custom-call | tf_op jit(solution)/shard_map/finish/pallas_call | solution.py:327
  (77 shorter events, 26.1 us)
Async XLA Ops:
  7.2 161.8 %all-gather.3.cloned.1.call-start = ((), (), s32[]{:S(2)}) async-start(), calls=%async_computation.3 | async-start | bytes 4456448 | tf_op jit(solution)/shard_map/all_gather | solution.py:434
  20.7 7.2 %collective-permute-start = (f32[16,2048]{1,0:T(8,128)S(1)}, f32[16,2048]{1,0:T(8,128)S(1)}, u32[]{:S(2)}, u32[]{:S(2)}) collective-permute-start(f32[16,2048]{1,0:T(8,128)S(1)} %slice.25), channel_id=1, source_target_pairs={{0,1},{1,2},{2,3},{3,0},{4,5},{5,6},{6,7},{7,4},{8,9},{9,10},{10,1... | collective-permute-start | bytes 393224 | tf_op jit(solution)/shard_map/ppermute | solution.py:381
  21.9 7.6 %collective-permute-start.1 = (f32[16,2048]{1,0:T(8,128)S(1)}, f32[16,2048]{1,0:T(8,128)S(1)}, u32[]{:S(2)}, u32[]{:S(2)}) collective-permute-start(f32[16,2048]{1,0:T(8,128)S(1)} %slice.25), channel_id=1, source_target_pairs={{0,3},{1,0},{2,1},{3,2},{4,7},{5,4},{6,5},{7,6},{8,11},{9,8},{10,9... | collective-permute-start | bytes 393224 | tf_op jit(solution)/shard_map/ppermute | solution.py:381
  23.4 7.0 %collective-permute-start.2 = (f32[16,2048]{1,0:T(8,128)S(1)}, f32[16,2048]{1,0:T(8,128)S(1)}, u32[]{:S(2)}, u32[]{:S(2)}) collective-permute-start(f32[16,2048]{1,0:T(8,128)S(1)} %slice.25), channel_id=1, source_target_pairs={{0,2},{1,3},{2,0},{3,1},{4,6},{5,7},{6,4},{7,5},{8,10},{9,11},{10,... | collective-permute-start | bytes 393224 | tf_op jit(solution)/shard_map/ppermute | solution.py:381
  27.9 7.0 %collective-permute-start.5 = (f32[16,2048]{1,0:T(8,128)S(1)}, f32[16,2048]{1,0:T(8,128)S(1)}, u32[]{:S(2)}, u32[]{:S(2)}) collective-permute-start(f32[16,2048]{1,0:T(8,128)S(1)} %slice.27), channel_id=1, source_target_pairs={{0,8},{1,9},{2,10},{3,11},{4,12},{5,13},{6,14},{7,15},{8,0},{9,1},... | collective-permute-start | bytes 393224 | tf_op jit(solution)/shard_map/ppermute | solution.py:381
  35.0 16.4 %collective-permute-start.6 = (f32[64,2048]{1,0:T(8,128)S(1)}, f32[64,2048]{1,0:T(8,128)}, u32[]{:S(2)}, u32[]{:S(2)}) collective-permute-start(f32[64,2048]{1,0:T(8,128)S(1)} %get-tuple-element.39.refs_0_), channel_id=1, source_target_pairs={{0,4},{1,5},{2,6},{3,7},{4,8},{5,9},{6,10},{7,11},{8,12},{9,13},{1... | collective-permute-start | bytes 1572872 | tf_op jit(solution)/shard_map/ppermute | solution.py:381
  35.1 16.3 %collective-permute-start.7 = (f32[64,2048]{1,0:T(8,128)S(1)}, f32[64,2048]{1,0:T(8,128)}, u32[]{:S(2)}, u32[]{:S(2)}) collective-permute-start(f32[64,2048]{1,0:T(8,128)S(1)} %get-tuple-element.39.refs_0_), channel_id=1, source_target_pairs={{0,12},{1,13},{2,14},{3,15},{4,0},{5,1},{6,2},{7,3},{8,4},{9,5},{1... | collective-permute-start | bytes 1572872 | tf_op jit(solution)/shard_map/ppermute | solution.py:381
  37.7 13.7 %collective-permute-start.8 = (f32[64,2048]{1,0:T(8,128)S(1)}, f32[64,2048]{1,0:T(8,128)}, u32[]{:S(2)}, u32[]{:S(2)}) collective-permute-start(f32[64,2048]{1,0:T(8,128)S(1)} %get-tuple-element.40.refs_1_), channel_id=1, source_target_pairs={{0,1},{1,2},{2,3},{3,0},{4,5},{5,6},{6,7},{7,4},{8,9},{9,10},{10,1... | collective-permute-start | bytes 1572872 | tf_op jit(solution)/shard_map/ppermute | solution.py:381
  38.1 13.4 %collective-permute-start.9 = (f32[64,2048]{1,0:T(8,128)S(1)}, f32[64,2048]{1,0:T(8,128)}, u32[]{:S(2)}, u32[]{:S(2)}) collective-permute-start(f32[64,2048]{1,0:T(8,128)S(1)} %get-tuple-element.40.refs_1_), channel_id=1, source_target_pairs={{0,3},{1,0},{2,1},{3,2},{4,7},{5,4},{6,5},{7,6},{8,11},{9,8},{10,9... | collective-permute-start | bytes 1572872 | tf_op jit(solution)/shard_map/ppermute | solution.py:381
  52.7 10.4 %collective-permute-start.10 = (f32[32,2048]{1,0:T(8,128)S(1)}, f32[32,2048]{1,0:T(8,128)S(1)}, u32[]{:S(2)}, u32[]{:S(2)}) collective-permute-start(f32[32,2048]{1,0:T(8,128)S(1)} %get-tuple-element.45), channel_id=1, source_target_pairs={{0,4},{1,5},{2,6},{3,7},{4,8},{5,9},{6,10},{7,11},{8,12},{9,13},{1... | collective-permute-start | bytes 786440 | tf_op jit(solution)/shard_map/ppermute | solution.py:381
  52.8 10.3 %collective-permute-start.11 = (f32[32,2048]{1,0:T(8,128)S(1)}, f32[32,2048]{1,0:T(8,128)S(1)}, u32[]{:S(2)}, u32[]{:S(2)}) collective-permute-start(f32[32,2048]{1,0:T(8,128)S(1)} %get-tuple-element.46), channel_id=1, source_target_pairs={{0,12},{1,13},{2,14},{3,15},{4,0},{5,1},{6,2},{7,3},{8,4},{9,5},{1... | collective-permute-start | bytes 786440 | tf_op jit(solution)/shard_map/ppermute | solution.py:381
  55.5 7.7 %collective-permute-start.12 = (f32[32,2048]{1,0:T(8,128)S(1)}, f32[32,2048]{1,0:T(8,128)S(1)}, u32[]{:S(2)}, u32[]{:S(2)}) collective-permute-start(f32[32,2048]{1,0:T(8,128)S(1)} %get-tuple-element.47), channel_id=1, source_target_pairs={{0,1},{1,2},{2,3},{3,0},{4,5},{5,6},{6,7},{7,4},{8,9},{9,10},{10,1... | collective-permute-start | bytes 786440 | tf_op jit(solution)/shard_map/ppermute | solution.py:381
  55.5 7.7 %collective-permute-start.13 = (f32[32,2048]{1,0:T(8,128)S(1)}, f32[32,2048]{1,0:T(8,128)S(1)}, u32[]{:S(2)}, u32[]{:S(2)}) collective-permute-start(f32[32,2048]{1,0:T(8,128)S(1)} %get-tuple-element.48), channel_id=1, source_target_pairs={{0,3},{1,0},{2,1},{3,2},{4,7},{5,4},{6,5},{7,6},{8,11},{9,8},{10,9... | collective-permute-start | bytes 786440 | tf_op jit(solution)/shard_map/ppermute | solution.py:381
  65.7 8.9 %collective-permute-start.14 = (f32[512,128]{1,0:T(8,128)S(1)}, f32[512,128]{1,0:T(8,128)S(1)}, u32[]{:S(2)}, u32[]{:S(2)}) collective-permute-start(f32[512,128]{1,0:T(8,128)S(1)} %get-tuple-element.67), channel_id=1, source_target_pairs={{0,0},{1,1},{2,2},{3,3},{4,16},{5,17},{6,18},{7,19},{8,32},{9,33},... | collective-permute-start | bytes 786440 | tf_op jit(solution)/shard_map/ppermute | solution.py:423
  66.4 8.3 %collective-permute-start.15 = (f32[512,128]{1,0:T(8,128)S(1)}, f32[512,128]{1,0:T(8,128)S(1)}, u32[]{:S(2)}, u32[]{:S(2)}) collective-permute-start(f32[512,128]{1,0:T(8,128)S(1)} %get-tuple-element.66), channel_id=1, source_target_pairs={{0,4},{1,5},{2,6},{3,7},{4,20},{5,21},{6,22},{7,23},{8,36},{9,37},... | collective-permute-start | bytes 786440 | tf_op jit(solution)/shard_map/ppermute | solution.py:423
  69.6 11.5 %collective-permute-start.16 = (f32[512,128]{1,0:T(8,128)S(1)}, f32[512,128]{1,0:T(8,128)S(1)}, u32[]{:S(2)}, u32[]{:S(2)}) collective-permute-start(f32[512,128]{1,0:T(8,128)S(1)} %get-tuple-element.65), channel_id=1, source_target_pairs={{0,8},{1,9},{2,10},{3,11},{4,24},{5,25},{6,26},{7,27},{8,40},{9,41... | collective-permute-start | bytes 786440 | tf_op jit(solution)/shard_map/ppermute | solution.py:423
  71.2 10.0 %collective-permute-start.17 = (f32[512,128]{1,0:T(8,128)S(1)}, f32[512,128]{1,0:T(8,128)S(1)}, u32[]{:S(2)}, u32[]{:S(2)}) collective-permute-start(f32[512,128]{1,0:T(8,128)S(1)} %get-tuple-element.64), channel_id=1, source_target_pairs={{0,12},{1,13},{2,14},{3,15},{4,28},{5,29},{6,30},{7,31},{8,44},{9,... | collective-permute-start | bytes 786440 | tf_op jit(solution)/shard_map/ppermute | solution.py:423
  83.4 5.7 %collective-permute-start.18 = (f32[256,512]{1,0:T(8,128)S(1)}, f32[256,512]{1,0:T(8,128)S(1)}, u32[]{:S(2)}, u32[]{:S(2)}) collective-permute-start(f32[256,512]{1,0:T(8,128)S(1)} %get-tuple-element.53), channel_id=1, source_target_pairs={{0,64},{64,0},{1,65},{65,1},{2,66},{66,2},{3,67},{67,3},{4,68},{68... | collective-permute-start | bytes 1572872 | tf_op jit(solution)/shard_map/ppermute | solution.py:429
  111.7 16.7 %all-to-all-start.2 = ((f32[64,4,512]{2,1,0:T(4,128)}), f32[64,4,512]{2,1,0:T(4,128)S(1)}, u32[]{:S(2)}, u32[]{:S(2)}) async-start(f32[64,4,512]{2,1,0:T(4,128)} %broadcast_in_dim.2), calls=%async_computation.2 | async-start | bytes 1048576 | tf_op jit(solution)/shard_map/all_to_all | solution.py:370
  116.3 12.3 %collective-permute-start.19 = (f32[512,128]{1,0:T(8,128)S(1)}, f32[512,128]{1,0:T(8,128)S(1)}, u32[]{:S(2)}, u32[]{:S(2)}) collective-permute-start(f32[512,128]{1,0:T(8,128)S(1)} %get-tuple-element.56), channel_id=1, source_target_pairs={{0,0},{1,1},{2,2},{3,3},{4,16},{5,17},{6,18},{7,19},{8,32},{9,33},... | collective-permute-start | bytes 786440 | tf_op jit(solution)/shard_map/ppermute | solution.py:431
  128.6 18.0 %collective-permute-start.20 = (f32[256,512]{1,0:T(8,128)S(1)}, f32[256,512]{1,0:T(8,128)S(1)}, u32[]{:S(2)}, u32[]{:S(2)}) collective-permute-start(f32[256,512]{1,0:T(8,128)S(1)} %reshape.31.own_ref), channel_id=1, source_target_pairs={{0,64},{64,0},{1,65},{65,1},{2,66},{66,2},{3,67},{67,3},{4,68},{68... | collective-permute-start | bytes 1572872 | tf_op jit(solution)/shard_map/ppermute | solution.py:438
  134.1 34.8 %collective-permute-start.21 = (f32[512,128]{1,0:T(8,128)S(1)}, f32[512,128]{1,0:T(8,128)S(1)}, u32[]{:S(2)}, u32[]{:S(2)}) collective-permute-start(f32[512,128]{1,0:T(8,128)S(1)} %collective-permute-done.19.p0), channel_id=1, source_target_pairs={{0,16},{16,32},{32,48},{48,0},{1,17},{17,33},{33,49},{49,1},{2,18}... | collective-permute-start | bytes 786440 | tf_op jit(solution)/shard_map/ppermute | solution.py:375
  139.5 29.4 %collective-permute-start.22 = (f32[512,128]{1,0:T(8,128)S(1)}, f32[512,128]{1,0:T(8,128)S(1)}, u32[]{:S(2)}, u32[]{:S(2)}) collective-permute-start(f32[512,128]{1,0:T(8,128)S(1)} %collective-permute-done.19.p0), channel_id=1, source_target_pairs={{0,32},{16,48},{32,0},{48,16},{1,33},{17,49},{33,1},{49,17},{2,34}... | collective-permute-start | bytes 786440 | tf_op jit(solution)/shard_map/ppermute | solution.py:375
  146.5 22.4 %collective-permute-start.23 = (f32[512,128]{1,0:T(8,128)S(1)}, f32[512,128]{1,0:T(8,128)S(1)}, u32[]{:S(2)}, u32[]{:S(2)}) collective-permute-start(f32[512,128]{1,0:T(8,128)S(1)} %collective-permute-done.19.p0), channel_id=1, source_target_pairs={{0,48},{16,0},{32,16},{48,32},{1,49},{17,1},{33,17},{49,33},{2,50}... | collective-permute-start | bytes 786440 | tf_op jit(solution)/shard_map/ppermute | solution.py:375
  (12 other events, 153.9 us)
Sparse Core Ops, SparseCore 0:
  110.8 56.2 all-gather.2
